TPU v7x, 256 devices: a whole 4x4x8 slice. The times are simulated.
256 devices in a mesh: frame: 4 (over y_lo, core), space: 64 (over x, y_hi, z).
Axes of the slice: x: 4, y: 4 (y_hi: 2, y_lo: 2; y = y_hi * 2 + y_lo), z: 8, core: 2. Of those that a mesh axis runs over, the one named last changes fastest.
Arguments:
- frames_in: bfloat16 [8, 8192, 2048], P('frame', 'space'), may hold values from -6 to 6
- levels: int32 [8], P('frame'), may hold values from 1 to 899
- fresh: bfloat16 [8192, 2048], P('space'), may hold values from -6 to 6
- w_mod: bfloat16 [256, 4096], replicated, may hold values from -0.375 to 0.375
- w_qkv: bfloat16 [2048, 3072], P('space'), may hold values from -0.26516504 to 0.26516504
- q_gain: float32 [8], replicated, may hold values from 0.5 to 64
- w_out: bfloat16 [1024, 2048], P('space'), may hold values from -0.1875 to 0.1875
Outputs:
- frames_out: bfloat16 [8, 8192, 2048], P('frame', 'space')
All inputs are finite; a program needn't handle non-finite values.
Results may differ from a plain program's by a relative error of at most 0.0075.
The roundings to bfloat16 on the way count: a program that leaves them out, or rounds other values in their place, can miss the bound.
Values may be sent and summed in bfloat16 or wider, within the bound.
No kernel may reach another device: no remote copies, remote signals or barrier semaphores. Data moves between devices by JAX's collectives and lax.ppermute only.
A program may use at most 128 MiB of HBM per device.

v0:
```python
import math

import jax
import jax.numpy as jnp
from jax import lax
from jax.sharding import PartitionSpec as P

LEVELS = 1000
FRAMES = 8


def with_halo(cells, sides, width):
    for axis, dim in sides:
        count = lax.axis_size(axis)
        head = lax.slice_in_dim(cells, 0, width, axis=dim)
        tail = lax.slice_in_dim(cells, cells.shape[dim] - width, cells.shape[dim], axis=dim)
        cells = jnp.concatenate(
            [
                lax.ppermute(tail, axis, [(i, (i + 1) % count) for i in range(count)]),
                cells,
                lax.ppermute(head, axis, [((i + 1) % count, i) for i in range(count)]),
            ],
            axis=dim,
        )
    return cells


def from_behind(array, axis, by):
    count = lax.axis_size(axis)
    pairs = [(i, i + by) for i in range(count) if 0 <= i + by < count]
    return lax.ppermute(array, axis, pairs)


def embed(levels, freq_count):
    half = freq_count // 2
    freqs = jnp.exp(-math.log(10000.0) * jnp.arange(half, dtype=jnp.float32) / half)
    angles = levels.astype(jnp.float32)[:, None] * freqs[None, :]
    return jnp.concatenate([jnp.cos(angles), jnp.sin(angles)], axis=1).astype(jnp.bfloat16)


def alpha_bar(steps):
    frac = steps.astype(jnp.float32) / LEVELS
    return jnp.cos((frac + 0.008) / 1.008 * (math.pi / 2)) ** 2


def body(frames_in, levels, fresh, w_mod, w_qkv, q_gain, w_out):
    local_frames, rows, width = frames_in.shape
    heads = q_gain.shape[0]
    head_dim = w_qkv.shape[1] // (3 * heads)
    inv = 1.0 / math.sqrt(head_dim)
    mod = jnp.dot(embed(levels, w_mod.shape[0]), w_mod, preferred_element_type=jnp.float32)
    shift = mod[:, :width]
    scale = mod[:, width:]
    x32 = frames_in.astype(jnp.float32)
    mean = jnp.mean(x32, axis=-1, keepdims=True)
    var = jnp.mean((x32 - mean) ** 2, axis=-1, keepdims=True)
    normed = (x32 - mean) * lax.rsqrt(var + 1e-06)
    xm = (normed * (1.0 + scale[:, None, :]) + shift[:, None, :]).astype(jnp.bfloat16)
    xm = xm.reshape(local_frames * rows, width)
    columns = xm
    qkv = jnp.dot(
        columns,
        lax.all_gather(w_qkv, "space", axis=0, tiled=True),
        preferred_element_type=jnp.float32,
    )
    qkv = qkv.reshape(local_frames, rows, 3, heads, head_dim)
    query = qkv[:, :, 0]
    key = qkv[:, :, 1]
    query = (
        query
        * lax.rsqrt(jnp.mean(query * query, axis=-1, keepdims=True) + 1e-06)
        * q_gain[None, None, :, None]
    )
    key = key * lax.rsqrt(jnp.mean(key * key, axis=-1, keepdims=True) + 1e-06)
    q_norm = query.astype(jnp.bfloat16)
    k_norm = key.astype(jnp.bfloat16)
    v_vals = qkv[:, :, 2].astype(jnp.bfloat16)
    stacked = jnp.stack([k_norm, v_vals], axis=0)
    padded = with_halo(stacked, (("space", 2),), rows)
    spatial = (
        jnp.einsum("frhd,fkhd->fhrk", q_norm, padded[0], preferred_element_type=jnp.float32) * inv
    )
    kk = jnp.arange(3 * rows)[None, :]
    rr = jnp.arange(rows)[:, None]
    band = jnp.abs(kk - rr - rows) <= rows
    spatial = jnp.where(band[None, None], spatial, -1e30)
    top_space = jnp.max(spatial, axis=-1)
    p_space = jnp.where(band[None, None], jnp.exp(spatial - top_space[..., None]), 0.0)
    sum_space = jnp.sum(p_space, axis=-1).transpose(0, 2, 1)
    acc_space = jnp.einsum(
        "fhrk,fkhd->frhd",
        p_space.astype(jnp.bfloat16),
        padded[1],
        preferred_element_type=jnp.float32,
    )
    top_space = top_space.transpose(0, 2, 1)
    mine = lax.axis_index("frame") * local_frames + jnp.arange(local_frames)
    start_top = jnp.full((local_frames, rows, heads), -1e30, jnp.float32)
    k_piece = lax.all_gather(k_norm, "frame", axis=0, tiled=True)
    other = jnp.arange(k_piece.shape[0])
    causal = jnp.logical_and(other[None, :] < mine[:, None], True)[:, None, None, :]
    scores = (
        jnp.einsum("frhd,grhd->frhg", q_norm, k_piece, preferred_element_type=jnp.float32) * inv
    )
    scores = jnp.where(causal, scores, -1e30)
    top_new = jnp.maximum(start_top, jnp.max(scores, axis=-1))
    probs = jnp.where(causal, jnp.exp(scores - top_new[..., None]), 0.0)
    sums = jnp.sum(probs, axis=-1)
    acc = jnp.einsum(
        "frhg,grhd->frhd",
        probs.astype(jnp.bfloat16),
        lax.all_gather(v_vals, "frame", axis=0, tiled=True),
        preferred_element_type=jnp.float32,
    )
    acc_time = acc
    top_all = jnp.maximum(top_space, top_new)
    weight_space = jnp.exp(top_space - top_all)
    weight_time = jnp.exp(top_new - top_all)
    total = sum_space * weight_space + sums * weight_time
    acc = acc_space * weight_space[..., None] + acc_time * weight_time[..., None]
    attended = (
        (acc / total[..., None]).astype(jnp.bfloat16).reshape(local_frames * rows, heads * head_dim)
    )
    columns = attended
    projected = jnp.dot(
        columns,
        lax.all_gather(w_out, "space", axis=0, tiled=True),
        preferred_element_type=jnp.float32,
    )
    eps = x32 + projected.reshape(local_frames, rows, width)
    later = jnp.maximum(levels - LEVELS // FRAMES, 0)
    a_now = alpha_bar(levels)[:, None, None]
    a_later = alpha_bar(later)[:, None, None]
    clean = (x32 - jnp.sqrt(1.0 - a_now) * eps) / jnp.sqrt(a_now)
    denoised = (jnp.sqrt(a_later) * clean + jnp.sqrt(1.0 - a_later) * eps).astype(jnp.bfloat16)
    arriving = from_behind(denoised[0:1], "frame", -1)
    is_last = lax.axis_index("frame") == lax.axis_size("frame") - 1
    tail = jnp.where(is_last, fresh[None], arriving)
    return jnp.concatenate([denoised[1:], tail], axis=0)


def solution(mesh):
    return jax.shard_map(
        body,
        mesh=mesh,
        in_specs=(
            P("frame", "space", None),
            P("frame"),
            P("space", None),
            P(),
            P("space", None),
            P(),
            P("space", None),
        ),
        out_specs=P("frame", "space", None),
        check_vma=False,
    )
```

profile of v0, /device:TPU:1, one launch (start us, length us, event | category | flops | bytes accessed | tf_op | source)
XLA Modules:
  0.0 450.4 jit_solution(5514404491794709641)
XLA Ops:
  6.5 0.7 all-gather.6.cloned.1.call-update
  7.3 0.7 convert_element_type.59
  8.0 1.4 convert_reduce_fusion
  9.4 1.6 fusion.9
  11.1 0.1 fusion.67
  11.2 0.4 fusion.69
  11.6 174.9 %all-gather.6.cloned.1.call-done = bf16[2048,3072]{1,0:T(8,128)(2,1)} async-done(((bf16[32,3072]{1,0:T(8,128)(2,1)}), bf16[2048,3072]{1,0:T(8,128)(2,1)}) %all-gather.6.cloned.1.call-update) | async-done | bytes 12582928 | tf_op jit(solution)/shard_map/all_gather | solution.py:63
  186.5 15.7 %copy.33 = bf16[3072,2048]{1,0:T(8,128)(2,1)} copy(bf16[3072,2048]{0,1:T(8,128)(2,1)} %bitcast.92) | data formatting | bytes 25165824 | tf_op jit(solution)/shard_map/dot_general | solution.py:61
  202.2 7.3 %fusion.51 = f32[2,128,3,8,128]{1,4,3,2,0:T(8,128)S(1)} fusion(bf16[3,8,128,2048,1]{3,2,1,0,4:T(8,128)(2,1)} %bitcast.93, bf16[2,128,2048]{2,1,0:T(8,128)(2,1)S(1)} %copy-done.5, f32[2,2048]{1,0:T(2,128)S(1)} %get-tuple-element.17, f32[2,2048]{1,0:T(2,128)S(1)} %get-tuple-element.16, f32[2,128]{1,0:T(2,128)S(1)} %add_rsqrt_fusion.2, ...), kind=kOutput, calls=%fused_computation.43 | convolution fusion | flops 3224371200 | bytes 16812032 | tf_op jit(solution)/shard_map/dot_general | solution.py:61
  209.5 0.2 fusion.53
  209.7 1.5 copy-done.1
  211.1 1.1 fusion.54
  212.3 1.1 copy.37
  213.4 1.3 slice.67
  214.8 1.1 copy.41
  215.9 0.5 all-gather.10.cloned.1.call-update
  216.4 1.3 slice_bitcast_fusion.13
  217.8 1.3 fusion.55
  219.1 1.1 pad_maximum_fusion.1
  220.2 3.2 collective-permute-start.1
  223.4 0.1 abs_compare_fusion
  223.4 0.1 iota_compare_fusion
  223.5 0.1 subtract_sqrt_fusion.1
  223.6 2.1 copy.39
  225.7 19.3 %collective-permute-done.1 = bf16[2,2,128,8,128]{2,4,3,1,0:T(8,128)(2,1)} collective-permute-done((bf16[2,2,128,8,128]{2,4,3,1,0:T(8,128)(2,1)}, bf16[2,2,128,8,128]{2,4,3,1,0:T(8,128)(2,1)}, u32[]{:S(2)}, u32[]{:S(2)}) %collective-permute-start.1) | collective-permute-done | bytes 1048608 | tf_op jit(solution)/shard_map/ppermute | solution.py:21
  245.0 7.6 %collective-permute-done = bf16[2,2,128,8,128]{2,4,3,1,0:T(8,128)(2,1)} collective-permute-done((bf16[2,2,128,8,128]{2,4,3,1,0:T(8,128)(2,1)}, bf16[2,2,128,8,128]{2,4,3,1,0:T(8,128)(2,1)}, u32[]{:S(2)}, u32[]{:S(2)}) %collective-permute-start) | collective-permute-done | bytes 1048608 | tf_op jit(solution)/shard_map/ppermute | solution.py:19
  252.7 1.8 pad_maximum_fusion
  254.5 1.7 copy-done.3
  256.2 0.8 fusion.2
  257.0 1.7 copy-done.2
  258.7 1.1 fusion.7
  259.8 5.5 %all-gather.8.cloned.1.call-done = bf16[8,128,8,128]{3,2,1,0:T(8,128)(2,1)} async-done(((bf16[2,128,8,128]{3,2,1,0:T(8,128)(2,1)}), bf16[8,128,8,128]{3,2,1,0:T(8,128)(2,1)}) %all-gather.8.cloned.1.call-update) | async-done | bytes 2097168 | tf_op jit(solution)/shard_map/all_gather | solution.py:99
  265.3 5.0 %fusion.83 = (f32[2,128,8]{0,2,1:T(8,128)S(1)}, f32[2,128,8,8]{3,0,2,1:T(2,128)}) fusion(bf16[2,128,8,128]{3,0,2,1:T(2,128)(2,1)S(1)} %copy-done.7, bf16[8,128,8,128]{3,2,1,0:T(8,128)(2,1)} %all-gather.8.cloned.1.call-done, pred[2,8]{1,0:T(4,128)(4,1)S(1)} %iota_compare_fusion), kind=kOutput, calls=%fused_computation.102 | convolution fusion | flops 4241408 | bytes 2695184 | tf_op jit(solution)/shard_map/frhd,grhd->frhg/dot_general | solution.py:103
  270.3 0.2 copy.40
  270.5 0.3 copy.43
  270.8 24.3 %all-gather.12.cloned.1.call-done = bf16[8,128,1,8,128]{4,3,2,1,0:T(8,128)(2,1)} async-done(((bf16[2,128,1,8,128]{4,3,2,1,0:T(8,128)(2,1)}), bf16[8,128,1,8,128]{4,3,2,1,0:T(8,128)(2,1)}) %all-gather.12.cloned.1.call-update) | async-done | bytes 2097168 | tf_op jit(solution)/shard_map/all_gather | solution.py:112
  295.1 5.2 %fusion.16 = f32[128,8,128,2]{2,3,1,0:T(2,128)} fusion(bf16[8,128,1,8,128]{4,3,2,1,0:T(8,128)(2,1)} %all-gather.12.cloned.1.call-done, f32[2,128,8,8]{3,0,2,1:T(2,128)} %get-tuple-element.25, pred[2,8]{1,0:T(4,128)(4,1)S(1)} %iota_compare_fusion, f32[2,128,8]{0,2,1:T(8,128)S(1)} %copy.43), kind=kOutput, calls=%fused_computation.21 | convolution fusion | flops 4243456 | bytes 3219472 | tf_op jit(solution)/shard_map/frhg,grhd->frhd/dot_general | solution.py:109
  300.3 2.3 copy.44
  302.6 3.8 fusion.63
  306.4 0.2 copy.45
  306.6 4.6 %divide_convert_fusion = bf16[2,128,8,128]{1,3,2,0:T(8,128)(2,1)} fusion(f32[128,8,128,2]{0,2,1,3:T(8,128)} %copy.44, f32[2,8,128,384]{3,2,1,0:T(8,128)} %copy-done.2, f32[2,8,128]{2,1,0:T(8,128)S(1)} %get-tuple-element.26, pred[128,384]{1,0:T(8,128)(4,1)S(1)} %abs_compare_fusion, bf16[2,2,384,8,128]{2,4,3,1,0:T(8,128)(2,1)} %copy-done.3, ...), kind=kOutput, calls=%fused_computation.55 | convolution fusion | flops 206569472 | bytes 6373376 | tf_op jit(solution)/shard_map/fhrk,fkhd->frhd/dot_general | solution.py:90
  311.2 112.4 %all-gather.10.cloned.1.call-done = bf16[1024,2048]{1,0:T(8,128)(2,1)} async-done(((bf16[16,2048]{1,0:T(8,128)(2,1)}), bf16[1024,2048]{1,0:T(8,128)(2,1)}) %all-gather.10.cloned.1.call-update) | async-done | bytes 4194320 | tf_op jit(solution)/shard_map/all_gather | solution.py:127
  423.6 4.0 fusion.21
  427.6 0.9 fusion.82
  428.4 6.0 %collective-permute-start.2 = (bf16[1,128,2048]{2,1,0:T(8,128)(2,1)}, bf16[1,128,2048]{2,1,0:T(8,128)(2,1)S(1)}, u32[]{:S(2)}, u32[]{:S(2)}) collective-permute-start(bf16[1,128,2048]{2,1,0:T(8,128)(2,1)} %get-tuple-element.15), channel_id=1, source_target_pairs={{64,0},{128,64},{192,128},{65,1},{129,65},{193,129},{66,2},{130,66... | collective-permute-start | bytes 1572872 | tf_op jit(solution)/shard_map/ppermute | solution.py:31
  434.5 7.2 %collective-permute-done.2 = bf16[1,128,2048]{2,1,0:T(8,128)(2,1)S(1)} collective-permute-done((bf16[1,128,2048]{2,1,0:T(8,128)(2,1)}, bf16[1,128,2048]{2,1,0:T(8,128)(2,1)S(1)}, u32[]{:S(2)}, u32[]{:S(2)}) %collective-permute-start.2) | collective-permute-done | bytes 524320 | tf_op jit(solution)/shard_map/ppermute | solution.py:31
  441.7 1.1 bitcast_select_fusion
  442.8 1.1 pad_maximum_fusion.2
  (33 shorter events, 0.3 us)
Async XLA Ops:
  6.5 4.7 %copy-start = (bf16[256,4096]{1,0:T(8,128)(2,1)S(1)}, bf16[256,4096]{1,0:T(8,128)(2,1)}, u32[]{:S(2)}) copy-start(bf16[256,4096]{1,0:T(8,128)(2,1)} %param.10) | copy-start | bytes 6291460
  6.5 179.9 %all-gather.6.cloned.1.call-start = ((), (), s32[]{:S(2)}) async-start(), calls=%async_computation | async-start | bytes 12779520 | tf_op jit(solution)/shard_map/all_gather | solution.py:63
  7.3 258.1 %all-gather.8.cloned.1.call-start = ((), (), s32[]{:S(2)}) async-start(), calls=%async_computation.1 | async-start | bytes 2621440 | tf_op jit(solution)/shard_map/all_gather | solution.py:99
  186.5 15.7 %copy-start.5 = (bf16[2,128,2048]{2,1,0:T(8,128)(2,1)S(1)}, bf16[2,128,2048]{2,1,0:T(8,128)(2,1)}, u32[]{:S(2)}) copy-start(bf16[2,128,2048]{2,1,0:T(8,128)(2,1)} %param.7) | copy-start | bytes 3145732
  202.2 8.9 %copy-start.9 = (f32[8]{0:T(128)S(1)}, f32[8]{0:T(128)}, u32[]{:S(2)}) copy-start(f32[8]{0:T(128)} %param.12) | copy-start | bytes 100
  209.5 1.7 copy-start.1
  213.4 81.7 %all-gather.12.cloned.1.call-start = ((), (), s32[]{:S(2)}) async-start(), calls=%async_computation.3 | async-start | bytes 2621440 | tf_op jit(solution)/shard_map/all_gather | solution.py:112
  214.8 8.7 %copy-start.8 = (s32[2]{0:T(128)S(1)}, s32[2]{0:T(128)}, u32[]{:S(2)}) copy-start(s32[2]{0:T(128)} %param.8) | copy-start | bytes 28
  215.9 207.7 %all-gather.10.cloned.1.call-start = ((), (), s32[]{:S(2)}) async-start(), calls=%async_computation.2 | async-start | bytes 4259840 | tf_op jit(solution)/shard_map/all_gather | solution.py:127
  220.2 24.9 %collective-permute-start.1 = (bf16[2,2,128,8,128]{2,4,3,1,0:T(8,128)(2,1)}, bf16[2,2,128,8,128]{2,4,3,1,0:T(8,128)(2,1)}, u32[]{:S(2)}, u32[]{:S(2)}) collective-permute-start(bf16[2,2,128,8,128]{2,4,3,1,0:T(8,128)(2,1)} %pad_maximum_fusion.1), channel_id=1, source_target_pairs={{1,0},{2,1},{3,2},{4,3},{5,4},{6,5},{7,6},{8,7},{9,8},{10,9},{11,1... | collective-permute-start | bytes 3145736 | tf_op jit(solution)/shard_map/ppermute | solution.py:21
  223.4 29.3 %collective-permute-start = (bf16[2,2,128,8,128]{2,4,3,1,0:T(8,128)(2,1)}, bf16[2,2,128,8,128]{2,4,3,1,0:T(8,128)(2,1)}, u32[]{:S(2)}, u32[]{:S(2)}) collective-permute-start(bf16[2,2,128,8,128]{2,4,3,1,0:T(8,128)(2,1)} %pad_maximum_fusion.1), channel_id=1, source_target_pairs={{0,1},{1,2},{2,3},{3,4},{4,5},{5,6},{6,7},{7,8},{8,9},{9,10},{10,1... | collective-permute-start | bytes 3145736 | tf_op jit(solution)/shard_map/ppermute | solution.py:19
  225.7 30.5 %copy-start.4 = (bf16[2,128,8,128]{1,3,2,0:T(8,128)(2,1)S(1)}, bf16[2,128,8,128]{1,3,2,0:T(8,128)(2,1)}, u32[]{:S(2)}) copy-start(bf16[2,128,8,128]{1,3,2,0:T(8,128)(2,1)} %get-tuple-element.13) | copy-start | bytes 1572868
  254.5 1.7 copy-start.3
  256.2 9.2 %copy-start.7 = (bf16[2,128,8,128]{3,0,2,1:T(2,128)(2,1)S(1)}, bf16[2,128,8,128]{3,0,2,1:T(2,128)(2,1)}, u32[]{:S(2)}) copy-start(bf16[2,128,8,128]{3,0,2,1:T(2,128)(2,1)} %copy.39) | copy-start | bytes 1572868
  257.0 1.7 copy-start.2
  306.6 117.0 %copy-start.6 = (bf16[2,128,2048]{2,1,0:T(8,128)(2,1)S(1)}, bf16[2,128,2048]{2,1,0:T(8,128)(2,1)}, u32[]{:S(2)}) copy-start(bf16[2,128,2048]{2,1,0:T(8,128)(2,1)} %param.7) | copy-start | bytes 3145732
  428.4 13.3 %collective-permute-start.2 = (bf16[1,128,2048]{2,1,0:T(8,128)(2,1)}, bf16[1,128,2048]{2,1,0:T(8,128)(2,1)S(1)}, u32[]{:S(2)}, u32[]{:S(2)}) collective-permute-start(bf16[1,128,2048]{2,1,0:T(8,128)(2,1)} %get-tuple-element.15), channel_id=1, source_target_pairs={{64,0},{128,64},{192,128},{65,1},{129,65},{193,129},{66,2},{130,66... | collective-permute-start | bytes 1572872 | tf_op jit(solution)/shard_map/ppermute | solution.py:31
Sparse Core Ops, SparseCore 0:
  11.0 175.3 all-gather.5
  213.5 51.7 all-gather.7
  267.1 27.9 all-gather.11
  298.6 124.9 all-gather.9
where the time goes:
time: 451 us; the launch traced here: 450 us
  waiting for transfers between devices  352 us (78%)
  local copies, waits for them, and re-layouts  31.3 us (7%)
  matrix products  27.2 us (6%)
  other arithmetic  16.7 us (4%)
  between operations  13.3 us (3%)
  starting transfers between devices  9.34 us (2%)
    all_gather x1, waiting for transfers between devices, body(): lax.all_gather(w_qkv, 'space', axis=0, tiled=True)  175 us
    all_gather x1, waiting for transfers between devices, body(): lax.all_gather(w_out, 'space', axis=0, tiled=True)  112 us
    all_gather x1, waiting for transfers between devices, body(): lax.all_gather(v_vals, 'frame', axis=0, tiled=True)  24.3 us
    ppermute x1, waiting for transfers between devices, with_halo(): lax.ppermute(head, axis, [((i + 1) % count, i) for i in range(count)])  19.3 us
    dot_general x1, local copies, waits for them, and re-layouts, body(): jnp.dot(columns, lax.all_gather(w_qkv, 'space', axis=0, tiled=True), pref...  15.7 us
  transfers between devices with their start and end apart: 7, of which 7 were waited for; matrix products, arithmetic and copies ran while one was open for 8% of the time, Pallas kernels for 0%

commit v1 on v0

v1 whole, which is shorter than its diff:
```python
import functools
import math

import jax
import jax.numpy as jnp
from jax import lax
from jax.experimental import pallas as pl
from jax.experimental.pallas import tpu as pltpu
from jax.sharding import Mesh, PartitionSpec as P

LEVELS = 1000
FRAMES = 8
F32 = jnp.float32
BF16 = jnp.bfloat16
AXES = ("yl", "core", "x", "yh", "z")
SIZES = (2, 2, 4, 2, 8)
SIZE = dict(zip(AXES, SIZES))
VMEM_LIMIT = 48 * 1024 * 1024


def embed(levels, freq_count):
    half = freq_count // 2
    freqs = jnp.exp(-math.log(10000.0) * jnp.arange(half, dtype=F32) / half)
    angles = levels.astype(F32)[:, None] * freqs[None, :]
    return jnp.concatenate([jnp.cos(angles), jnp.sin(angles)], axis=1).astype(BF16)


def alpha_bar(steps):
    frac = steps.astype(F32) / LEVELS
    return jnp.cos((frac + 0.008) / 1.008 * (math.pi / 2)) ** 2


def swap(array, axis):
    return lax.ppermute(array, axis, [(0, 1), (1, 0)])


def both_ways(array, axis, by):
    n = SIZE[axis]
    pairs = [(i, (i + by) % n) for i in range(n)]
    pairs += [(n + i, n + (i - by) % n) for i in range(n)]
    return lax.ppermute(array, ("core", axis), pairs)


def pick(array, index, axis=0):
    return lax.dynamic_index_in_dim(array, index, axis, keepdims=False)


def call(body, out_shape, scalars, arrays, scratch=(), flops=0):
    specs = [pl.BlockSpec(memory_space=pltpu.SMEM)] * len(scalars)
    specs += [pl.BlockSpec(memory_space=pltpu.VMEM)] * len(arrays)
    moved = sum(a.size * a.dtype.itemsize for a in arrays)
    moved += sum(math.prod(s.shape) * s.dtype.itemsize for s in jax.tree.leaves(out_shape))
    return pl.pallas_call(
        body,
        out_shape=out_shape,
        in_specs=specs,
        out_specs=jax.tree.map(lambda _: pl.BlockSpec(memory_space=pltpu.VMEM), out_shape),
        scratch_shapes=list(scratch),
        compiler_params=pltpu.CompilerParams(vmem_limit_bytes=VMEM_LIMIT),
        cost_estimate=pl.CostEstimate(flops=flops, bytes_accessed=moved, transcendentals=0),
    )(*scalars, *arrays)


def norm_kernel(x_ref, shift_ref, scale_ref, out_ref):
    frames, rows, width = x_ref.shape
    chunk = 32
    for f in range(frames):
        shift = shift_ref[f][None]
        scale = 1.0 + scale_ref[f][None]

        @pl.loop(0, rows // chunk)
        def _(step):
            at = pl.ds(pl.multiple_of(step * chunk, chunk), chunk)
            x = x_ref[f, at, :].astype(F32)
            mean = jnp.mean(x, axis=-1, keepdims=True)
            x = x - mean
            var = jnp.mean(x * x, axis=-1, keepdims=True)
            out_ref[f, at, :] = (x * lax.rsqrt(var + 1e-06) * scale + shift).astype(BF16)


def norm_rows(x, shift, scale):
    return call(norm_kernel, jax.ShapeDtypeStruct(x.shape, BF16), (), (x, shift, scale), flops=20 * x.size)


def place_z_kernel(ids, own_ref, r1, r2, r3, r4, s1, s2, s3, s4, k_ref, q_ref):
    c, sign, zi = ids[0], ids[1], ids[2]
    outs = (k_ref, q_ref)

    def put(ref, z):
        for part in range(2):
            outs[part][:, :, pl.ds(z, 1)] = ref[:, part][:, :, None]

    put(own_ref, zi)
    for by, (mine, other) in enumerate(((r1, s1), (r2, s2), (r3, s3)), 1):
        put(mine, lax.rem(zi - sign * by + 8, 8))
        put(other, lax.rem(zi + sign * by + 8, 8))
    far = lax.rem(zi + 4, 8)
    for part in range(2):
        outs[part][pl.ds(c, 1), :, pl.ds(far, 1)] = r4[part][None, :, None]
        outs[part][pl.ds(1 - c, 1), :, pl.ds(far, 1)] = s4[part][None, :, None]


def place_x_kernel(ids, own_ref, r1, r2, s1, s2, v_ref):
    c, sign, xi = ids[0], ids[1], ids[3]
    v_ref[pl.ds(xi, 1)] = own_ref[...][None]
    v_ref[pl.ds(lax.rem(xi - sign + 4, 4), 1)] = r1[...][None]
    v_ref[pl.ds(lax.rem(xi + sign + 4, 4), 1)] = s1[...][None]
    far = lax.rem(xi + 2, 4)
    v_ref[pl.ds(far, 1), pl.ds(c, 1)] = r2[...][None, None]
    v_ref[pl.ds(far, 1), pl.ds(1 - c, 1)] = s2[...][None, None]


def weight_from_x(ids, refs, w_ref):
    own_ref, r1, r2, s1, s2 = refs
    c, sign, xi = ids[0], ids[1], ids[3]
    w_ref[pl.ds(xi, 1)] = own_ref[:, pl.ds(c, 1)].reshape(1, 2, 8, 32, 256)
    w_ref[pl.ds(lax.rem(xi - sign + 4, 4), 1)] = r1[:, pl.ds(c, 1)].reshape(1, 2, 8, 32, 256)
    w_ref[pl.ds(lax.rem(xi + sign + 4, 4), 1)] = s1[...][None]
    far = lax.rem(xi + 2, 4)
    w_ref[pl.ds(far, 1), pl.ds(c, 1)] = r2[pl.ds(c, 1)][None]
    w_ref[pl.ds(far, 1), pl.ds(1 - c, 1)] = s2[...][None, None]


def weight_from_z(ids, refs, w_ref):
    own_ref, r1, r2, r3, r4, s1, s2, s3, s4 = refs
    c, sign, zi = ids[0], ids[1], ids[2]
    w_ref[:, :, pl.ds(zi, 1)] = own_ref[:, :, pl.ds(c, 1)]
    for by, (mine, other) in enumerate(((r1, s1), (r2, s2), (r3, s3)), 1):
        w_ref[:, :, pl.ds(lax.rem(zi - sign * by + 8, 8), 1)] = mine[:, :, pl.ds(c, 1)]
        w_ref[:, :, pl.ds(lax.rem(zi + sign * by + 8, 8), 1)] = other[...][:, :, None]
    far = lax.rem(zi + 4, 8)
    w_ref[pl.ds(2 * c, 2), :, pl.ds(far, 1)] = r4[:, :, pl.ds(c, 1)]
    w_ref[pl.ds(2 - 2 * c, 2), :, pl.ds(far, 1)] = s4[...][:, :, None]


def project_kernel(gather, normed, ids, gains, *refs):
    *pieces, x0, x1, x2, x3, out_ref, w_ref = refs
    gather(ids, pieces, w_ref)
    weight = w_ref[...].reshape(2048, 256)
    for group, x_ref in enumerate((x0, x1, x2, x3)):
        first = ids[4 + group]
        got = jnp.dot(x_ref[...].reshape(256, 2048), weight, preferred_element_type=F32)
        if normed:
            heads = []
            for h in range(2):
                part = got[:, h * 128 : (h + 1) * 128]
                part = part * lax.rsqrt(jnp.mean(part * part, axis=-1, keepdims=True) + 1e-06)
                heads.append(part * gains[h])
            got = jnp.concatenate(heads, axis=1)
        out_ref[pl.ds(first, 2)] = got.astype(BF16).reshape(2, 128, 256)


def project(ids, gains, pieces, xs, gather, normed):
    return call(
        functools.partial(project_kernel, gather, normed),
        jax.ShapeDtypeStruct((FRAMES, 128, 256), BF16),
        (ids, gains),
        (*pieces, *xs),
        scratch=[pltpu.VMEM((4, 2, 8, 32, 256), BF16)],
        flops=2 * 1024 * 2048 * 256,
    )


def attend_kernel(q_ref, k_ref, v_ref, kl_ref, kr_ref, vl_ref, vr_ref, out_ref):
    inv = 1.0 / math.sqrt(128)
    rr = lax.broadcasted_iota(jnp.int32, (128, 128), 0)
    kk = lax.broadcasted_iota(jnp.int32, (128, 128), 1)
    in_left = kk >= rr
    in_right = kk <= rr
    nt = (((1,), (1,)), ((), ()))
    for f in range(1, FRAMES):
        for h in range(2):
            lanes = slice(h * 128, (h + 1) * 128)
            q = q_ref[f, :, lanes]
            left = lax.dot_general(q, kl_ref[f - 1, :, lanes], nt, preferred_element_type=F32) * inv
            mid = lax.dot_general(q, k_ref[f, :, lanes], nt, preferred_element_type=F32) * inv
            right = lax.dot_general(q, kr_ref[f - 1, :, lanes], nt, preferred_element_type=F32) * inv
            left = jnp.where(in_left, left, -1e30)
            right = jnp.where(in_right, right, -1e30)
            q32 = q.astype(F32)
            earlier = [
                jnp.sum(q32 * k_ref[g, :, lanes].astype(F32), axis=-1, keepdims=True) * inv
                for g in range(f)
            ]
            top = jnp.max(jnp.maximum(jnp.maximum(left, mid), right), axis=-1, keepdims=True)
            for score in earlier:
                top = jnp.maximum(top, score)
            left = jnp.where(in_left, jnp.exp(left - top), 0.0)
            mid = jnp.exp(mid - top)
            right = jnp.where(in_right, jnp.exp(right - top), 0.0)
            total = jnp.sum(left + mid + right, axis=-1, keepdims=True)
            acc = jnp.dot(left.astype(BF16), vl_ref[f - 1, :, lanes], preferred_element_type=F32)
            acc += jnp.dot(mid.astype(BF16), v_ref[f, :, lanes], preferred_element_type=F32)
            acc += jnp.dot(right.astype(BF16), vr_ref[f - 1, :, lanes], preferred_element_type=F32)
            for g, score in enumerate(earlier):
                p = jnp.exp(score - top)
                total += p
                acc += p.astype(BF16).astype(F32) * v_ref[g, :, lanes].astype(F32)
            out_ref[f - 1, :, lanes] = (acc / total).astype(BF16)
    out_ref[FRAMES - 1] = jnp.zeros_like(out_ref[FRAMES - 1])


def finish_kernel(ids, coefs, o_ref, wa_ref, wb_ref, x0_ref, x1_ref, fresh_ref, out_ref):
    c, last = ids[0], ids[8]
    for which, w_ref in enumerate((wa_ref, wb_ref)):
        side = c if which == 0 else 1 - c
        columns = pl.ds(pl.multiple_of(side * 1024, 1024), 1024)
        eps = None
        for s in range(4):
            weight = jnp.concatenate(
                [w_ref[s, :, yh].reshape(128, 1024) for yh in range(2)], axis=0
            )
            term = jnp.dot(o_ref[s].reshape(256, 256), weight, preferred_element_type=F32)
            eps = term if eps is None else eps + term
        for slot, x_ref in enumerate((x0_ref, x1_ref)):
            x = x_ref[:, columns].astype(F32)
            e = x + eps[slot * 128 : (slot + 1) * 128]
            done = coefs[4 * slot] * ((x - coefs[4 * slot + 1] * e) * coefs[4 * slot + 2])
            done = (done + coefs[4 * slot + 3] * e).astype(BF16)
            if slot == 1:
                done = jnp.where(last == 1, fresh_ref[:, columns], done)
            out_ref[slot, :, columns] = done


def body(frames_in, levels, fresh, w_mod, w_qkv, q_gain, w_out):
    width = frames_in.shape[2]
    yl, c = lax.axis_index("yl"), lax.axis_index("core")
    xi, yhi, zi = lax.axis_index("x"), lax.axis_index("yh"), lax.axis_index("z")
    me = 2 * yl + c
    groups = (me, 2 * yl + 1 - c, 2 * (1 - yl) + c, 2 * (1 - yl) + 1 - c)
    ids = jnp.stack(
        [c, 1 - 2 * c, zi, xi, *(2 * g for g in groups), (me == 3).astype(jnp.int32)]
    ).astype(jnp.int32)
    gains = lax.dynamic_slice(q_gain, (2 * me,), (2,))
    ones = jnp.ones((2,), F32)

    mine = pick(w_qkv.reshape(32, 3, 2, 2, 256), yl, 2).transpose(1, 2, 0, 3)
    mine = jnp.stack([mine[2], mine[1], mine[0]]).reshape(192, 256)
    half = lax.dynamic_slice(w_out, (0, 1024 * c), (16, 1024)).reshape(64, 256)
    pack = jnp.concatenate([mine, half], axis=0)
    got = swap(pack, "yh")
    pair = jnp.stack([jnp.where(yhi == 0, pack, got), jnp.where(yhi == 0, got, pack)])
    out_half = lax.all_gather(pair[:, 192:].reshape(32, 1024), ("x", "z"), axis=0, tiled=True)
    pair = pair[:, :192].reshape(2, 3, 2, 32, 256)
    value, rest = pair[:, 0], pair[:, 1:]

    mod = jnp.dot(embed(levels, w_mod.shape[0]), w_mod, preferred_element_type=F32)
    own = norm_rows(frames_in, mod[:, :width], mod[:, width:])
    across = swap(own, "yl")
    beside = swap(own, "core")
    diagonal = swap(across, "core")
    xs = (own, beside, across, diagonal)

    a1 = both_ways(value, "x", 1)
    a2 = both_ways(pick(value, c), "x", 2)
    block = call(
        place_x_kernel,
        jax.ShapeDtypeStruct((4, 2, 2, 32, 256), BF16),
        (ids,),
        (value, a1, a2, swap(a1, "core"), swap(a2, "core")),
    )
    r1 = both_ways(block, "z", 1)
    r2 = both_ways(r1, "z", 1)
    r3 = both_ways(r2, "z", 1)
    r4 = both_ways(lax.dynamic_slice_in_dim(r3, 2 * c, 2, 0), "z", 1)
    sent = [swap(pick(r, 1 - c, 2), "core") for r in (r1, r2, r3, r4)]
    values = project(ids, ones, (block, r1, r2, r3, r4, *sent), xs, weight_from_z, False)

    b = [both_ways(rest, "z", by) for by in (1, 2, 3)]
    b.append(both_ways(pick(rest, c), "z", 4))
    k_block, q_block = call(
        place_z_kernel,
        [jax.ShapeDtypeStruct((2, 2, 8, 32, 256), BF16)] * 2,
        (ids,),
        (rest, *b, *(swap(t, "core") for t in b)),
    )

    def round_x(block):
        r1 = both_ways(block, "x", 1)
        r2 = both_ways(pick(r1, c), "x", 1)
        return block, r1, r2, swap(pick(r1, 1 - c, 1), "core"), swap(pick(r2, 1 - c), "core")

    keys = project(ids, ones, round_x(k_block), xs, weight_from_x, True)
    queries = project(ids, gains, round_x(q_block), xs, weight_from_x, True)

    ring = ("x", "yh", "z")
    up = [(i, (i + 1) % 64) for i in range(64)]
    down = [((i + 1) % 64, i) for i in range(64)]
    vl, vr = lax.ppermute(values[1:], ring, up), lax.ppermute(values[1:], ring, down)
    kl, kr = lax.ppermute(keys[1:], ring, up), lax.ppermute(keys[1:], ring, down)
    o = call(
        attend_kernel,
        jax.ShapeDtypeStruct((FRAMES, 128, 256), BF16),
        (),
        (queries, keys, values, kl, kr, vl, vr),
        flops=14 * 6 * 2 * 128 * 128 * 128,
    )
    o = lax.all_to_all(o.reshape(4, 2, 128, 256), ("yl", "core"), 0, 0)

    back = [(i + 1, i) for i in range(3)]
    next_x = lax.ppermute(frames_in[0], ("yl", "core"), back)
    next_level = lax.ppermute(levels[:1], ("yl", "core"), back)
    now = jnp.concatenate([levels[1:], next_level])
    a_now = alpha_bar(now)
    a_later = alpha_bar(jnp.maximum(now - LEVELS // FRAMES, 0))
    coefs = jnp.stack(
        [jnp.sqrt(a_later), jnp.sqrt(1.0 - a_now), 1.0 / jnp.sqrt(a_now), jnp.sqrt(1.0 - a_later)],
        axis=1,
    ).reshape(8)
    out_half = out_half.reshape(4, 8, 2, 16, 1024)
    return call(
        finish_kernel,
        jax.ShapeDtypeStruct(frames_in.shape, BF16),
        (ids, coefs),
        (o, out_half, swap(out_half, "core"), frames_in[1], next_x, fresh),
        flops=2 * 256 * 1024 * 2048,
    )


def solution(mesh):
    cut = Mesh(mesh.devices.reshape(SIZES), AXES)
    frame, space = ("yl", "core"), ("x", "yh", "z")
    return jax.shard_map(
        body,
        mesh=cut,
        in_specs=(
            P(frame, space, None),
            P(frame),
            P(space, None),
            P(),
            P(space, None),
            P(),
            P(space, None),
        ),
        out_specs=P(frame, space, None),
        check_vma=False,
    )
```

time: 451 us -> 185 us (0.41)
  waiting for transfers between devices: 352 us -> 40.5 us
  starting transfers between devices: 9.34 us -> 74.6 us
  matrix products: 27.2 us -> 0.38 us
  Pallas kernels: 0 us -> 25.5 us
  other arithmetic: 16.7 us -> 2.86 us
    all_gather x4 -> x1, waiting for transfers between devices: 317 us -> 17.8 us  [body(): lax.all_gather(pair[:, 192:].reshape(32, 1024), ('x', 'z'), axis=0, tiled...]
    ppermute x3 -> x39, starting transfers between devices: 9.22 us -> 70.7 us  [the longest x19 28.9 us: swap(): return lax.ppermute(array, axis, [(0, 1), (1, 0)])]
    dot_general x7 -> x1, matrix products: 27.2 us -> 0.38 us  [body(): jnp.dot(embed(levels, w_mod.shape[0]), w_mod, preferred_element_type=F32)]
    pallas_call x0 -> x8, Pallas kernels: none -> 25.5 us  [call(): pl.pallas_call(body, out_shape=out_shape, in_specs=specs, out_specs=jax.t...]
    ppermute x3 -> x39, waiting for transfers between devices: 34.2 us -> 16.2 us  [the longest x14 7.59 us: both_ways(): return lax.ppermute(array, ('core', axis), pairs)]
    dot_general x2 -> x0, local copies, waits for them, and re-layouts: 18 us -> none  [the longest x1 15.7 us: body(): jnp.dot(columns, lax.all_gather(w_qkv, 'space', axis=0, tiled=True), pref...]
    squeeze x0 -> x13, local copies, waits for them, and re-layouts: none -> 10.7 us  [the longest x12 9.64 us: pick(): return lax.dynamic_index_in_dim(array, index, axis, keepdims=False)]
    reduce_sum x5 -> x0, other arithmetic: 8.19 us -> none  [the longest x1 3.79 us: body(): sums = jnp.sum(probs, axis=-1)]
  transfers between devices with their start and end apart: 7 -> 41, of which waited for: 7 -> 12; matrix products, arithmetic and copies ran while one was open for 8% -> 9% of each run, Pallas kernels for 0% -> 11%
where the time goes in v1:
time: 185 us; the launch traced here: 184 us
  starting transfers between devices  74.6 us (40%)
  waiting for transfers between devices  40.5 us (22%)
  local copies, waits for them, and re-layouts  26.8 us (14%)
  Pallas kernels  25.5 us (14%)
  between operations  13.8 us (7%)
  other arithmetic  2.86 us (2%)
    ppermute x19, starting transfers between devices, swap(): return lax.ppermute(array, axis, [(0, 1), (1, 0)])  28.9 us
    pallas_call x8, Pallas kernels, call(): pl.pallas_call(body, out_shape=out_shape, in_specs=specs, out_specs=jax.t...  25.5 us
    ppermute x14, starting transfers between devices, both_ways(): return lax.ppermute(array, ('core', axis), pairs)  22.2 us
    all_gather x1, waiting for transfers between devices, body(): lax.all_gather(pair[:, 192:].reshape(32, 1024), ('x', 'z'), axis=0, tiled...  17.8 us
    unnamed x37, local copies, waits for them, and re-layouts  11.4 us
    squeeze x12, local copies, waits for them, and re-layouts, pick(): return lax.dynamic_index_in_dim(array, index, axis, keepdims=False)  9.64 us
    ppermute x14, waiting for transfers between devices, both_ways(): return lax.ppermute(array, ('core', axis), pairs)  7.59 us
    ppermute x1, starting transfers between devices, body(): lax.ppermute(keys[1:], ring, down)  7.24 us
  transfers between devices with their start and end apart: 41, of which 12 were waited for; matrix products, arithmetic and copies ran while one was open for 9% of the time, Pallas kernels for 11%

profile of v1, /device:TPU:1, one launch (start us, length us, event | category | flops | bytes accessed | tf_op | source)
XLA Modules:
  0.0 184.5 jit_solution(3389413337931171682)
XLA Ops:
  7.5 1.1 reshape.161
  8.7 3.8 %collective-permute-start.1 = (bf16[256,256]{1,0:T(8,128)(2,1)S(1)}, bf16[256,256]{1,0:T(8,128)(2,1)S(1)}, u32[]{:S(2)}, u32[]{:S(2)}) collective-permute-start(bf16[256,256]{1,0:T(8,128)(2,1)S(1)} %pad_maximum_fusion), channel_id=1, source_target_pairs={{0,8},{8,0},{1,9},{9,1},{2,10},{10,2},{3,11},{11,3},{4,12},{12,4},... | collective-permute-start | bytes 393224 | tf_op jit(solution)/shard_map/ppermute | solution.py:34
  12.6 2.4 %collective-permute-done.1 = bf16[256,256]{1,0:T(8,128)(2,1)S(1)} collective-permute-done((bf16[256,256]{1,0:T(8,128)(2,1)S(1)}, bf16[256,256]{1,0:T(8,128)(2,1)S(1)}, u32[]{:S(2)}, u32[]{:S(2)}) %collective-permute-start.1) | collective-permute-done | bytes 131104 | tf_op jit(solution)/shard_map/ppermute | solution.py:34
  16.2 1.2 copy-done.1
  17.5 1.9 %shard_map.74.refs_5_.refs_9_ = bf16[2,128,2048]{2,1,0:T(8,128)(2,1)S(1)} custom-call(bf16[2,128,2048]{2,1,0:T(8,128)(2,1)S(1)} %copy-done.1, f32[2,2048]{1,0:T(2,128)S(1)} %get-tuple-element.21.shift_ref, f32[2,2048]{1,0:T(2,128)S(1)} %get-tuple-element.20.scale_ref), custom_call_target="tpu_custom_call" | custom-call | flops 10485760 | bytes 2129920 | tf_op jit(solution)/shard_map/pallas_call | solution.py:53
  19.4 2.0 %collective-permute-start.15 = (bf16[2,128,2048]{2,1,0:T(8,128)(2,1)S(1)}, bf16[2,128,2048]{2,1,0:T(8,128)(2,1)}, u32[]{:S(2)}, u32[]{:S(2)}) collective-permute-start(bf16[2,128,2048]{2,1,0:T(8,128)(2,1)S(1)} %shard_map.74.refs_5_.refs_9_), channel_id=1, source_target_pairs={{0,128},{128,0},{1,129},{129,1},{2,130},{130,2},{3,131},{131,3},{4... | collective-permute-start | bytes 3145736 | tf_op jit(solution)/shard_map/ppermute | solution.py:34
  21.4 5.7 %collective-permute-start.2 = (bf16[2,2,2,32,256]{4,3,2,1,0:T(8,128)(2,1)S(1)}, bf16[2,2,2,32,256]{4,3,2,1,0:T(8,128)(2,1)}, u32[]{:S(2)}, u32[]{:S(2)}) collective-permute-start(bf16[2,2,2,32,256]{4,3,2,1,0:T(8,128)(2,1)S(1)} %slice.67.own_ref), channel_id=1, source_target_pairs={{0,1},{1,2},{2,3},{3,4},{4,5},{5,6},{6,7},{7,0},{64,71},{65,64},{6... | collective-permute-start | bytes 393224 | tf_op jit(solution)/shard_map/ppermute | solution.py:41
  27.1 1.5 collective-permute-start.5
  28.6 2.8 %collective-permute-start.22 = (bf16[2,32,256]{2,1,0:T(8,128)(2,1)S(1)}, bf16[2,32,256]{2,1,0:T(8,128)(2,1)S(1)}, u32[]{:S(2)}, u32[]{:S(2)}) collective-permute-start(bf16[2,32,256]{2,1,0:T(8,128)(2,1)S(1)} %dynamic-slice_bitcast_fusion.11), channel_id=1, source_target_pairs={{0,32},{16,48},{32,0},{48,16},{64,96},{80,112},{96,64},{112,80},{1... | collective-permute-start | bytes 98312 | tf_op jit(solution)/shard_map/ppermute | solution.py:41
  32.9 2.8 %collective-permute-done.5.r4 = bf16[2,2,32,256]{3,2,1,0:T(8,128)(2,1)} collective-permute-done((bf16[2,2,32,256]{3,2,1,0:T(8,128)(2,1)S(1)}, bf16[2,2,32,256]{3,2,1,0:T(8,128)(2,1)}, u32[]{:S(2)}, u32[]{:S(2)}) %collective-permute-start.5) | collective-permute-done | bytes 65568 | tf_op jit(solution)/shard_map/ppermute | solution.py:41
  35.7 1.9 %collective-permute-start.4 = (bf16[2,2,2,32,256]{4,3,2,1,0:T(8,128)(2,1)S(1)}, bf16[2,2,2,32,256]{4,3,2,1,0:T(8,128)(2,1)}, u32[]{:S(2)}, u32[]{:S(2)}) collective-permute-start(bf16[2,2,2,32,256]{4,3,2,1,0:T(8,128)(2,1)S(1)} %slice.67.own_ref), channel_id=1, source_target_pairs={{0,3},{1,4},{2,5},{3,6},{4,7},{5,0},{6,1},{7,2},{64,69},{65,70},{6... | collective-permute-start | bytes 393224 | tf_op jit(solution)/shard_map/ppermute | solution.py:41
  37.6 3.2 %collective-permute-start.24 = (bf16[2,32,256]{2,1,0:T(8,128)(2,1)S(1)}, bf16[2,32,256]{2,1,0:T(8,128)(2,1)S(1)}, u32[]{:S(2)}, u32[]{:S(2)}) collective-permute-start(bf16[2,32,256]{2,1,0:T(8,128)(2,1)S(1)} %collective-permute-done.22.r2), channel_id=1, source_target_pairs={{0,64},{64,0},{1,65},{65,1},{2,66},{66,2},{3,67},{67,3},{4,68},{68... | collective-permute-start | bytes 98312 | tf_op jit(solution)/shard_map/ppermute | solution.py:34
  43.4 4.9 %collective-permute-start.6 = (bf16[2,2,2,32,256]{4,3,2,1,0:T(8,128)(2,1)}, bf16[2,2,2,32,256]{4,3,2,1,0:T(8,128)(2,1)}, u32[]{:S(2)}, u32[]{:S(2)}) collective-permute-start(bf16[2,2,2,32,256]{4,3,2,1,0:T(8,128)(2,1)} %collective-permute-done.2.r1), channel_id=1, source_target_pairs={{0,64},{64,0},{1,65},{65,1},{2,66},{66,2},{3,67},{67,3},{4,68},{68... | collective-permute-start | bytes 393224 | tf_op jit(solution)/shard_map/ppermute | solution.py:34
  48.3 1.8 collective-permute-start.7
  55.6 2.3 %shard_map.73 = (bf16[2,2,8,32,256]{4,3,2,1,0:T(8,128)(2,1)}, bf16[2,2,8,32,256]{4,3,2,1,0:T(8,128)(2,1)}) custom-call(s32[9]{0:T(128)S(1)} %stack.62.ids, bf16[2,2,2,32,256]{4,3,2,1,0:T(8,128)(2,1)S(1)} %slice.67.own_ref, bf16[2,2,2,32,256]{4,3,2,1,0:T(8,128)(2,1)} %collective-permute-done.2.r1, bf16[2,2,2,32,256]{4,3,2,1,0:T(8,128)(2,1)} %collective-permute-done.3.r2, ...), custom_call_target="tpu_custom_call" | custom-call | bytes 2097152 | tf_op jit(solution)/shard_map/pallas_call | solution.py:53
  57.9 2.3 %collective-permute-start.17 = (bf16[2,2,8,32,256]{4,3,2,1,0:T(8,128)(2,1)}, bf16[2,2,8,32,256]{4,3,2,1,0:T(8,128)(2,1)}, u32[]{:S(2)}, u32[]{:S(2)}) collective-permute-start(bf16[2,2,8,32,256]{4,3,2,1,0:T(8,128)(2,1)} %get-tuple-element.8.refs_0_), channel_id=1, source_target_pairs={{0,16},{16,32},{32,48},{48,0},{64,112},{80,64},{96,80},{112,96},{1... | collective-permute-start | bytes 1572872 | tf_op jit(solution)/shard_map/ppermute | solution.py:41
  60.3 1.9 %collective-permute-start.14 = (bf16[2,128,2048]{2,1,0:T(8,128)(2,1)S(1)}, bf16[2,128,2048]{2,1,0:T(8,128)(2,1)}, u32[]{:S(2)}, u32[]{:S(2)}) collective-permute-start(bf16[2,128,2048]{2,1,0:T(8,128)(2,1)S(1)} %shard_map.74.refs_5_.refs_9_), channel_id=1, source_target_pairs={{0,64},{64,0},{1,65},{65,1},{2,66},{66,2},{3,67},{67,3},{4,68},{68... | collective-permute-start | bytes 3145736 | tf_op jit(solution)/shard_map/ppermute | solution.py:34
  62.2 1.3 collective-permute-start.10
  65.9 3.3 %collective-permute-done.26.refs_2_ = bf16[4,2,2,32,256]{4,3,2,1,0:T(8,128)(2,1)} collective-permute-done((bf16[4,2,2,32,256]{4,3,2,1,0:T(8,128)(2,1)}, bf16[4,2,2,32,256]{4,3,2,1,0:T(8,128)(2,1)}, u32[]{:S(2)}, u32[]{:S(2)}) %collective-permute-start.26) | collective-permute-done | bytes 262176 | tf_op jit(solution)/shard_map/ppermute | solution.py:41
  69.3 2.4 %collective-permute-start.29 = (bf16[4,2,32,256]{3,2,1,0:T(8,128)(2,1)S(1)}, bf16[4,2,32,256]{3,2,1,0:T(8,128)(2,1)S(1)}, u32[]{:S(2)}, u32[]{:S(2)}) collective-permute-start(bf16[4,2,32,256]{3,2,1,0:T(8,128)(2,1)S(1)} %dynamic-slice_bitcast_fusion.6), channel_id=1, source_target_pairs={{0,64},{64,0},{1,65},{65,1},{2,66},{66,2},{3,67},{67,3},{4,68},{68... | collective-permute-start | bytes 393224 | tf_op jit(solution)/shard_map/ppermute | solution.py:34
  71.6 1.6 dynamic-slice_bitcast_fusion.5
  73.3 1.7 dynamic-slice_bitcast_fusion.1
  75.0 2.4 %collective-permute-start.18 = (bf16[2,8,32,256]{3,2,1,0:T(8,128)(2,1)}, bf16[2,8,32,256]{3,2,1,0:T(8,128)(2,1)}, u32[]{:S(2)}, u32[]{:S(2)}) collective-permute-start(bf16[2,8,32,256]{3,2,1,0:T(8,128)(2,1)} %dynamic-slice_bitcast_fusion.1), channel_id=1, source_target_pairs={{0,16},{16,32},{32,48},{48,0},{64,112},{80,64},{96,80},{112,96},{1... | collective-permute-start | bytes 786440 | tf_op jit(solution)/shard_map/ppermute | solution.py:41
  77.4 1.7 dynamic-slice_bitcast_fusion.3
  79.1 17.8 %all-gather.2.cloned.1.call-done = bf16[1024,1024]{1,0:T(8,128)(2,1)} async-done(((bf16[32,1024]{1,0:T(8,128)(2,1)}), bf16[1024,1024]{1,0:T(8,128)(2,1)}) %all-gather.2.cloned.1.call-update) | async-done | bytes 2097168 | tf_op jit(solution)/shard_map/all_gather | solution.py:243
  96.9 4.6 %collective-permute-start.37 = (bf16[4,8,2,16,1024]{4,3,2,1,0:T(8,128)(2,1)}, bf16[4,8,2,16,1024]{4,3,2,1,0:T(8,128)(2,1)}, u32[]{:S(2)}, u32[]{:S(2)}) collective-permute-start(bf16[4,8,2,16,1024]{4,3,2,1,0:T(8,128)(2,1)} %bitcast.58), channel_id=1, source_target_pairs={{0,64},{64,0},{1,65},{65,1},{2,66},{66,2},{3,67},{67,3},{4,68},{68... | collective-permute-start | bytes 6291464 | tf_op jit(solution)/shard_map/ppermute | solution.py:34
  104.5 1.2 collective-permute-done.30.refs_6_
  106.7 1.6 collective-permute-start.28
  110.9 2.5 %collective-permute-start.20 = (bf16[8,32,256]{2,1,0:T(8,128)(2,1)S(1)}, bf16[8,32,256]{2,1,0:T(8,128)(2,1)S(1)}, u32[]{:S(2)}, u32[]{:S(2)}) collective-permute-start(bf16[8,32,256]{2,1,0:T(8,128)(2,1)S(1)} %dynamic-slice_bitcast_fusion.7), channel_id=1, source_target_pairs={{0,64},{64,0},{1,65},{65,1},{2,66},{66,2},{3,67},{67,3},{4,68},{68... | collective-permute-start | bytes 393224 | tf_op jit(solution)/shard_map/ppermute | solution.py:34
  114.9 3.8 %shard_map.76.k_ref = bf16[8,128,256]{2,1,0:T(8,128)(2,1)S(1)} custom-call(s32[9]{0:T(128)S(1)} %stack.62.ids, f32[2]{0:T(128)S(1)} %broadcast_13_gains.2.gains, bf16[2,2,8,32,256]{4,3,2,1,0:T(8,128)(2,1)} %get-tuple-element.8.refs_0_, bf16[2,2,8,32,256]{4,3,2,1,0:T(8,128)(2,1)} %collective-permute-done.17.refs_1_, ...), custom_call_target="tpu_custom_call" | custom-call | flops 1073741824 | bytes 6422528 | tf_op jit(solution)/shard_map/pallas_call | solution.py:53
  118.7 2.4 %collective-permute-start = (s32[1]{0:T(128)}, s32[1]{0:T(128)}, u32[]{:S(2)}, u32[]{:S(2)}) collective-permute-start(s32[1]{0:T(128)} %get-tuple-element.25), channel_id=1, source_target_pairs={{64,0},{128,64},{192,128},{65,1},{129,65},{193,129},{66,2},{130,66... | collective-permute-start | bytes 20 | tf_op jit(solution)/shard_map/ppermute | solution.py:302
  121.4 3.5 %shard_map.78.v_ref = bf16[8,128,256]{2,1,0:T(8,128)(2,1)S(1)} custom-call(s32[9]{0:T(128)S(1)} %stack.62.ids, f32[2]{0:T(128)S(1)} %broadcast_13_gains.2.gains, bf16[4,2,2,32,256]{4,3,2,1,0:T(8,128)(2,1)S(1)} %shard_map.77.refs_0_, bf16[4,2,2,32,256]{4,3,2,1,0:T(8,128)(2,1)} %collective-permute-done.25.refs_1_, ...), custom_call_target="tpu_custom_call" | custom-call | flops 1073741824 | bytes 6356992 | tf_op jit(solution)/shard_map/pallas_call | solution.py:53
  125.0 7.2 %collective-permute-start.34 = (bf16[7,128,256]{2,1,0:T(8,128)(2,1)S(1)}, bf16[7,128,256]{2,1,0:T(8,128)(2,1)S(1)}, u32[]{:S(2)}, u32[]{:S(2)}) collective-permute-start(bf16[7,128,256]{2,1,0:T(8,128)(2,1)S(1)} %slice.71), channel_id=1, source_target_pairs={{1,0},{2,1},{3,2},{4,3},{5,4},{6,5},{7,6},{8,7},{9,8},{10,9},{11,1... | collective-permute-start | bytes 1376264 | tf_op jit(solution)/shard_map/ppermute | solution.py:290
  132.2 7.2 %collective-permute-start.36 = (bf16[7,128,256]{2,1,0:T(8,128)(2,1)S(1)}, bf16[7,128,256]{2,1,0:T(8,128)(2,1)S(1)}, u32[]{:S(2)}, u32[]{:S(2)}) collective-permute-start(bf16[7,128,256]{2,1,0:T(8,128)(2,1)S(1)} %slice.72), channel_id=1, source_target_pairs={{1,0},{2,1},{3,2},{4,3},{5,4},{6,5},{7,6},{8,7},{9,8},{10,9},{11,1... | collective-permute-start | bytes 1376264 | tf_op jit(solution)/shard_map/ppermute | solution.py:289
  139.4 1.1 slice_bitcast_fusion
  140.5 1.3 fusion.9
  141.8 2.4 %collective-permute-start.38 = (bf16[128,2048]{1,0:T(8,128)(2,1)}, bf16[128,2048]{1,0:T(8,128)(2,1)}, u32[]{:S(2)}, u32[]{:S(2)}) collective-permute-start(bf16[128,2048]{1,0:T(8,128)(2,1)} %get-tuple-element.11), channel_id=1, source_target_pairs={{64,0},{128,64},{192,128},{65,1},{129,65},{193,129},{66,2},{130,66... | collective-permute-start | bytes 1572872 | tf_op jit(solution)/shard_map/ppermute | solution.py:301
  144.2 3.7 %shard_map.75.q_ref = bf16[8,128,256]{2,1,0:T(8,128)(2,1)S(1)} custom-call(s32[9]{0:T(128)S(1)} %stack.62.ids, f32[2]{0:T(128)S(1)} %dynamic_slice.56.gains, bf16[2,2,8,32,256]{4,3,2,1,0:T(8,128)(2,1)} %get-tuple-element.7.refs_0_, bf16[2,2,8,32,256]{4,3,2,1,0:T(8,128)(2,1)} %collective-permute-done.10.refs_1_, ...), custom_call_target="tpu_custom_call" | custom-call | flops 1073741824 | bytes 6422528 | tf_op jit(solution)/shard_map/pallas_call | solution.py:53
  147.9 2.2 %collective-permute-done.35.vl_ref = bf16[7,128,256]{2,1,0:T(8,128)(2,1)S(1)} collective-permute-done((bf16[7,128,256]{2,1,0:T(8,128)(2,1)S(1)}, bf16[7,128,256]{2,1,0:T(8,128)(2,1)S(1)}, u32[]{:S(2)}, u32[]{:S(2)}) %collective-permute-start.35) | collective-permute-done | bytes 458784 | tf_op jit(solution)/shard_map/ppermute | solution.py:289
  150.2 2.1 %collective-permute-done.36.vr_ref = bf16[7,128,256]{2,1,0:T(8,128)(2,1)S(1)} collective-permute-done((bf16[7,128,256]{2,1,0:T(8,128)(2,1)S(1)}, bf16[7,128,256]{2,1,0:T(8,128)(2,1)S(1)}, u32[]{:S(2)}, u32[]{:S(2)}) %collective-permute-start.36) | collective-permute-done | bytes 458784 | tf_op jit(solution)/shard_map/ppermute | solution.py:289
  152.3 5.5 %shard_map.79 = bf16[8,128,256]{2,1,0:T(8,128)(2,1)} custom-call(bf16[8,128,256]{2,1,0:T(8,128)(2,1)S(1)} %shard_map.75.q_ref, bf16[8,128,256]{2,1,0:T(8,128)(2,1)S(1)} %shard_map.76.k_ref, bf16[8,128,256]{2,1,0:T(8,128)(2,1)S(1)} %shard_map.78.v_ref, bf16[7,128,256]{2,1,0:T(8,128)(2,1)S(1)} %collective-permute-done.33.kl_ref, ...), custom_call_target="tpu_custom_call" | custom-call | flops 352321536 | bytes 3932160 | tf_op jit(solution)/shard_map/pallas_call | solution.py:53
  157.7 4.0 %all-to-all-start = ((bf16[4,2,128,256]{3,2,1,0:T(8,128)(2,1)}), bf16[4,2,128,256]{3,2,1,0:T(8,128)(2,1)S(1)}, u32[]{:S(2)}, u32[]{:S(2)}) async-start(bf16[4,2,128,256]{3,2,1,0:T(8,128)(2,1)} %bitcast.31), calls=%async_computation | async-start | bytes 1048576 | tf_op jit(solution)/shard_map/all_to_all | solution.py:298
  161.7 1.3 subtract_sqrt_fusion.1
  163.1 6.5 %all-to-all-done.o_ref = bf16[4,2,128,256]{3,2,1,0:T(8,128)(2,1)S(1)} async-done(((bf16[4,2,128,256]{3,2,1,0:T(8,128)(2,1)}), bf16[4,2,128,256]{3,2,1,0:T(8,128)(2,1)S(1)}, u32[]{:S(2)}, u32[]{:S(2)}) %all-to-all-start) | async-done | bytes 524320 | tf_op jit(solution)/shard_map/all_to_all | solution.py:298
  169.7 1.6 copy-done.3
  171.3 1.0 copy-done.4
  172.3 1.0 copy-done.5
  173.3 4.3 %shard_map.80 = bf16[2,128,2048]{2,1,0:T(8,128)(2,1)} custom-call(s32[9]{0:T(128)S(1)} %stack.62.ids, f32[8]{0:T(128)S(1)} %reshape.160.coefs, bf16[4,2,128,256]{3,2,1,0:T(8,128)(2,1)S(1)} %all-to-all-done.o_ref, bf16[4,8,2,16,1024]{4,3,2,1,0:T(8,128)(2,1)S(1)} %bitcast.59, bf16[4,8,2,16,1024]{4,3,2,1,0:T(8,128)(2,1)} %collective-permute-done.37.wb_ref, ...), custom_call_target="tpu_custom_call" | custom-call | flops 1073741824 | bytes 7340032 | tf_op jit(solution)/shard_map/pallas_call | solution.py:53
  (123 shorter events, 23.2 us)
Async XLA Ops:
  6.5 9.3 %copy-start = (bf16[256,4096]{1,0:T(8,128)(2,1)S(1)}, bf16[256,4096]{1,0:T(8,128)(2,1)}, u32[]{:S(2)}) copy-start(bf16[256,4096]{1,0:T(8,128)(2,1)} %param.10) | copy-start | bytes 6291460
  6.5 9.2 %copy-start.16 = (s32[2]{0:T(128)S(1)}, s32[2]{0:T(128)}, u32[]{:S(2)}) copy-start(s32[2]{0:T(128)} %param.8) | copy-start | bytes 28
  6.5 90.3 %all-gather.2.cloned.1.call-start = ((), (), s32[]{:S(2)}) async-start(), calls=%async_computation.1 | async-start | bytes 2162688 | tf_op jit(solution)/shard_map/all_gather | solution.py:243
  8.7 6.2 %collective-permute-start.1 = (bf16[256,256]{1,0:T(8,128)(2,1)S(1)}, bf16[256,256]{1,0:T(8,128)(2,1)S(1)}, u32[]{:S(2)}, u32[]{:S(2)}) collective-permute-start(bf16[256,256]{1,0:T(8,128)(2,1)S(1)} %pad_maximum_fusion), channel_id=1, source_target_pairs={{0,8},{8,0},{1,9},{9,1},{2,10},{10,2},{3,11},{11,3},{4,12},{12,4},... | collective-permute-start | bytes 393224 | tf_op jit(solution)/shard_map/ppermute | solution.py:34
  16.2 1.2 copy-start.1
  17.5 46.8 %copy-start.17 = (f32[8]{0:T(128)S(1)}, f32[8]{0:T(128)}, u32[]{:S(2)}) copy-start(f32[8]{0:T(128)} %param.12) | copy-start | bytes 100
  19.4 53.8 %collective-permute-start.15 = (bf16[2,128,2048]{2,1,0:T(8,128)(2,1)S(1)}, bf16[2,128,2048]{2,1,0:T(8,128)(2,1)}, u32[]{:S(2)}, u32[]{:S(2)}) collective-permute-start(bf16[2,128,2048]{2,1,0:T(8,128)(2,1)S(1)} %shard_map.74.refs_5_.refs_9_), channel_id=1, source_target_pairs={{0,128},{128,0},{1,129},{129,1},{2,130},{130,2},{3,131},{131,3},{4... | collective-permute-start | bytes 3145736 | tf_op jit(solution)/shard_map/ppermute | solution.py:34
  21.4 21.8 %collective-permute-start.2 = (bf16[2,2,2,32,256]{4,3,2,1,0:T(8,128)(2,1)S(1)}, bf16[2,2,2,32,256]{4,3,2,1,0:T(8,128)(2,1)}, u32[]{:S(2)}, u32[]{:S(2)}) collective-permute-start(bf16[2,2,2,32,256]{4,3,2,1,0:T(8,128)(2,1)S(1)} %slice.67.own_ref), channel_id=1, source_target_pairs={{0,1},{1,2},{2,3},{3,4},{4,5},{5,6},{6,7},{7,0},{64,71},{65,64},{6... | collective-permute-start | bytes 393224 | tf_op jit(solution)/shard_map/ppermute | solution.py:41
  27.1 8.6 %collective-permute-start.5 = (bf16[2,2,32,256]{3,2,1,0:T(8,128)(2,1)S(1)}, bf16[2,2,32,256]{3,2,1,0:T(8,128)(2,1)}, u32[]{:S(2)}, u32[]{:S(2)}) collective-permute-start(bf16[2,2,32,256]{3,2,1,0:T(8,128)(2,1)S(1)} %dynamic-slice_bitcast_fusion.10), channel_id=1, source_target_pairs={{0,4},{1,5},{2,6},{3,7},{4,0},{5,1},{6,2},{7,3},{64,68},{65,69},{6... | collective-permute-start | bytes 196616 | tf_op jit(solution)/shard_map/ppermute | solution.py:41
  28.5 19.8 %copy-start.6 = (bf16[2,2,32,256]{3,2,1,0:T(8,128)(2,1)}, bf16[2,2,32,256]{3,2,1,0:T(8,128)(2,1)S(1)}, u32[]{:S(2)}) copy-start(bf16[2,2,32,256]{3,2,1,0:T(8,128)(2,1)S(1)} %get-tuple-element.16.own_ref) | copy-start | bytes 196612
  28.6 4.4 %collective-permute-start.22 = (bf16[2,32,256]{2,1,0:T(8,128)(2,1)S(1)}, bf16[2,32,256]{2,1,0:T(8,128)(2,1)S(1)}, u32[]{:S(2)}, u32[]{:S(2)}) collective-permute-start(bf16[2,32,256]{2,1,0:T(8,128)(2,1)S(1)} %dynamic-slice_bitcast_fusion.11), channel_id=1, source_target_pairs={{0,32},{16,48},{32,0},{48,16},{64,96},{80,112},{96,64},{112,80},{1... | collective-permute-start | bytes 98312 | tf_op jit(solution)/shard_map/ppermute | solution.py:41
  31.4 6.2 %collective-permute-start.21 = (bf16[2,2,32,256]{3,2,1,0:T(8,128)(2,1)S(1)}, bf16[2,2,32,256]{3,2,1,0:T(8,128)(2,1)S(1)}, u32[]{:S(2)}, u32[]{:S(2)}) collective-permute-start(bf16[2,2,32,256]{3,2,1,0:T(8,128)(2,1)S(1)} %get-tuple-element.16.own_ref), channel_id=1, source_target_pairs={{0,16},{16,32},{32,48},{48,0},{64,112},{80,64},{96,80},{112,96},{1... | collective-permute-start | bytes 196616 | tf_op jit(solution)/shard_map/ppermute | solution.py:41
  32.9 10.5 %collective-permute-start.3 = (bf16[2,2,2,32,256]{4,3,2,1,0:T(8,128)(2,1)S(1)}, bf16[2,2,2,32,256]{4,3,2,1,0:T(8,128)(2,1)}, u32[]{:S(2)}, u32[]{:S(2)}) collective-permute-start(bf16[2,2,2,32,256]{4,3,2,1,0:T(8,128)(2,1)S(1)} %slice.67.own_ref), channel_id=1, source_target_pairs={{0,2},{1,3},{2,4},{3,5},{4,6},{5,7},{6,0},{7,1},{64,70},{65,71},{6... | collective-permute-start | bytes 393224 | tf_op jit(solution)/shard_map/ppermute | solution.py:41
  35.7 12.6 %collective-permute-start.4 = (bf16[2,2,2,32,256]{4,3,2,1,0:T(8,128)(2,1)S(1)}, bf16[2,2,2,32,256]{4,3,2,1,0:T(8,128)(2,1)}, u32[]{:S(2)}, u32[]{:S(2)}) collective-permute-start(bf16[2,2,2,32,256]{4,3,2,1,0:T(8,128)(2,1)S(1)} %slice.67.own_ref), channel_id=1, source_target_pairs={{0,3},{1,4},{2,5},{3,6},{4,7},{5,0},{6,1},{7,2},{64,69},{65,70},{6... | collective-permute-start | bytes 393224 | tf_op jit(solution)/shard_map/ppermute | solution.py:41
  37.6 4.1 %collective-permute-start.24 = (bf16[2,32,256]{2,1,0:T(8,128)(2,1)S(1)}, bf16[2,32,256]{2,1,0:T(8,128)(2,1)S(1)}, u32[]{:S(2)}, u32[]{:S(2)}) collective-permute-start(bf16[2,32,256]{2,1,0:T(8,128)(2,1)S(1)} %collective-permute-done.22.r2), channel_id=1, source_target_pairs={{0,64},{64,0},{1,65},{65,1},{2,66},{66,2},{3,67},{67,3},{4,68},{68... | collective-permute-start | bytes 98312 | tf_op jit(solution)/shard_map/ppermute | solution.py:34
  42.3 7.9 %collective-permute-start.23 = (bf16[2,2,32,256]{3,2,1,0:T(8,128)(2,1)S(1)}, bf16[2,2,32,256]{3,2,1,0:T(8,128)(2,1)S(1)}, u32[]{:S(2)}, u32[]{:S(2)}) collective-permute-start(bf16[2,2,32,256]{3,2,1,0:T(8,128)(2,1)S(1)} %collective-permute-done.21.r1), channel_id=1, source_target_pairs={{0,64},{64,0},{1,65},{65,1},{2,66},{66,2},{3,67},{67,3},{4,68},{68... | collective-permute-start | bytes 196616 | tf_op jit(solution)/shard_map/ppermute | solution.py:34
  43.2 12.2 %collective-permute-start.9 = (bf16[2,2,32,256]{3,2,1,0:T(8,128)(2,1)}, bf16[2,2,32,256]{3,2,1,0:T(8,128)(2,1)}, u32[]{:S(2)}, u32[]{:S(2)}) collective-permute-start(bf16[2,2,32,256]{3,2,1,0:T(8,128)(2,1)} %collective-permute-done.5.r4), channel_id=1, source_target_pairs={{0,64},{64,0},{1,65},{65,1},{2,66},{66,2},{3,67},{67,3},{4,68},{68... | collective-permute-start | bytes 196616 | tf_op jit(solution)/shard_map/ppermute | solution.py:34
  43.4 12.2 %collective-permute-start.6 = (bf16[2,2,2,32,256]{4,3,2,1,0:T(8,128)(2,1)}, bf16[2,2,2,32,256]{4,3,2,1,0:T(8,128)(2,1)}, u32[]{:S(2)}, u32[]{:S(2)}) collective-permute-start(bf16[2,2,2,32,256]{4,3,2,1,0:T(8,128)(2,1)} %collective-permute-done.2.r1), channel_id=1, source_target_pairs={{0,64},{64,0},{1,65},{65,1},{2,66},{66,2},{3,67},{67,3},{4,68},{68... | collective-permute-start | bytes 393224 | tf_op jit(solution)/shard_map/ppermute | solution.py:34
  48.3 7.2 %collective-permute-start.7 = (bf16[2,2,2,32,256]{4,3,2,1,0:T(8,128)(2,1)}, bf16[2,2,2,32,256]{4,3,2,1,0:T(8,128)(2,1)}, u32[]{:S(2)}, u32[]{:S(2)}) collective-permute-start(bf16[2,2,2,32,256]{4,3,2,1,0:T(8,128)(2,1)} %collective-permute-done.3.r2), channel_id=1, source_target_pairs={{0,64},{64,0},{1,65},{65,1},{2,66},{66,2},{3,67},{67,3},{4,68},{68... | collective-permute-start | bytes 393224 | tf_op jit(solution)/shard_map/ppermute | solution.py:34
  50.7 4.8 %collective-permute-start.8 = (bf16[2,2,2,32,256]{4,3,2,1,0:T(8,128)(2,1)}, bf16[2,2,2,32,256]{4,3,2,1,0:T(8,128)(2,1)}, u32[]{:S(2)}, u32[]{:S(2)}) collective-permute-start(bf16[2,2,2,32,256]{4,3,2,1,0:T(8,128)(2,1)} %collective-permute-done.4.r3), channel_id=1, source_target_pairs={{0,64},{64,0},{1,65},{65,1},{2,66},{66,2},{3,67},{67,3},{4,68},{68... | collective-permute-start | bytes 393224 | tf_op jit(solution)/shard_map/ppermute | solution.py:34
  55.5 8.0 %collective-permute-start.25 = (bf16[4,2,2,32,256]{4,3,2,1,0:T(8,128)(2,1)S(1)}, bf16[4,2,2,32,256]{4,3,2,1,0:T(8,128)(2,1)}, u32[]{:S(2)}, u32[]{:S(2)}) collective-permute-start(bf16[4,2,2,32,256]{4,3,2,1,0:T(8,128)(2,1)S(1)} %shard_map.77.refs_0_), channel_id=1, source_target_pairs={{0,1},{1,2},{2,3},{3,4},{4,5},{5,6},{6,7},{7,0},{64,71},{65,64},{6... | collective-permute-start | bytes 786440 | tf_op jit(solution)/shard_map/ppermute | solution.py:41
  57.9 15.3 %collective-permute-start.17 = (bf16[2,2,8,32,256]{4,3,2,1,0:T(8,128)(2,1)}, bf16[2,2,8,32,256]{4,3,2,1,0:T(8,128)(2,1)}, u32[]{:S(2)}, u32[]{:S(2)}) collective-permute-start(bf16[2,2,8,32,256]{4,3,2,1,0:T(8,128)(2,1)} %get-tuple-element.8.refs_0_), channel_id=1, source_target_pairs={{0,16},{16,32},{32,48},{48,0},{64,112},{80,64},{96,80},{112,96},{1... | collective-permute-start | bytes 1572872 | tf_op jit(solution)/shard_map/ppermute | solution.py:41
  60.3 46.4 %collective-permute-start.14 = (bf16[2,128,2048]{2,1,0:T(8,128)(2,1)S(1)}, bf16[2,128,2048]{2,1,0:T(8,128)(2,1)}, u32[]{:S(2)}, u32[]{:S(2)}) collective-permute-start(bf16[2,128,2048]{2,1,0:T(8,128)(2,1)S(1)} %shard_map.74.refs_5_.refs_9_), channel_id=1, source_target_pairs={{0,64},{64,0},{1,65},{65,1},{2,66},{66,2},{3,67},{67,3},{4,68},{68... | collective-permute-start | bytes 3145736 | tf_op jit(solution)/shard_map/ppermute | solution.py:34
  62.2 12.8 %collective-permute-start.10 = (bf16[2,2,8,32,256]{4,3,2,1,0:T(8,128)(2,1)}, bf16[2,2,8,32,256]{4,3,2,1,0:T(8,128)(2,1)}, u32[]{:S(2)}, u32[]{:S(2)}) collective-permute-start(bf16[2,2,8,32,256]{4,3,2,1,0:T(8,128)(2,1)} %get-tuple-element.7.refs_0_), channel_id=1, source_target_pairs={{0,16},{16,32},{32,48},{48,0},{64,112},{80,64},{96,80},{112,96},{1... | collective-permute-start | bytes 1572872 | tf_op jit(solution)/shard_map/ppermute | solution.py:41
  63.4 5.8 %collective-permute-start.26 = (bf16[4,2,2,32,256]{4,3,2,1,0:T(8,128)(2,1)}, bf16[4,2,2,32,256]{4,3,2,1,0:T(8,128)(2,1)}, u32[]{:S(2)}, u32[]{:S(2)}) collective-permute-start(bf16[4,2,2,32,256]{4,3,2,1,0:T(8,128)(2,1)} %collective-permute-done.25.refs_1_), channel_id=1, source_target_pairs={{0,1},{1,2},{2,3},{3,4},{4,5},{5,6},{6,7},{7,0},{64,71},{65,64},{6... | collective-permute-start | bytes 786440 | tf_op jit(solution)/shard_map/ppermute | solution.py:41
  69.3 9.8 %collective-permute-start.29 = (bf16[4,2,32,256]{3,2,1,0:T(8,128)(2,1)S(1)}, bf16[4,2,32,256]{3,2,1,0:T(8,128)(2,1)S(1)}, u32[]{:S(2)}, u32[]{:S(2)}) collective-permute-start(bf16[4,2,32,256]{3,2,1,0:T(8,128)(2,1)S(1)} %dynamic-slice_bitcast_fusion.6), channel_id=1, source_target_pairs={{0,64},{64,0},{1,65},{65,1},{2,66},{66,2},{3,67},{67,3},{4,68},{68... | collective-permute-start | bytes 393224 | tf_op jit(solution)/shard_map/ppermute | solution.py:34
  73.2 29.3 %collective-permute-start.27 = (bf16[4,2,2,32,256]{4,3,2,1,0:T(8,128)(2,1)}, bf16[4,2,2,32,256]{4,3,2,1,0:T(8,128)(2,1)}, u32[]{:S(2)}, u32[]{:S(2)}) collective-permute-start(bf16[4,2,2,32,256]{4,3,2,1,0:T(8,128)(2,1)} %collective-permute-done.26.refs_2_), channel_id=1, source_target_pairs={{0,1},{1,2},{2,3},{3,4},{4,5},{5,6},{6,7},{7,0},{64,71},{65,64},{6... | collective-permute-start | bytes 786440 | tf_op jit(solution)/shard_map/ppermute | solution.py:41
  73.2 41.5 %collective-permute-start.16 = (bf16[2,128,2048]{2,1,0:T(8,128)(2,1)}, bf16[2,128,2048]{2,1,0:T(8,128)(2,1)}, u32[]{:S(2)}, u32[]{:S(2)}) collective-permute-start(bf16[2,128,2048]{2,1,0:T(8,128)(2,1)} %collective-permute-done.15.refs_7_.refs_11_), channel_id=1, source_target_pairs={{0,64},{64,0},{1,65},{65,1},{2,66},{66,2},{3,67},{67,3},{4,68},{68... | collective-permute-start | bytes 3145736 | tf_op jit(solution)/shard_map/ppermute | solution.py:34
  75.0 31.7 %collective-permute-start.18 = (bf16[2,8,32,256]{3,2,1,0:T(8,128)(2,1)}, bf16[2,8,32,256]{3,2,1,0:T(8,128)(2,1)}, u32[]{:S(2)}, u32[]{:S(2)}) collective-permute-start(bf16[2,8,32,256]{3,2,1,0:T(8,128)(2,1)} %dynamic-slice_bitcast_fusion.1), channel_id=1, source_target_pairs={{0,16},{16,32},{32,48},{48,0},{64,112},{80,64},{96,80},{112,96},{1... | collective-permute-start | bytes 786440 | tf_op jit(solution)/shard_map/ppermute | solution.py:41
  96.9 72.8 %collective-permute-start.37 = (bf16[4,8,2,16,1024]{4,3,2,1,0:T(8,128)(2,1)}, bf16[4,8,2,16,1024]{4,3,2,1,0:T(8,128)(2,1)}, u32[]{:S(2)}, u32[]{:S(2)}) collective-permute-start(bf16[4,8,2,16,1024]{4,3,2,1,0:T(8,128)(2,1)} %bitcast.58), channel_id=1, source_target_pairs={{0,64},{64,0},{1,65},{65,1},{2,66},{66,2},{3,67},{67,3},{4,68},{68... | collective-permute-start | bytes 6291464 | tf_op jit(solution)/shard_map/ppermute | solution.py:34
  102.5 3.2 %collective-permute-start.30 = (bf16[4,2,32,256]{3,2,1,0:T(8,128)(2,1)}, bf16[4,2,32,256]{3,2,1,0:T(8,128)(2,1)S(1)}, u32[]{:S(2)}, u32[]{:S(2)}) collective-permute-start(bf16[4,2,32,256]{3,2,1,0:T(8,128)(2,1)} %dynamic-slice_bitcast_fusion.5), channel_id=1, source_target_pairs={{0,64},{64,0},{1,65},{65,1},{2,66},{66,2},{3,67},{67,3},{4,68},{68... | collective-permute-start | bytes 393224 | tf_op jit(solution)/shard_map/ppermute | solution.py:34
  105.7 7.7 %collective-permute-start.11 = (bf16[2,8,32,256]{3,2,1,0:T(8,128)(2,1)}, bf16[2,8,32,256]{3,2,1,0:T(8,128)(2,1)S(1)}, u32[]{:S(2)}, u32[]{:S(2)}) collective-permute-start(bf16[2,8,32,256]{3,2,1,0:T(8,128)(2,1)} %dynamic-slice_bitcast_fusion.3), channel_id=1, source_target_pairs={{0,16},{16,32},{32,48},{48,0},{64,112},{80,64},{96,80},{112,96},{1... | collective-permute-start | bytes 786440 | tf_op jit(solution)/shard_map/ppermute | solution.py:41
  106.7 7.1 %collective-permute-start.19 = (bf16[2,8,32,256]{3,2,1,0:T(8,128)(2,1)S(1)}, bf16[2,8,32,256]{3,2,1,0:T(8,128)(2,1)S(1)}, u32[]{:S(2)}, u32[]{:S(2)}) collective-permute-start(bf16[2,8,32,256]{3,2,1,0:T(8,128)(2,1)S(1)} %dynamic-slice_bitcast_fusion), channel_id=1, source_target_pairs={{0,64},{64,0},{1,65},{65,1},{2,66},{66,2},{3,67},{67,3},{4,68},{68... | collective-permute-start | bytes 786440 | tf_op jit(solution)/shard_map/ppermute | solution.py:34
  106.7 4.2 %collective-permute-start.28 = (bf16[2,2,2,32,256]{4,3,2,1,0:T(8,128)(2,1)S(1)}, bf16[2,2,2,32,256]{4,3,2,1,0:T(8,128)(2,1)S(1)}, u32[]{:S(2)}, u32[]{:S(2)}) collective-permute-start(bf16[2,2,2,32,256]{4,3,2,1,0:T(8,128)(2,1)S(1)} %constant_dynamic-slice_fusion), channel_id=1, source_target_pairs={{0,1},{1,2},{2,3},{3,4},{4,5},{5,6},{6,7},{7,0},{64,71},{65,64},{6... | collective-permute-start | bytes 393224 | tf_op jit(solution)/shard_map/ppermute | solution.py:41
  110.9 3.5 %collective-permute-start.20 = (bf16[8,32,256]{2,1,0:T(8,128)(2,1)S(1)}, bf16[8,32,256]{2,1,0:T(8,128)(2,1)S(1)}, u32[]{:S(2)}, u32[]{:S(2)}) collective-permute-start(bf16[8,32,256]{2,1,0:T(8,128)(2,1)S(1)} %dynamic-slice_bitcast_fusion.7), channel_id=1, source_target_pairs={{0,64},{64,0},{1,65},{65,1},{2,66},{66,2},{3,67},{67,3},{4,68},{68... | collective-permute-start | bytes 393224 | tf_op jit(solution)/shard_map/ppermute | solution.py:34
  113.4 18.8 %collective-permute-start.12 = (bf16[2,8,32,256]{3,2,1,0:T(8,128)(2,1)S(1)}, bf16[2,8,32,256]{3,2,1,0:T(8,128)(2,1)S(1)}, u32[]{:S(2)}, u32[]{:S(2)}) collective-permute-start(bf16[2,8,32,256]{3,2,1,0:T(8,128)(2,1)S(1)} %dynamic-slice_bitcast_fusion.2), channel_id=1, source_target_pairs={{0,64},{64,0},{1,65},{65,1},{2,66},{66,2},{3,67},{67,3},{4,68},{68... | collective-permute-start | bytes 786440 | tf_op jit(solution)/shard_map/ppermute | solution.py:34
  113.8 4.9 %collective-permute-start.31 = (bf16[4,2,32,256]{3,2,1,0:T(8,128)(2,1)S(1)}, bf16[4,2,32,256]{3,2,1,0:T(8,128)(2,1)S(1)}, u32[]{:S(2)}, u32[]{:S(2)}) collective-permute-start(bf16[4,2,32,256]{3,2,1,0:T(8,128)(2,1)S(1)} %dynamic-slice_bitcast_fusion.4), channel_id=1, source_target_pairs={{0,64},{64,0},{1,65},{65,1},{2,66},{66,2},{3,67},{67,3},{4,68},{68... | collective-permute-start | bytes 393224 | tf_op jit(solution)/shard_map/ppermute | solution.py:34
  114.4 6.8 %collective-permute-start.32 = (bf16[2,2,32,256]{3,2,1,0:T(8,128)(2,1)S(1)}, bf16[2,2,32,256]{3,2,1,0:T(8,128)(2,1)S(1)}, u32[]{:S(2)}, u32[]{:S(2)}) collective-permute-start(bf16[2,2,32,256]{3,2,1,0:T(8,128)(2,1)S(1)} %dynamic-slice_bitcast_fusion.9), channel_id=1, source_target_pairs={{0,64},{64,0},{1,65},{65,1},{2,66},{66,2},{3,67},{67,3},{4,68},{68... | collective-permute-start | bytes 196616 | tf_op jit(solution)/shard_map/ppermute | solution.py:34
  114.7 17.5 %collective-permute-start.13 = (bf16[8,32,256]{2,1,0:T(8,128)(2,1)S(1)}, bf16[8,32,256]{2,1,0:T(8,128)(2,1)S(1)}, u32[]{:S(2)}, u32[]{:S(2)}) collective-permute-start(bf16[8,32,256]{2,1,0:T(8,128)(2,1)S(1)} %dynamic-slice_bitcast_fusion.8), channel_id=1, source_target_pairs={{0,64},{64,0},{1,65},{65,1},{2,66},{66,2},{3,67},{67,3},{4,68},{68... | collective-permute-start | bytes 393224 | tf_op jit(solution)/shard_map/ppermute | solution.py:34
  118.7 20.7 %copy-start.2 = (bf16[2,128,2048]{2,1,0:T(8,128)(2,1)S(1)}, bf16[2,128,2048]{2,1,0:T(8,128)(2,1)}, u32[]{:S(2)}) copy-start(bf16[2,128,2048]{2,1,0:T(8,128)(2,1)} %x_ref.1) | copy-start | bytes 3145732
  118.7 6.2 %collective-permute-start = (s32[1]{0:T(128)}, s32[1]{0:T(128)}, u32[]{:S(2)}, u32[]{:S(2)}) collective-permute-start(s32[1]{0:T(128)} %get-tuple-element.25), channel_id=1, source_target_pairs={{64,0},{128,64},{192,128},{65,1},{129,65},{193,129},{66,2},{130,66... | collective-permute-start | bytes 20 | tf_op jit(solution)/shard_map/ppermute | solution.py:302
  121.1 20.7 %collective-permute-start.33 = (bf16[7,128,256]{2,1,0:T(8,128)(2,1)S(1)}, bf16[7,128,256]{2,1,0:T(8,128)(2,1)S(1)}, u32[]{:S(2)}, u32[]{:S(2)}) collective-permute-start(bf16[7,128,256]{2,1,0:T(8,128)(2,1)S(1)} %slice.71), channel_id=1, source_target_pairs={{0,1},{1,2},{2,3},{3,4},{4,5},{5,6},{6,7},{7,8},{8,9},{9,10},{10,1... | collective-permute-start | bytes 1376264 | tf_op jit(solution)/shard_map/ppermute | solution.py:290
  125.0 22.9 %collective-permute-start.34 = (bf16[7,128,256]{2,1,0:T(8,128)(2,1)S(1)}, bf16[7,128,256]{2,1,0:T(8,128)(2,1)S(1)}, u32[]{:S(2)}, u32[]{:S(2)}) collective-permute-start(bf16[7,128,256]{2,1,0:T(8,128)(2,1)S(1)} %slice.71), channel_id=1, source_target_pairs={{1,0},{2,1},{3,2},{4,3},{5,4},{6,5},{7,6},{8,7},{9,8},{10,9},{11,1... | collective-permute-start | bytes 1376264 | tf_op jit(solution)/shard_map/ppermute | solution.py:290
  132.2 17.9 %collective-permute-start.35 = (bf16[7,128,256]{2,1,0:T(8,128)(2,1)S(1)}, bf16[7,128,256]{2,1,0:T(8,128)(2,1)S(1)}, u32[]{:S(2)}, u32[]{:S(2)}) collective-permute-start(bf16[7,128,256]{2,1,0:T(8,128)(2,1)S(1)} %slice.72), channel_id=1, source_target_pairs={{0,1},{1,2},{2,3},{3,4},{4,5},{5,6},{6,7},{7,8},{8,9},{9,10},{10,1... | collective-permute-start | bytes 1376264 | tf_op jit(solution)/shard_map/ppermute | solution.py:289
  132.2 20.0 %collective-permute-start.36 = (bf16[7,128,256]{2,1,0:T(8,128)(2,1)S(1)}, bf16[7,128,256]{2,1,0:T(8,128)(2,1)S(1)}, u32[]{:S(2)}, u32[]{:S(2)}) collective-permute-start(bf16[7,128,256]{2,1,0:T(8,128)(2,1)S(1)} %slice.72), channel_id=1, source_target_pairs={{1,0},{2,1},{3,2},{4,3},{5,4},{6,5},{7,6},{8,7},{9,8},{10,9},{11,1... | collective-permute-start | bytes 1376264 | tf_op jit(solution)/shard_map/ppermute | solution.py:289
  141.8 21.3 %collective-permute-start.38 = (bf16[128,2048]{1,0:T(8,128)(2,1)}, bf16[128,2048]{1,0:T(8,128)(2,1)}, u32[]{:S(2)}, u32[]{:S(2)}) collective-permute-start(bf16[128,2048]{1,0:T(8,128)(2,1)} %get-tuple-element.11), channel_id=1, source_target_pairs={{64,0},{128,64},{192,128},{65,1},{129,65},{193,129},{66,2},{130,66... | collective-permute-start | bytes 1572872 | tf_op jit(solution)/shard_map/ppermute | solution.py:301
  157.7 11.9 %all-to-all-start = ((bf16[4,2,128,256]{3,2,1,0:T(8,128)(2,1)}), bf16[4,2,128,256]{3,2,1,0:T(8,128)(2,1)S(1)}, u32[]{:S(2)}, u32[]{:S(2)}) async-start(bf16[4,2,128,256]{3,2,1,0:T(8,128)(2,1)} %bitcast.31), calls=%async_computation | async-start | bytes 1048576 | tf_op jit(solution)/shard_map/all_to_all | solution.py:298
  169.7 1.6 copy-start.3
  (11 other events, 8.6 us)
Sparse Core Ops, SparseCore 0:
  15.8 81.0 all-gather.1

commit v2 on v1

v2 whole, which is shorter than its diff:
```python
import functools
import math

import jax
import jax.numpy as jnp
from jax import lax
from jax.experimental import pallas as pl
from jax.experimental.pallas import tpu as pltpu
from jax.sharding import Mesh, PartitionSpec as P

LEVELS = 1000
FRAMES = 8
F32 = jnp.float32
BF16 = jnp.bfloat16
AXES = ("yl", "core", "x", "yh", "z")
SIZES = (2, 2, 4, 2, 8)
SIZE = dict(zip(AXES, SIZES))
PLACES = (0, 3, 1, 2)
VMEM_LIMIT = 20 * 1024 * 1024


def embed(levels, freq_count):
    half = freq_count // 2
    freqs = jnp.exp(-math.log(10000.0) * jnp.arange(half, dtype=F32) / half)
    angles = levels.astype(F32)[:, None] * freqs[None, :]
    return jnp.concatenate([jnp.cos(angles), jnp.sin(angles)], axis=1).astype(BF16)


def alpha_bar(steps):
    frac = steps.astype(F32) / LEVELS
    return jnp.cos((frac + 0.008) / 1.008 * (math.pi / 2)) ** 2


def swap(array, axis):
    return lax.ppermute(array, axis, [(0, 1), (1, 0)])


def shift(array, axis, by):
    n = SIZE[axis]
    return lax.ppermute(array, axis, [(i, (i + by) % n) for i in range(n)])


def after(array, *others):
    return lax.optimization_barrier((array, *others))[0]


def gather(array, axis):
    copies = lax.optimization_barrier(jnp.broadcast_to(array[None], (SIZE[axis], *array.shape)))
    return lax.all_to_all(copies, axis, 0, 0)


def call(body, out_shape, scalars, far, near=(), scratch=()):
    specs = [pl.BlockSpec(memory_space=pltpu.SMEM)] * len(scalars)
    specs += [pl.BlockSpec(memory_space=pltpu.HBM)] * len(far)
    specs += [pl.BlockSpec(memory_space=pltpu.VMEM)] * len(near)
    return pl.pallas_call(
        body,
        out_shape=out_shape,
        in_specs=specs,
        out_specs=jax.tree.map(lambda _: pl.BlockSpec(memory_space=pltpu.VMEM), out_shape),
        scratch_shapes=list(scratch),
        compiler_params=pltpu.CompilerParams(vmem_limit_bytes=VMEM_LIMIT),
        cost_estimate=pl.CostEstimate(flops=0, bytes_accessed=0, transcendentals=0),
    )(*scalars, *far, *near)


def norm_kernel(x_ref, shift_ref, scale_ref, out_ref, copy_ref):
    copy_ref[...] = x_ref[0]
    frames, rows, width = x_ref.shape
    chunk = 32
    for f in range(frames):
        shift = shift_ref[f][None]
        scale = 1.0 + scale_ref[f][None]

        @pl.loop(0, rows // chunk)
        def _(step):
            at = pl.ds(pl.multiple_of(step * chunk, chunk), chunk)
            x = x_ref[f, at, :].astype(F32)
            mean = jnp.mean(x, axis=-1, keepdims=True)
            x = x - mean
            var = jnp.mean(x * x, axis=-1, keepdims=True)
            out_ref[f, at, :] = (x * lax.rsqrt(var + 1e-06) * scale + shift).astype(BF16)


def norm_rows(x, shift, scale):
    shapes = [jax.ShapeDtypeStruct(x.shape, BF16), jax.ShapeDtypeStruct(x.shape[1:], BF16)]
    return call(norm_kernel, shapes, (), (), (x, shift, scale))


def project_kernel(ids, gains, *refs):
    *pieces, late, x0, x1, x2, x3, first_ref, out_ref, q_ref, w_ref, x_ref, sems = refs
    copies = [(ref, x_ref.at[pl.ds(ids[4 + group], 2)]) for group, ref in enumerate((x0, x1, x2, x3))]
    for place, by in enumerate(PLACES):
        x = lax.rem(ids[3] + by, 4)
        for yh in range(2):
            copies.append((pieces[place].at[:, yh, :32], w_ref.at[0, x, yh]))
            copies.append((pieces[place].at[:, yh, 32:], w_ref.at[1, x, yh]))
            copies.append((late.at[:, place, yh, :32], w_ref.at[2, x, yh]))
    copies = [pltpu.make_async_copy(a, b, sems.at[i]) for i, (a, b) in enumerate(copies)]
    for copy in copies:
        copy.start()
    for copy in copies:
        copy.wait()
    for part in range(3):
        weight = w_ref[part].reshape(2048, 256)
        for f in range(0, FRAMES, 4):
            rows = x_ref[f : f + 4].reshape(512, 2048)
            got = jnp.dot(rows, weight, preferred_element_type=F32)
            if part != 1:
                heads = []
                for h in range(2):
                    one = got[:, h * 128 : (h + 1) * 128]
                    one = one * lax.rsqrt(jnp.mean(one * one, axis=-1, keepdims=True) + 1e-06)
                    heads.append(one * gains[h] if part == 2 else one)
                got = jnp.concatenate(heads, axis=1)
            got = got.astype(BF16)
            if part < 2 and f == 0:
                first_ref[part] = got[:128]
                out_ref[:3, part] = got[128:].reshape(3, 128, 256)
            elif part < 2:
                out_ref[3:, part] = got.reshape(4, 128, 256)
            else:
                q_ref[f : f + 4] = got.reshape(4, 128, 256)


def project(ids, gains, pieces, late, xs):
    return call(
        project_kernel,
        [
            jax.ShapeDtypeStruct((2, 128, 256), BF16),
            jax.ShapeDtypeStruct((FRAMES - 1, 2, 128, 256), BF16),
            jax.ShapeDtypeStruct((FRAMES, 128, 256), BF16),
        ],
        (ids, gains),
        (*pieces, late, *xs),
        scratch=[
            pltpu.VMEM((3, 4, 2, 8, 32, 256), BF16),
            pltpu.VMEM((FRAMES, 128, 2048), BF16),
            pltpu.SemaphoreType.DMA((28,)),
        ],
    )


def attend_kernel(q_ref, first_ref, kv_ref, left_ref, right_ref, out_ref):
    inv = 1.0 / math.sqrt(128)
    rr = lax.broadcasted_iota(jnp.int32, (128, 128), 0)
    kk = lax.broadcasted_iota(jnp.int32, (128, 128), 1)
    in_left = kk >= rr
    in_right = kk <= rr
    nt = (((1,), (1,)), ((), ()))

    def frame(g, part, lanes):
        return (first_ref[part, :, lanes] if g == 0 else kv_ref[g - 1, part, :, lanes]).astype(F32)

    for f in range(1, FRAMES):
        for h in range(2):
            lanes = slice(h * 128, (h + 1) * 128)
            q = q_ref[f, :, lanes]
            left, mid, right = (
                lax.dot_general(q, ref[f - 1, 0, :, lanes], nt, preferred_element_type=F32) * inv
                for ref in (left_ref, kv_ref, right_ref)
            )
            left = jnp.where(in_left, left, -1e30)
            right = jnp.where(in_right, right, -1e30)
            q32 = q.astype(F32)
            earlier = [
                jnp.sum(q32 * frame(g, 0, lanes), axis=-1, keepdims=True) * inv for g in range(f)
            ]
            top = jnp.max(jnp.maximum(jnp.maximum(left, mid), right), axis=-1, keepdims=True)
            for score in earlier:
                top = jnp.maximum(top, score)
            left = jnp.where(in_left, jnp.exp(left - top), 0.0)
            mid = jnp.exp(mid - top)
            right = jnp.where(in_right, jnp.exp(right - top), 0.0)
            total = jnp.sum(left + mid + right, axis=-1, keepdims=True)
            acc = None
            for p, ref in ((left, left_ref), (mid, kv_ref), (right, right_ref)):
                term = jnp.dot(p.astype(BF16), ref[f - 1, 1, :, lanes], preferred_element_type=F32)
                acc = term if acc is None else acc + term
            for g, score in enumerate(earlier):
                p = jnp.exp(score - top)
                total += p
                acc += p.astype(BF16).astype(F32) * frame(g, 1, lanes)
            out_ref[f - 1, :, lanes] = (acc / total).astype(BF16)
    out_ref[FRAMES - 1] = jnp.zeros_like(out_ref[FRAMES - 1])


def finish_kernel(ids, coefs, wa_hbm, wb_hbm, x0_hbm, x1_hbm, fresh_hbm, o_ref, out_ref, w_ref, x_ref, sems, x_sems):
    c, last = ids[0], ids[8]
    copies = {}
    for which, hbm in enumerate((wa_hbm, wb_hbm)):
        for place in range(4):
            copies[which, place] = pltpu.make_async_copy(
                hbm.at[:, place, :, 32:96], w_ref.at[which, place], sems.at[which, place]
            )
            copies[which, place].start()
        if which == 0:
            rows = [
                pltpu.make_async_copy(hbm, x_ref.at[i], x_sems.at[i])
                for i, hbm in enumerate((x0_hbm.at[1], x1_hbm, fresh_hbm))
            ]
            for copy in rows:
                copy.start()
    for which in range(2):
        side = c if which == 0 else 1 - c
        eps = [None] * 4
        for place, by in enumerate(PLACES):
            copies[which, place].wait()
            o = o_ref[pl.ds(lax.rem(ids[3] + by, 4), 1)].reshape(256, 256)
            for part in range(4):
                weight = jnp.concatenate(
                    [
                        w_ref[which, place, :, yh, 16 * part : 16 * part + 16].reshape(128, 256)
                        for yh in range(2)
                    ],
                    axis=0,
                )
                term = jnp.dot(o, weight, preferred_element_type=F32)
                eps[part] = term if place == 0 else eps[part] + term
        if which == 0:
            for copy in rows:
                copy.wait()
        for part in range(4):
            columns = pl.ds(pl.multiple_of(side * 1024 + part * 256, 256), 256)
            for slot in range(2):
                x = x_ref[slot, :, columns].astype(F32)
                e = x + eps[part][slot * 128 : (slot + 1) * 128]
                done = coefs[4 * slot] * ((x - coefs[4 * slot + 1] * e) * coefs[4 * slot + 2])
                done = (done + coefs[4 * slot + 3] * e).astype(BF16)
                if slot == 1:
                    done = jnp.where(last == 1, x_ref[2, :, columns], done)
                out_ref[slot, :, columns] = done


def body(frames_in, levels, fresh, w_mod, w_qkv, q_gain, w_out):
    width = frames_in.shape[2]
    yl, c = lax.axis_index("yl"), lax.axis_index("core")
    xi, yhi, zi = lax.axis_index("x"), lax.axis_index("yh"), lax.axis_index("z")
    me = 2 * yl + c
    groups = (me, 2 * yl + 1 - c, 2 * (1 - yl) + c, 2 * (1 - yl) + 1 - c)
    ids = jnp.stack(
        [c, 1 - 2 * c, zi, xi, *(2 * g for g in groups), (me == 3).astype(jnp.int32)]
    ).astype(jnp.int32)
    gains = lax.dynamic_slice(q_gain, (2 * me,), (2,))

    columns = [lax.dynamic_slice(w_qkv, (0, 1024 * part + 256 * me), (32, 256)) for part in (1, 2, 0)]
    half = lax.dynamic_slice(w_out, (0, 1024 * c), (16, 1024))
    half = half.reshape(16, 4, 256).transpose(1, 0, 2).reshape(64, 256)
    pack = jnp.concatenate([*columns, half], axis=0)
    back = [(i + 1, i) for i in range(3)]
    next_level = lax.ppermute(levels[:1], ("yl", "core"), back)
    other = swap(pack, "yh")
    pair = jnp.stack([jnp.where(yhi == 0, pack, other), jnp.where(yhi == 0, other, pack)])

    mod = jnp.dot(embed(levels, w_mod.shape[0]), w_mod, preferred_element_type=F32)
    own, first_x = norm_rows(frames_in, mod[:, :width], mod[:, width:])
    pair, own, next_level = lax.optimization_barrier((pair, own, next_level))
    across = swap(own, "yl")
    beside = swap(own, "core")

    def along_x(block):
        return block, shift(block, "x", 1), shift(block, "x", -1), shift(block, "x", 2)

    late = along_x(pair[:, 64:])
    block = gather(pair[:, :64], "z")
    late = lax.all_gather(jnp.stack(late), "z", axis=0)
    block, across, beside = lax.optimization_barrier((block, across, beside))
    pieces = along_x(block)
    diagonal = swap(across, "core")
    next_x = lax.ppermute(after(first_x, block), ("yl", "core"), back)
    diagonal, next_x, *pieces = lax.optimization_barrier((diagonal, next_x, *pieces))
    xs = (own, beside, across, diagonal)

    line = ("x", "yh", "z")
    right = [(i, (i + 1) % 64) for i in range(64)]
    left = [((i + 1) % 64, i) for i in range(64)]
    first, here, queries = project(ids, gains, pieces, late, xs)
    from_left, from_right = lax.ppermute(here, line, right), lax.ppermute(here, line, left)

    mine = call(
        attend_kernel,
        jax.ShapeDtypeStruct((FRAMES, 128, 256), BF16),
        (),
        (),
        (queries, first, here, from_left, from_right),
    )
    o = lax.all_to_all(mine.reshape(4, 2, 128, 256), ("yl", "core"), 0, 0)

    now = jnp.concatenate([levels[1:], next_level])
    a_now = alpha_bar(now)
    a_later = alpha_bar(jnp.maximum(now - LEVELS // FRAMES, 0))
    coefs = jnp.stack(
        [jnp.sqrt(a_later), jnp.sqrt(1.0 - a_now), 1.0 / jnp.sqrt(a_now), jnp.sqrt(1.0 - a_later)],
        axis=1,
    ).reshape(8)
    return call(
        finish_kernel,
        jax.ShapeDtypeStruct(frames_in.shape, BF16),
        (ids, coefs),
        (late, swap(after(late, mine), "core"), frames_in, next_x, fresh),
        (o,),
        scratch=[
            pltpu.VMEM((2, 4, 8, 2, 64, 256), BF16),
            pltpu.VMEM((3, 128, 2048), BF16),
            pltpu.SemaphoreType.DMA((2, 4)),
            pltpu.SemaphoreType.DMA((3,)),
        ],
    )


def solution(mesh):
    cut = Mesh(mesh.devices.reshape(SIZES), AXES)
    frame, space = ("yl", "core"), ("x", "yh", "z")
    return jax.shard_map(
        body,
        mesh=cut,
        in_specs=(
            P(frame, space, None),
            P(frame),
            P(space, None),
            P(),
            P(space, None),
            P(),
            P(space, None),
        ),
        out_specs=P(frame, space, None),
        check_vma=False,
    )
```

time: 185 us -> 167 us (0.903)
  starting transfers between devices: 74.6 us -> 25.2 us
  blocking collectives: 0 us -> 29.8 us
  waiting for transfers between devices: 40.5 us -> 63.9 us
  local copies, waits for them, and re-layouts: 26.8 us -> 10.4 us
  Pallas kernels: 25.5 us -> 19.3 us
    ppermute x19 -> x9, waiting for transfers between devices: 11.9 us -> 57.2 us  [the longest x6 23.8 us: shift(): return lax.ppermute(array, axis, [(i, (i + by) % n) for i in range(n)])]
    ppermute x19 -> x9, starting transfers between devices: 39.3 us -> 9.36 us  [the longest x6 5.92 us: shift(): return lax.ppermute(array, axis, [(i, (i + by) % n) for i in range(n)])]
    all_to_all x0 -> x1, blocking collectives: none -> 29.8 us  [gather(): return lax.all_to_all(copies, axis, 0, 0)]
    ppermute x19 -> x5, starting transfers between devices: 28.9 us -> 6.57 us  [swap(): return lax.ppermute(array, axis, [(0, 1), (1, 0)])]
    all_gather x1, waiting for transfers between devices: 17.8 us -> 0.01 us  [body(): late = lax.all_gather(jnp.stack(late), 'z', axis=0)]
    squeeze x13 -> x0, local copies, waits for them, and re-layouts: 10.7 us -> none  [the longest x12 9.64 us: pick(): return lax.dynamic_index_in_dim(array, index, axis, keepdims=False)]
    pallas_call x8 -> x4, Pallas kernels: 25.5 us -> 19.3 us  [call(): pl.pallas_call(body, out_shape=out_shape, in_specs=specs, out_specs=jax.t...]
    unnamed x37 -> x20, local copies, waits for them, and re-layouts: 11.4 us -> 7.04 us
  transfers between devices with their start and end apart: 41 -> 17, of which waited for: 12 -> 9; matrix products, arithmetic and copies ran while one was open for 9% -> 3% of each run, Pallas kernels for 11% -> 1%
where the time goes in v2:
time: 167 us
  waiting for transfers between devices  63.9 us (38%)
  blocking collectives  29.8 us (18%)
  starting transfers between devices  25.2 us (15%)
  Pallas kernels  19.3 us (12%)
  between operations  13.6 us (8%)
  local copies, waits for them, and re-layouts  10.4 us (6%)
  other arithmetic  4.26 us (3%)
    all_to_all x1, blocking collectives, gather(): return lax.all_to_all(copies, axis, 0, 0)  29.8 us
    ppermute x6, waiting for transfers between devices, shift(): return lax.ppermute(array, axis, [(i, (i + by) % n) for i in range(n)])  23.8 us
    ppermute x1, waiting for transfers between devices, body(): lax.ppermute(here, line, left)  20.1 us
    pallas_call x4, Pallas kernels, call(): pl.pallas_call(body, out_shape=out_shape, in_specs=specs, out_specs=jax.t...  19.3 us
    ppermute x1, waiting for transfers between devices, body(): next_x = lax.ppermute(after(first_x, block), ('yl', 'core'), back)  7.37 us
    unnamed x20, local copies, waits for them, and re-layouts  7.04 us
    all_to_all x1, waiting for transfers between devices, body(): o = lax.all_to_all(mine.reshape(4, 2, 128, 256), ('yl', 'core'), 0, 0)  6.6 us
    ppermute x5, starting transfers between devices, swap(): return lax.ppermute(array, axis, [(0, 1), (1, 0)])  6.57 us
  transfers between devices with their start and end apart: 17, of which 9 were waited for; matrix products, arithmetic and copies ran while one was open for 3% of the time, Pallas kernels for 1%

profile of v2, /device:TPU:1, one launch (start us, length us, event | category | flops | bytes accessed | tf_op | source)
XLA Modules:
  0.0 166.7 jit_solution(6326503615937944285)
XLA Ops:
  6.5 1.5 fusion.10
  8.0 5.1 %collective-permute-start.1 = (s32[1]{0:T(128)}, s32[1]{0:T(128)}, u32[]{:S(2)}, u32[]{:S(2)}) collective-permute-start(s32[1]{0:T(128)} %get-tuple-element.57), channel_id=1, source_target_pairs={{64,0},{128,64},{192,128},{65,1},{129,65},{193,129},{66,2},{130,66... | collective-permute-start | bytes 20 | tf_op jit(solution)/shard_map/ppermute | solution.py:251
  13.2 0.8 constant_dynamic-slice_fusion
  14.0 0.8 constant_dynamic-slice_fusion.3
  14.8 1.3 collective-permute-start
  16.0 0.7 convert_element_type.33
  16.7 0.1 fusion
  16.8 0.4 fusion.2
  17.2 2.0 %shard_map.73 = (bf16[2,128,2048]{2,1,0:T(8,128)(2,1)S(1)}, bf16[128,2048]{1,0:T(8,128)(2,1)S(1)}) custom-call(bf16[2,128,2048]{2,1,0:T(8,128)(2,1)S(1)} %copy-done.1, f32[2,2048]{1,0:T(2,128)S(1)} %get-tuple-element.53.shift_ref, f32[2,2048]{1,0:T(2,128)S(1)} %get-tuple-element.52.scale_ref), custom_call_target="tpu_custom_call" | custom-call | tf_op jit(solution)/shard_map/pallas_call | solution.py:56
  19.2 1.0 copy-done.3
  20.1 0.8 copy-done.8
  21.0 2.6 %collective-permute-start.3 = (bf16[2,96,256]{2,1,0:T(8,128)(2,1)S(1)}, bf16[2,96,256]{2,1,0:T(8,128)(2,1)S(1)}, u32[]{:S(2)}, u32[]{:S(2)}) collective-permute-start(bf16[2,96,256]{2,1,0:T(8,128)(2,1)S(1)} %get-tuple-element.49), channel_id=1, source_target_pairs={{0,48},{16,0},{32,16},{48,32},{1,49},{17,1},{33,17},{49,33},{2,50}... | collective-permute-start | bytes 294920 | tf_op jit(solution)/shard_map/ppermute | solution.py:40
  23.6 1.7 %collective-permute-start.4 = (bf16[2,96,256]{2,1,0:T(8,128)(2,1)S(1)}, bf16[2,96,256]{2,1,0:T(8,128)(2,1)S(1)}, u32[]{:S(2)}, u32[]{:S(2)}) collective-permute-start(bf16[2,96,256]{2,1,0:T(8,128)(2,1)S(1)} %get-tuple-element.49), channel_id=1, source_target_pairs={{0,32},{16,48},{32,0},{48,16},{1,33},{17,49},{33,1},{49,17},{2,34}... | collective-permute-start | bytes 294920 | tf_op jit(solution)/shard_map/ppermute | solution.py:40
  25.3 0.8 collective-permute-done.3
  26.1 5.3 %collective-permute-done.2 = bf16[2,96,256]{2,1,0:T(8,128)(2,1)S(1)} collective-permute-done((bf16[2,96,256]{2,1,0:T(8,128)(2,1)S(1)}, bf16[2,96,256]{2,1,0:T(8,128)(2,1)S(1)}, u32[]{:S(2)}, u32[]{:S(2)}) %collective-permute-start.2) | collective-permute-done | bytes 98336 | tf_op jit(solution)/shard_map/ppermute | solution.py:40
  31.4 0.8 pad_maximum_fusion
  32.2 0.8 collective-permute-start.6
  33.0 0.9 collective-permute-start.5
  34.0 29.8 %all_to_all.10.refs_0_ = bf16[8,2,64,256]{3,2,1,0:T(8,128)(2,1)} all-to-all(bf16[8,2,64,256]{3,2,1,0:T(8,128)(2,1)S(1)} %broadcast_in_dim.2), channel_id=1, replica_groups=mesh['yl'=2,'core'=2,'x'=4,'yh'=2,'z'=8] {'z'}, dimensions={0} | all-to-all | bytes 1048576 | tf_op jit(solution)/shard_map/all_to_all | solution.py:49
  63.7 1.0 copy-done.5
  64.7 2.4 %collective-permute-start.7 = (bf16[2,128,2048]{2,1,0:T(8,128)(2,1)}, bf16[2,128,2048]{2,1,0:T(8,128)(2,1)}, u32[]{:S(2)}, u32[]{:S(2)}) collective-permute-start(bf16[2,128,2048]{2,1,0:T(8,128)(2,1)} %collective-permute-done.5.refs_7_), channel_id=1, source_target_pairs={{0,64},{64,0},{1,65},{65,1},{2,66},{66,2},{3,67},{67,3},{4,68},{68... | collective-permute-start | bytes 3145736 | tf_op jit(solution)/shard_map/ppermute | solution.py:35
  67.1 1.9 %collective-permute-start.8 = (bf16[128,2048]{1,0:T(8,128)(2,1)}, bf16[128,2048]{1,0:T(8,128)(2,1)}, u32[]{:S(2)}, u32[]{:S(2)}) collective-permute-start(bf16[128,2048]{1,0:T(8,128)(2,1)} %copy-done.8), channel_id=1, source_target_pairs={{64,0},{128,64},{192,128},{65,1},{129,65},{193,129},{66,2},{130,66... | collective-permute-start | bytes 1572872 | tf_op jit(solution)/shard_map/ppermute | solution.py:270
  69.0 0.1 collective-permute-start.11
  69.1 0.1 collective-permute-start.10
  69.2 1.5 collective-permute-start.9
  70.8 0.1 stack.74.ids
  70.8 7.4 %collective-permute-done.8.x1_hbm = bf16[128,2048]{1,0:T(8,128)(2,1)} collective-permute-done((bf16[128,2048]{1,0:T(8,128)(2,1)}, bf16[128,2048]{1,0:T(8,128)(2,1)}, u32[]{:S(2)}, u32[]{:S(2)}) %collective-permute-start.8) | collective-permute-done | bytes 524320 | tf_op jit(solution)/shard_map/ppermute | solution.py:270
  78.2 6.4 %collective-permute-done.11.refs_3_ = bf16[8,2,64,256]{3,2,1,0:T(8,128)(2,1)} collective-permute-done((bf16[8,2,64,256]{3,2,1,0:T(8,128)(2,1)}, bf16[8,2,64,256]{3,2,1,0:T(8,128)(2,1)}, u32[]{:S(2)}, u32[]{:S(2)}) %collective-permute-start.11) | collective-permute-done | bytes 524320 | tf_op jit(solution)/shard_map/ppermute | solution.py:40
  84.6 8.9 %collective-permute-done.10.refs_2_ = bf16[8,2,64,256]{3,2,1,0:T(8,128)(2,1)} collective-permute-done((bf16[8,2,64,256]{3,2,1,0:T(8,128)(2,1)}, bf16[8,2,64,256]{3,2,1,0:T(8,128)(2,1)}, u32[]{:S(2)}, u32[]{:S(2)}) %collective-permute-start.10) | collective-permute-done | bytes 524320 | tf_op jit(solution)/shard_map/ppermute | solution.py:40
  93.6 2.4 %collective-permute-done.9.refs_1_ = bf16[8,2,64,256]{3,2,1,0:T(8,128)(2,1)} collective-permute-done((bf16[8,2,64,256]{3,2,1,0:T(8,128)(2,1)}, bf16[8,2,64,256]{3,2,1,0:T(8,128)(2,1)}, u32[]{:S(2)}, u32[]{:S(2)}) %collective-permute-start.9) | collective-permute-done | bytes 524320 | tf_op jit(solution)/shard_map/ppermute | solution.py:40
  96.0 1.2 copy-done.4
  97.2 1.2 copy-done.6
  98.4 7.1 %shard_map.74 = (bf16[2,128,256]{2,1,0:T(8,128)(2,1)S(1)}, bf16[7,2,128,256]{3,2,1,0:T(8,128)(2,1)S(1)}, bf16[8,128,256]{2,1,0:T(8,128)(2,1)S(1)}) custom-call(s32[9]{0:T(128)S(1)} %stack.74.ids, f32[2]{0:T(128)S(1)} %dynamic_slice.19.gains, bf16[8,2,64,256]{3,2,1,0:T(8,128)(2,1)} %all_to_all.10.refs_0_, ...), custom_call_target="tpu_custom_call" | custom-call | tf_op jit(solution)/shard_map/pallas_call | solution.py:56
  105.5 0.1 collective-permute-start.13
  105.6 1.5 collective-permute-start.12
  107.1 20.1 %collective-permute-done.13.right_ref = bf16[7,2,128,256]{3,2,1,0:T(8,128)(2,1)S(1)} collective-permute-done((bf16[7,2,128,256]{3,2,1,0:T(8,128)(2,1)S(1)}, bf16[7,2,128,256]{3,2,1,0:T(8,128)(2,1)S(1)}, u32[]{:S(2)}, u32[]{:S(2)}) %collective-permute-start.13) | collective-permute-done | bytes 917536 | tf_op jit(solution)/shard_map/ppermute | solution.py:278
  127.2 6.0 %collective-permute-done.12.left_ref = bf16[7,2,128,256]{3,2,1,0:T(8,128)(2,1)S(1)} collective-permute-done((bf16[7,2,128,256]{3,2,1,0:T(8,128)(2,1)S(1)}, bf16[7,2,128,256]{3,2,1,0:T(8,128)(2,1)S(1)}, u32[]{:S(2)}, u32[]{:S(2)}) %collective-permute-start.12) | collective-permute-done | bytes 917536 | tf_op jit(solution)/shard_map/ppermute | solution.py:278
  133.1 4.7 %shard_map.75 = bf16[8,128,256]{2,1,0:T(8,128)(2,1)S(1)} custom-call(bf16[8,128,256]{2,1,0:T(8,128)(2,1)S(1)} %get-tuple-element.38.q_ref, bf16[2,128,256]{2,1,0:T(8,128)(2,1)S(1)} %get-tuple-element.39.first_ref, bf16[7,2,128,256]{3,2,1,0:T(8,128)(2,1)S(1)} %get-tuple-element.40.kv_ref, bf16[7,2,128,256]{3,2,1,0:T(8,128)(2,1)S(1)} %collective-permute-done.12.left_ref, ...), custom_call_target="tpu_custom_call" | custom-call | tf_op jit(solution)/shard_map/pallas_call | solution.py:56
  137.9 0.8 copy-done.2
  138.6 1.2 collective-permute-start.14
  139.9 1.3 subtract_sqrt_fusion.1
  141.2 4.1 %all-to-all-start.1 = ((bf16[4,2,128,256]{3,2,1,0:T(8,128)(2,1)}), bf16[4,2,128,256]{3,2,1,0:T(8,128)(2,1)}, u32[]{:S(2)}, u32[]{:S(2)}) async-start(bf16[4,2,128,256]{3,2,1,0:T(8,128)(2,1)} %bitcast.25), calls=%async_computation.1 | async-start | bytes 1048576 | tf_op jit(solution)/shard_map/all_to_all | solution.py:287
  145.3 1.3 fusion.8
  146.6 0.1 pad_maximum_fusion.3
  146.7 0.1 reshape.149.coefs
  146.7 6.6 %all-to-all-done.1.o_ref = bf16[4,2,128,256]{3,2,1,0:T(8,128)(2,1)} async-done(((bf16[4,2,128,256]{3,2,1,0:T(8,128)(2,1)}), bf16[4,2,128,256]{3,2,1,0:T(8,128)(2,1)}, u32[]{:S(2)}, u32[]{:S(2)}) %all-to-all-start.1) | async-done | bytes 524320 | tf_op jit(solution)/shard_map/all_to_all | solution.py:287
  153.3 1.0 copy-done.7
  154.4 5.5 %shard_map.76 = bf16[2,128,2048]{2,1,0:T(8,128)(2,1)} custom-call(s32[9]{0:T(128)S(1)} %stack.74.ids, f32[8]{0:T(128)S(1)} %reshape.149.coefs, bf16[8,4,2,96,256]{4,3,2,1,0:T(8,128)(2,1)} %bitcast.19.refs_4_.wa_hbm, bf16[8,4,2,96,256]{4,3,2,1,0:T(8,128)(2,1)} %collective-permute-done.14.wb_hbm, bf16[2,128,2048]{2,1,0:T(8,128)(2,1)S(1)} %copy-done.1, ...), custom_call_target="tpu_custom_call" | custom-call | tf_op jit(solution)/shard_map/pallas_call | solution.py:56
  (36 shorter events, 0.3 us)
Async XLA Ops:
  6.5 10.3 %copy-start = (bf16[256,4096]{1,0:T(8,128)(2,1)S(1)}, bf16[256,4096]{1,0:T(8,128)(2,1)}, u32[]{:S(2)}) copy-start(bf16[256,4096]{1,0:T(8,128)(2,1)} %param.10) | copy-start | bytes 6291460
  6.5 10.7 %copy-start.1 = (bf16[2,128,2048]{2,1,0:T(8,128)(2,1)S(1)}, bf16[2,128,2048]{2,1,0:T(8,128)(2,1)}, u32[]{:S(2)}) copy-start(bf16[2,128,2048]{2,1,0:T(8,128)(2,1)} %x0_hbm.1) | copy-start | bytes 3145732
  6.5 89.4 %all-gather.3.cloned.1.call-start = ((), (), s32[]{:S(2)}) async-start(), calls=%async_computation.2 | async-start | bytes 3538944 | tf_op jit(solution)/shard_map/all_gather | solution.py:266
  8.0 13.0 %collective-permute-start.1 = (s32[1]{0:T(128)}, s32[1]{0:T(128)}, u32[]{:S(2)}, u32[]{:S(2)}) collective-permute-start(s32[1]{0:T(128)} %get-tuple-element.57), channel_id=1, source_target_pairs={{64,0},{128,64},{192,128},{65,1},{129,65},{193,129},{66,2},{130,66... | collective-permute-start | bytes 20 | tf_op jit(solution)/shard_map/ppermute | solution.py:251
  14.8 6.2 %collective-permute-start = (bf16[160,256]{1,0:T(8,128)(2,1)S(1)}, bf16[160,256]{1,0:T(8,128)(2,1)S(1)}, u32[]{:S(2)}, u32[]{:S(2)}) collective-permute-start(bf16[160,256]{1,0:T(8,128)(2,1)S(1)} %pad_maximum_fusion.2), channel_id=1, source_target_pairs={{0,8},{8,0},{1,9},{9,1},{2,10},{10,2},{3,11},{11,3},{4,12},{12,4},... | collective-permute-start | bytes 245768 | tf_op jit(solution)/shard_map/ppermute | solution.py:35
  19.2 1.0 copy-start.3
  20.1 0.8 copy-start.8
  20.9 49.8 %copy-start.9 = (f32[8]{0:T(128)S(1)}, f32[8]{0:T(128)}, u32[]{:S(2)}) copy-start(f32[8]{0:T(128)} %param.12) | copy-start | bytes 100
  21.0 5.0 %collective-permute-start.3 = (bf16[2,96,256]{2,1,0:T(8,128)(2,1)S(1)}, bf16[2,96,256]{2,1,0:T(8,128)(2,1)S(1)}, u32[]{:S(2)}, u32[]{:S(2)}) collective-permute-start(bf16[2,96,256]{2,1,0:T(8,128)(2,1)S(1)} %get-tuple-element.49), channel_id=1, source_target_pairs={{0,48},{16,0},{32,16},{48,32},{1,49},{17,1},{33,17},{49,33},{2,50}... | collective-permute-start | bytes 294920 | tf_op jit(solution)/shard_map/ppermute | solution.py:40
  23.6 7.8 %collective-permute-start.2 = (bf16[2,96,256]{2,1,0:T(8,128)(2,1)S(1)}, bf16[2,96,256]{2,1,0:T(8,128)(2,1)S(1)}, u32[]{:S(2)}, u32[]{:S(2)}) collective-permute-start(bf16[2,96,256]{2,1,0:T(8,128)(2,1)S(1)} %get-tuple-element.49), channel_id=1, source_target_pairs={{0,16},{16,32},{32,48},{48,0},{1,17},{17,33},{33,49},{49,1},{2,18}... | collective-permute-start | bytes 294920 | tf_op jit(solution)/shard_map/ppermute | solution.py:40
  23.6 7.8 %collective-permute-start.4 = (bf16[2,96,256]{2,1,0:T(8,128)(2,1)S(1)}, bf16[2,96,256]{2,1,0:T(8,128)(2,1)S(1)}, u32[]{:S(2)}, u32[]{:S(2)}) collective-permute-start(bf16[2,96,256]{2,1,0:T(8,128)(2,1)S(1)} %get-tuple-element.49), channel_id=1, source_target_pairs={{0,32},{16,48},{32,0},{48,16},{1,33},{17,49},{33,1},{49,17},{2,34}... | collective-permute-start | bytes 294920 | tf_op jit(solution)/shard_map/ppermute | solution.py:40
  32.2 31.5 %collective-permute-start.6 = (bf16[2,128,2048]{2,1,0:T(8,128)(2,1)}, bf16[2,128,2048]{2,1,0:T(8,128)(2,1)S(1)}, u32[]{:S(2)}, u32[]{:S(2)}) collective-permute-start(bf16[2,128,2048]{2,1,0:T(8,128)(2,1)} %copy-done.3), channel_id=1, source_target_pairs={{0,64},{64,0},{1,65},{65,1},{2,66},{66,2},{3,67},{67,3},{4,68},{68... | collective-permute-start | bytes 3145736 | tf_op jit(solution)/shard_map/ppermute | solution.py:35
  33.0 31.7 %collective-permute-start.5 = (bf16[2,128,2048]{2,1,0:T(8,128)(2,1)}, bf16[2,128,2048]{2,1,0:T(8,128)(2,1)}, u32[]{:S(2)}, u32[]{:S(2)}) collective-permute-start(bf16[2,128,2048]{2,1,0:T(8,128)(2,1)} %copy-done.3), channel_id=1, source_target_pairs={{0,128},{128,0},{1,129},{129,1},{2,130},{130,2},{3,131},{131,3},{4... | collective-permute-start | bytes 3145736 | tf_op jit(solution)/shard_map/ppermute | solution.py:35
  63.7 1.0 copy-start.5
  64.7 31.2 %collective-permute-start.7 = (bf16[2,128,2048]{2,1,0:T(8,128)(2,1)}, bf16[2,128,2048]{2,1,0:T(8,128)(2,1)}, u32[]{:S(2)}, u32[]{:S(2)}) collective-permute-start(bf16[2,128,2048]{2,1,0:T(8,128)(2,1)} %collective-permute-done.5.refs_7_), channel_id=1, source_target_pairs={{0,64},{64,0},{1,65},{65,1},{2,66},{66,2},{3,67},{67,3},{4,68},{68... | collective-permute-start | bytes 3145736 | tf_op jit(solution)/shard_map/ppermute | solution.py:35
  67.1 11.1 %collective-permute-start.8 = (bf16[128,2048]{1,0:T(8,128)(2,1)}, bf16[128,2048]{1,0:T(8,128)(2,1)}, u32[]{:S(2)}, u32[]{:S(2)}) collective-permute-start(bf16[128,2048]{1,0:T(8,128)(2,1)} %copy-done.8), channel_id=1, source_target_pairs={{64,0},{128,64},{192,128},{65,1},{129,65},{193,129},{66,2},{130,66... | collective-permute-start | bytes 1572872 | tf_op jit(solution)/shard_map/ppermute | solution.py:270
  69.0 15.6 %collective-permute-start.11 = (bf16[8,2,64,256]{3,2,1,0:T(8,128)(2,1)}, bf16[8,2,64,256]{3,2,1,0:T(8,128)(2,1)}, u32[]{:S(2)}, u32[]{:S(2)}) collective-permute-start(bf16[8,2,64,256]{3,2,1,0:T(8,128)(2,1)} %all_to_all.10.refs_0_), channel_id=1, source_target_pairs={{0,32},{16,48},{32,0},{48,16},{1,33},{17,49},{33,1},{49,17},{2,34}... | collective-permute-start | bytes 1572872 | tf_op jit(solution)/shard_map/ppermute | solution.py:40
  69.1 24.4 %collective-permute-start.10 = (bf16[8,2,64,256]{3,2,1,0:T(8,128)(2,1)}, bf16[8,2,64,256]{3,2,1,0:T(8,128)(2,1)}, u32[]{:S(2)}, u32[]{:S(2)}) collective-permute-start(bf16[8,2,64,256]{3,2,1,0:T(8,128)(2,1)} %all_to_all.10.refs_0_), channel_id=1, source_target_pairs={{0,48},{16,0},{32,16},{48,32},{1,49},{17,1},{33,17},{49,33},{2,50}... | collective-permute-start | bytes 1572872 | tf_op jit(solution)/shard_map/ppermute | solution.py:40
  69.2 26.7 %collective-permute-start.9 = (bf16[8,2,64,256]{3,2,1,0:T(8,128)(2,1)}, bf16[8,2,64,256]{3,2,1,0:T(8,128)(2,1)}, u32[]{:S(2)}, u32[]{:S(2)}) collective-permute-start(bf16[8,2,64,256]{3,2,1,0:T(8,128)(2,1)} %all_to_all.10.refs_0_), channel_id=1, source_target_pairs={{0,16},{16,32},{32,48},{48,0},{1,17},{17,33},{33,49},{49,1},{2,18}... | collective-permute-start | bytes 1572872 | tf_op jit(solution)/shard_map/ppermute | solution.py:40
  96.0 1.2 copy-start.4
  97.2 1.2 copy-start.6
  105.5 21.6 %collective-permute-start.13 = (bf16[7,2,128,256]{3,2,1,0:T(8,128)(2,1)S(1)}, bf16[7,2,128,256]{3,2,1,0:T(8,128)(2,1)S(1)}, u32[]{:S(2)}, u32[]{:S(2)}) collective-permute-start(bf16[7,2,128,256]{3,2,1,0:T(8,128)(2,1)S(1)} %get-tuple-element.40.kv_ref), channel_id=1, source_target_pairs={{1,0},{2,1},{3,2},{4,3},{5,4},{6,5},{7,6},{8,7},{9,8},{10,9},{11,1... | collective-permute-start | bytes 2752520 | tf_op jit(solution)/shard_map/ppermute | solution.py:278
  105.6 27.5 %collective-permute-start.12 = (bf16[7,2,128,256]{3,2,1,0:T(8,128)(2,1)S(1)}, bf16[7,2,128,256]{3,2,1,0:T(8,128)(2,1)S(1)}, u32[]{:S(2)}, u32[]{:S(2)}) collective-permute-start(bf16[7,2,128,256]{3,2,1,0:T(8,128)(2,1)S(1)} %get-tuple-element.40.kv_ref), channel_id=1, source_target_pairs={{0,1},{1,2},{2,3},{3,4},{4,5},{5,6},{6,7},{7,8},{8,9},{9,10},{10,1... | collective-permute-start | bytes 2752520 | tf_op jit(solution)/shard_map/ppermute | solution.py:278
  137.8 0.8 copy-start.2
  138.6 14.7 %collective-permute-start.14 = (bf16[8,4,2,96,256]{4,3,2,1,0:T(8,128)(2,1)}, bf16[8,4,2,96,256]{4,3,2,1,0:T(8,128)(2,1)}, u32[]{:S(2)}, u32[]{:S(2)}) collective-permute-start(bf16[8,4,2,96,256]{4,3,2,1,0:T(8,128)(2,1)} %bitcast.19.refs_4_.wa_hbm), channel_id=1, source_target_pairs={{0,64},{64,0},{1,65},{65,1},{2,66},{66,2},{3,67},{67,3},{4,68},{68... | collective-permute-start | bytes 9437192 | tf_op jit(solution)/shard_map/ppermute | solution.py:35
  141.2 12.2 %all-to-all-start.1 = ((bf16[4,2,128,256]{3,2,1,0:T(8,128)(2,1)}), bf16[4,2,128,256]{3,2,1,0:T(8,128)(2,1)}, u32[]{:S(2)}, u32[]{:S(2)}) async-start(bf16[4,2,128,256]{3,2,1,0:T(8,128)(2,1)} %bitcast.25), calls=%async_computation.1 | async-start | bytes 1048576 | tf_op jit(solution)/shard_map/all_to_all | solution.py:287
  153.3 1.0 copy-start.7
Sparse Core Ops, SparseCore 0:
  32.3 54.4 all-gather.2

commit v3 on v2

v3 whole, which is shorter than its diff:
```python
import functools
import math

import jax
import jax.numpy as jnp
from jax import lax
from jax.experimental import pallas as pl
from jax.experimental.pallas import tpu as pltpu
from jax.sharding import Mesh, PartitionSpec as P

LEVELS = 1000
FRAMES = 8
F32 = jnp.float32
BF16 = jnp.bfloat16
AXES = ("yl", "core", "x", "yh", "z")
SIZES = (2, 2, 4, 2, 8)
SIZE = dict(zip(AXES, SIZES))
NEAR_LIMIT = 20 * 1024 * 1024
FAR_LIMIT = 56 * 1024 * 1024


def embed(levels, freq_count):
    half = freq_count // 2
    freqs = jnp.exp(-math.log(10000.0) * jnp.arange(half, dtype=F32) / half)
    angles = levels.astype(F32)[:, None] * freqs[None, :]
    return jnp.concatenate([jnp.cos(angles), jnp.sin(angles)], axis=1).astype(BF16)


def alpha_bar(steps):
    frac = steps.astype(F32) / LEVELS
    return jnp.cos((frac + 0.008) / 1.008 * (math.pi / 2)) ** 2


def swap(array, axis):
    return lax.ppermute(array, axis, [(0, 1), (1, 0)])


def shift(array, axis, by):
    n = SIZE[axis]
    return lax.ppermute(array, axis, [(i, (i + by) % n) for i in range(n)])


def after(array, *others):
    return lax.optimization_barrier((array, *others))[0]


def gather(array, axis):
    size = math.prod(SIZE[a] for a in ((axis,) if isinstance(axis, str) else axis))
    copies = lax.optimization_barrier(jnp.broadcast_to(array[None], (size, *array.shape)))
    return lax.all_to_all(copies, axis, 0, 0)


def call(body, out_shape, scalars, far, near=(), scratch=()):
    limit = FAR_LIMIT if far else NEAR_LIMIT
    specs = [pl.BlockSpec(memory_space=pltpu.SMEM)] * len(scalars)
    specs += [pl.BlockSpec(memory_space=pl.ANY)] * len(far)
    specs += [pl.BlockSpec(memory_space=pltpu.VMEM)] * len(near)
    return pl.pallas_call(
        body,
        out_shape=out_shape,
        in_specs=specs,
        out_specs=jax.tree.map(lambda _: pl.BlockSpec(memory_space=pltpu.VMEM), out_shape),
        scratch_shapes=list(scratch),
        compiler_params=pltpu.CompilerParams(vmem_limit_bytes=limit),
        cost_estimate=pl.CostEstimate(flops=0, bytes_accessed=0, transcendentals=0),
    )(*scalars, *far, *near)


def norm_kernel(x_ref, shift_ref, scale_ref, out_ref, copy_ref):
    copy_ref[...] = x_ref[0]
    frames, rows, width = x_ref.shape
    chunk = 32
    for f in range(frames):
        shift = shift_ref[f][None]
        scale = 1.0 + scale_ref[f][None]

        @pl.loop(0, rows // chunk)
        def _(step):
            at = pl.ds(pl.multiple_of(step * chunk, chunk), chunk)
            x = x_ref[f, at, :].astype(F32)
            mean = jnp.mean(x, axis=-1, keepdims=True)
            x = x - mean
            var = jnp.mean(x * x, axis=-1, keepdims=True)
            out_ref[f, at, :] = (x * lax.rsqrt(var + 1e-06) * scale + shift).astype(BF16)


def norm_rows(x, shift, scale):
    shapes = [jax.ShapeDtypeStruct(x.shape, BF16), jax.ShapeDtypeStruct(x.shape[1:], BF16)]
    return call(norm_kernel, shapes, (), (), (x, shift, scale))


def project_kernel(ids, gains, rows_hbm, x0, x1, x2, x3, first_ref, out_ref, q_ref, w_ref, x_ref, sems):
    copies = [(ref, x_ref.at[pl.ds(ids[4 + group], 2)]) for group, ref in enumerate((x0, x1, x2, x3))]
    copies += [(rows_hbm.at[z], w_ref.at[:, z]) for z in range(8)]
    copies = [pltpu.make_async_copy(a, b, sems.at[i]) for i, (a, b) in enumerate(copies)]
    for copy in copies:
        copy.start()
    for copy in copies:
        copy.wait()
    for part in range(3):
        weight = w_ref[:, :, 32 * part : 32 * part + 32].reshape(2048, 256)
        rows = x_ref[...].reshape(1024, 2048)
        got = jnp.dot(rows, weight, preferred_element_type=F32)
        if part != 1:
            heads = []
            for h in range(2):
                one = got[:, h * 128 : (h + 1) * 128]
                one = one * lax.rsqrt(jnp.mean(one * one, axis=-1, keepdims=True) + 1e-06)
                heads.append(one * gains[h] if part == 2 else one)
            got = jnp.concatenate(heads, axis=1)
        got = got.astype(BF16).reshape(FRAMES, 128, 256)
        if part < 2:
            first_ref[part] = got[0]
            out_ref[:, part] = got[1:]
        else:
            q_ref[...] = got


def project(ids, gains, rows, xs):
    return call(
        project_kernel,
        [
            jax.ShapeDtypeStruct((2, 128, 256), BF16),
            jax.ShapeDtypeStruct((FRAMES - 1, 2, 128, 256), BF16),
            jax.ShapeDtypeStruct((FRAMES, 128, 256), BF16),
        ],
        (ids, gains),
        (rows, *xs),
        scratch=[
            pltpu.VMEM((8, 8, 96, 256), BF16),
            pltpu.VMEM((FRAMES, 128, 2048), BF16),
            pltpu.SemaphoreType.DMA((12,)),
        ],
    )


def attend_kernel(ids, q_ref, first_ref, kv_ref, left_ref, right_ref, o0, o1, o2, o3, out_ref):
    inv = 1.0 / math.sqrt(128)
    rr = lax.broadcasted_iota(jnp.int32, (128, 128), 0)
    kk = lax.broadcasted_iota(jnp.int32, (128, 128), 1)
    in_left = kk >= rr
    in_right = kk <= rr
    nt = (((1,), (1,)), ((), ()))

    def frame(g, part, lanes):
        return (first_ref[part, :, lanes] if g == 0 else kv_ref[g - 1, part, :, lanes]).astype(F32)

    for f in range(1, FRAMES):
        for h in range(2):
            lanes = slice(h * 128, (h + 1) * 128)
            q = q_ref[f, :, lanes]
            left, mid, right = (
                lax.dot_general(q, ref[f - 1, 0, :, lanes], nt, preferred_element_type=F32) * inv
                for ref in (left_ref, kv_ref, right_ref)
            )
            left = jnp.where(in_left, left, -1e30)
            right = jnp.where(in_right, right, -1e30)
            q32 = q.astype(F32)
            earlier = [
                jnp.sum(q32 * frame(g, 0, lanes), axis=-1, keepdims=True) * inv for g in range(f)
            ]
            top = jnp.max(jnp.maximum(jnp.maximum(left, mid), right), axis=-1, keepdims=True)
            for score in earlier:
                top = jnp.maximum(top, score)
            left = jnp.where(in_left, jnp.exp(left - top), 0.0)
            mid = jnp.exp(mid - top)
            right = jnp.where(in_right, jnp.exp(right - top), 0.0)
            total = jnp.sum(left + mid + right, axis=-1, keepdims=True)
            acc = None
            for p, ref in ((left, left_ref), (mid, kv_ref), (right, right_ref)):
                term = jnp.dot(p.astype(BF16), ref[f - 1, 1, :, lanes], preferred_element_type=F32)
                acc = term if acc is None else acc + term
            for g, score in enumerate(earlier):
                p = jnp.exp(score - top)
                total += p
                acc += p.astype(BF16).astype(F32) * frame(g, 1, lanes)
            out_ref[ids[9 + (f - 1) // 2], (f - 1) % 2, :, lanes] = (acc / total).astype(BF16)
    out_ref[ids[12], 1] = jnp.zeros((128, 256), BF16)
    for which, ref in enumerate((o0, o1, o2, o3)):
        ref[...] = out_ref[which]


def finish_kernel(ids, coefs, wa_hbm, wb_hbm, x0_hbm, x1_hbm, fresh_hbm, o0, o1, o2, o3, out_ref, w_ref, x_ref, o_ref, sems, x_sems):
    c, last, yhi = ids[0], ids[8], ids[1]
    rows = [
        pltpu.make_async_copy(hbm, x_ref.at[i], x_sems.at[i])
        for i, hbm in enumerate((x0_hbm.at[1], x1_hbm, fresh_hbm))
    ]
    weights = [
        [
            pltpu.make_async_copy(hbm.at[:, side], w_ref.at[which, :, :, side], sems.at[which, side])
            for side in range(2)
        ]
        for which, hbm in enumerate((wa_hbm, wb_hbm))
    ]
    for copy in (*weights[0], *rows, *weights[1]):
        copy.start()
    for which, ref in enumerate((o0, o1, o2, o3)):
        for h in range(2):
            lanes = ref[:, :, h * 128 : (h + 1) * 128]
            o_ref[pl.ds(2 * ids[9 + which] + h, 1)] = lanes.reshape(1, 256, 128)
    o = [
        jnp.concatenate([o_ref[2 * x + yhi], o_ref[2 * x + 1 - yhi]], axis=1) for x in range(4)
    ]
    for which, part in ((which, part) for which in range(2) for part in range(4)):
        if part == 0:
            for copy in weights[which]:
                copy.wait()
        if which == 0 and part == 0:
            for copy in rows:
                copy.wait()
        start = (c if which == 0 else 1 - c) * 1024 + part * 256
        columns = pl.ds(pl.multiple_of(start, 256), 256)
        eps = None
        for x in range(4):
            weight = w_ref[which, x, part].reshape(256, 256)
            term = jnp.dot(o[x], weight, preferred_element_type=F32)
            eps = term if eps is None else eps + term
        for slot in range(2):
            x = x_ref[slot, :, columns].astype(F32)
            e = x + eps[slot * 128 : (slot + 1) * 128]
            done = coefs[4 * slot] * ((x - coefs[4 * slot + 1] * e) * coefs[4 * slot + 2])
            done = (done + coefs[4 * slot + 3] * e).astype(BF16)
            if slot == 1:
                done = jnp.where(last == 1, x_ref[2, :, columns], done)
            out_ref[slot, :, columns] = done


def body(frames_in, levels, fresh, w_mod, w_qkv, q_gain, w_out):
    width = frames_in.shape[2]
    yl, c = lax.axis_index("yl"), lax.axis_index("core")
    xi, yhi, zi = lax.axis_index("x"), lax.axis_index("yh"), lax.axis_index("z")
    me = 2 * yl + c
    near = [(me ^ k) for k in range(4)]
    ids = jnp.stack([c, yhi, zi, xi, *(2 * g for g in near), me // 3, *near]).astype(jnp.int32)
    gains = lax.dynamic_slice(q_gain, (2 * me,), (2,))

    columns = [lax.dynamic_slice(w_qkv, (0, 1024 * part + 256 * me), (32, 256)) for part in (1, 2, 0)]
    block = gather(jnp.concatenate(columns, axis=0), ("x", "yh"))
    rows = lax.all_gather(block, "z", axis=0)

    mod = jnp.dot(embed(levels, w_mod.shape[0]), w_mod, preferred_element_type=F32)
    own, first_x = norm_rows(frames_in, mod[:, :width], mod[:, width:])
    across = swap(after(own, block), "yl")
    beside = swap(own, "core")

    half = lax.dynamic_slice(w_out, (0, 1024 * c), (16, 1024))
    half = half.reshape(16, 4, 256).transpose(1, 0, 2).reshape(64, 256)
    half = gather(after(half, block), "z")
    half, across, beside = lax.optimization_barrier((half, across, beside))
    half = half.reshape(8, 4, 16, 256).transpose(1, 0, 2, 3).reshape(4, 128, 256)
    diagonal = swap(across, "core")
    other = swap(after(half, diagonal), "yh")
    out_rows = lax.all_gather(jnp.stack([half, other]), "x", axis=0)
    rows, diagonal = lax.optimization_barrier((rows, diagonal))
    xs = (own, beside, across, diagonal)

    line = ("x", "yh", "z")
    right = [(i, (i + 1) % 64) for i in range(64)]
    left = [((i + 1) % 64, i) for i in range(64)]
    first, here, queries = project(ids, gains, rows, xs)
    from_left, from_right = lax.ppermute(here, line, right), lax.ppermute(here, line, left)

    back = [(i + 1, i) for i in range(3)]
    next_level = lax.ppermute(after(levels[:1], here), ("yl", "core"), back)
    next_x = lax.ppermute(after(first_x, here), ("yl", "core"), back)
    from_left, from_right, next_x, next_level = lax.optimization_barrier(
        (from_left, from_right, next_x, next_level)
    )
    pair = jax.ShapeDtypeStruct((2, 128, 256), BF16)
    o = call(
        attend_kernel,
        [pair] * 4,
        (ids,),
        (),
        (queries, first, here, from_left, from_right),
        scratch=[pltpu.VMEM((4, 2, 128, 256), BF16)],
    )
    out_other = swap(after(out_rows, o[0]), "core")
    o = (
        o[0],
        swap(o[1], "core"),
        swap(o[2], "yl"),
        lax.ppermute(o[3], ("yl", "core"), [(i, 3 - i) for i in range(4)]),
    )

    now = jnp.concatenate([levels[1:], next_level])
    a_now = alpha_bar(now)
    a_later = alpha_bar(jnp.maximum(now - LEVELS // FRAMES, 0))
    coefs = jnp.stack(
        [jnp.sqrt(a_later), jnp.sqrt(1.0 - a_now), 1.0 / jnp.sqrt(a_now), jnp.sqrt(1.0 - a_later)],
        axis=1,
    ).reshape(8)
    return call(
        finish_kernel,
        jax.ShapeDtypeStruct(frames_in.shape, BF16),
        (ids, coefs),
        (out_rows, out_other, frames_in, next_x, fresh),
        o,
        scratch=[
            pltpu.VMEM((2, 4, 4, 2, 128, 256), BF16),
            pltpu.VMEM((3, 128, 2048), BF16),
            pltpu.VMEM((8, 256, 128), BF16),
            pltpu.SemaphoreType.DMA((2, 2)),
            pltpu.SemaphoreType.DMA((3,)),
        ],
    )


def solution(mesh):
    cut = Mesh(mesh.devices.reshape(SIZES), AXES)
    frame, space = ("yl", "core"), ("x", "yh", "z")
    return jax.shard_map(
        body,
        mesh=cut,
        in_specs=(
            P(frame, space, None),
            P(frame),
            P(space, None),
            P(),
            P(space, None),
            P(),
            P(space, None),
        ),
        out_specs=P(frame, space, None),
        check_vma=False,
    )
```

time: 167 us -> 149 us (0.89); the launches traced: 167 us -> 146 us
  waiting for transfers between devices: 63.9 us -> 37.9 us
  blocking collectives: 29.8 us -> 38.9 us
  starting transfers between devices: 25.2 us -> 19 us
  Pallas kernels: 19.3 us -> 22.7 us
    ppermute x1, waiting for transfers between devices: 20.1 us -> 0.01 us  [body(): lax.ppermute(here, line, left)]
    ppermute x5 -> x7, waiting for transfers between devices: 0.01 us -> 12.6 us  [swap(): return lax.ppermute(array, axis, [(0, 1), (1, 0)])]
    ppermute x8 -> x3, waiting for transfers between devices: 31.2 us -> 21.1 us  [the longest x1 18.7 us: body(): next_level = lax.ppermute(after(levels[:1], here), ('yl', 'core'), back)]
    all_to_all x1 -> x2, blocking collectives: 29.8 us -> 38.9 us  [gather(): return lax.all_to_all(copies, axis, 0, 0)]
    ppermute x1, starting transfers between devices: 0.08 us -> 7.18 us  [body(): lax.ppermute(here, line, left)]
    all_to_all x1 -> x0, waiting for transfers between devices: 6.6 us -> none  [body(): o = lax.all_to_all(mine.reshape(4, 2, 128, 256), ('yl', 'core'), 0, 0)]
    ppermute x1, waiting for transfers between devices: 5.99 us -> 0.01 us  [body(): lax.ppermute(here, line, right)]
    ppermute x8 -> x3, starting transfers between devices: 13 us -> 7.4 us  [the longest x1 3.36 us: body(): next_x = lax.ppermute(after(first_x, here), ('yl', 'core'), back)]
  transfers between devices with their start and end apart: 17 -> 14, of which waited for: 9 -> 6; matrix products, arithmetic and copies ran while one was open for 3% -> 5% of each run, Pallas kernels for 1% -> 12%
where the time goes in v3:
time: 149 us; the launch traced here: 146 us
  blocking collectives  38.9 us (26%)
  waiting for transfers between devices  37.9 us (25%)
  Pallas kernels  22.7 us (15%)
  starting transfers between devices  19 us (13%)
  between operations  13.7 us (9%)
  local copies, waits for them, and re-layouts  8.99 us (6%)
  other arithmetic  4.48 us (3%)
    all_to_all x2, blocking collectives, gather(): return lax.all_to_all(copies, axis, 0, 0)  38.9 us
    pallas_call x4, Pallas kernels, call(): pl.pallas_call(body, out_shape=out_shape, in_specs=specs, out_specs=jax.t...  22.7 us
    ppermute x1, waiting for transfers between devices, body(): next_level = lax.ppermute(after(levels[:1], here), ('yl', 'core'), back)  18.7 us
    ppermute x7, waiting for transfers between devices, swap(): return lax.ppermute(array, axis, [(0, 1), (1, 0)])  12.6 us
    ppermute x1, starting transfers between devices, body(): lax.ppermute(here, line, left)  7.18 us
    unnamed x36, local copies, waits for them, and re-layouts  5.49 us
    ppermute x7, starting transfers between devices, swap(): return lax.ppermute(array, axis, [(0, 1), (1, 0)])  4.28 us
    all_gather x1, waiting for transfers between devices, body(): rows = lax.all_gather(block, 'z', axis=0)  4.21 us
  transfers between devices with their start and end apart: 14, of which 6 were waited for; matrix products, arithmetic and copies ran while one was open for 5% of the time, Pallas kernels for 12%

profile of v3, /device:TPU:1, one launch (start us, length us, event | category | flops | bytes accessed | tf_op | source)
XLA Modules:
  0.0 146.0 jit_solution(409743643919144619)
XLA Ops:
  6.5 0.9 constant_dynamic-slice_fusion.3
  7.5 0.0 copy-start.15
  7.5 16.1 %all_to_all.10 = bf16[8,96,256]{2,1,0:T(8,128)(2,1)} all-to-all(bf16[8,96,256]{2,1,0:T(8,128)(2,1)S(1)} %broadcast_in_dim.4), channel_id=1, replica_groups=mesh['yl'=2,'core'=2,'x'=4,'yh'=2,'z'=8] {'x','yh'}, dimensions={0} | all-to-all | bytes 786432 | tf_op jit(solution)/shard_map/all_to_all | solution.py:50
  23.6 0.0 all-gather.5.cloned.1.call-update
  23.7 0.0 all-gather.7.cloned.1.call-start
  23.7 0.7 convert_element_type.32
  24.4 0.1 fusion
  24.5 0.4 fusion.2
  24.9 2.9 %shard_map.73 = (bf16[2,128,2048]{2,1,0:T(8,128)(2,1)}, bf16[128,2048]{1,0:T(8,128)(2,1)S(1)}) custom-call(bf16[2,128,2048]{2,1,0:T(8,128)(2,1)S(1)} %copy-done.1, f32[2,2048]{1,0:T(2,128)S(1)} %get-tuple-element.59.shift_ref, f32[2,2048]{1,0:T(2,128)S(1)} %get-tuple-element.58.scale_ref), custom_call_target="tpu_custom_call" | custom-call | tf_op jit(solution)/shard_map/pallas_call | solution.py:58
  27.8 0.8 copy-done.7
  28.6 2.3 %collective-permute-start.1 = (bf16[2,128,2048]{2,1,0:T(8,128)(2,1)}, bf16[2,128,2048]{2,1,0:T(8,128)(2,1)S(1)}, u32[]{:S(2)}, u32[]{:S(2)}) collective-permute-start(bf16[2,128,2048]{2,1,0:T(8,128)(2,1)} %get-tuple-element.31.x0), channel_id=1, source_target_pairs={{0,64},{64,0},{1,65},{65,1},{2,66},{66,2},{3,67},{67,3},{4,68},{68... | collective-permute-start | bytes 3145736 | tf_op jit(solution)/shard_map/ppermute | solution.py:35
  31.0 0.4 collective-permute-start
  31.5 22.8 %all_to_all.11 = bf16[8,64,256]{2,1,0:T(8,128)(2,1)S(1)} all-to-all(bf16[8,64,256]{2,1,0:T(8,128)(2,1)S(1)} %broadcast_in_dim.5), channel_id=1, replica_groups=mesh['yl'=2,'core'=2,'x'=4,'yh'=2,'z'=8] {'z'}, dimensions={0} | all-to-all | bytes 524288 | tf_op jit(solution)/shard_map/all_to_all | solution.py:50
  54.3 1.8 %collective-permute-done.x2 = bf16[2,128,2048]{2,1,0:T(8,128)(2,1)} collective-permute-done((bf16[2,128,2048]{2,1,0:T(8,128)(2,1)}, bf16[2,128,2048]{2,1,0:T(8,128)(2,1)}, u32[]{:S(2)}, u32[]{:S(2)}) %collective-permute-start) | collective-permute-done | bytes 1048608 | tf_op jit(solution)/shard_map/ppermute | solution.py:35
  56.1 0.8 collective-permute-start.2
  56.9 2.5 %collective-permute-done.2.x3 = bf16[2,128,2048]{2,1,0:T(8,128)(2,1)S(1)} collective-permute-done((bf16[2,128,2048]{2,1,0:T(8,128)(2,1)}, bf16[2,128,2048]{2,1,0:T(8,128)(2,1)S(1)}, u32[]{:S(2)}, u32[]{:S(2)}) %collective-permute-start.2) | collective-permute-done | bytes 1048608 | tf_op jit(solution)/shard_map/ppermute | solution.py:35
  59.4 0.8 collective-permute-start.7
  60.1 8.3 %collective-permute-done.7 = bf16[4,128,256]{2,1,0:T(8,128)(2,1)S(1)} collective-permute-done((bf16[4,128,256]{2,1,0:T(8,128)(2,1)S(1)}, bf16[4,128,256]{2,1,0:T(8,128)(2,1)S(1)}, u32[]{:S(2)}, u32[]{:S(2)}) %collective-permute-start.7) | collective-permute-done | bytes 262176 | tf_op jit(solution)/shard_map/ppermute | solution.py:35
  68.4 0.8 pad_maximum_fusion
  69.2 0.0 all-gather.7.cloned.1.call-update
  69.3 0.6 dynamic_slice.15.gains
  69.9 0.7 stack.68.ids
  70.6 4.2 %all-gather.5.cloned.1.call-done = bf16[64,96,256]{2,1,0:T(8,128)(2,1)} async-done(((bf16[8,96,256]{2,1,0:T(8,128)(2,1)}), bf16[64,96,256]{2,1,0:T(8,128)(2,1)}) %all-gather.5.cloned.1.call-update) | async-done | bytes 3145744 | tf_op jit(solution)/shard_map/all_gather | solution.py:240
  74.8 8.5 %shard_map.74 = (bf16[2,128,256]{2,1,0:T(8,128)(2,1)}, bf16[7,2,128,256]{3,2,1,0:T(8,128)(2,1)}, bf16[8,128,256]{2,1,0:T(8,128)(2,1)}) custom-call(s32[13]{0:T(128)} %stack.68.ids, f32[2]{0:T(128)} %dynamic_slice.15.gains, bf16[8,8,96,256]{3,2,1,0:T(8,128)(2,1)} %bitcast.26, bf16[2,128,2048]{2,1,0:T(8,128)(2,1)} %get-tuple-element.31.x0, ...), custom_call_target="tpu_custom_call" | custom-call | tf_op jit(solution)/shard_map/pallas_call | solution.py:58
  83.4 0.1 collective-permute-start.3
  83.4 7.2 %collective-permute-start.4 = (bf16[7,2,128,256]{3,2,1,0:T(8,128)(2,1)}, bf16[7,2,128,256]{3,2,1,0:T(8,128)(2,1)S(1)}, u32[]{:S(2)}, u32[]{:S(2)}) collective-permute-start(bf16[7,2,128,256]{3,2,1,0:T(8,128)(2,1)} %get-tuple-element.36.kv_ref), channel_id=1, source_target_pairs={{1,0},{2,1},{3,2},{4,3},{5,4},{6,5},{7,6},{8,7},{9,8},{10,9},{11,1... | collective-permute-start | bytes 2752520 | tf_op jit(solution)/shard_map/ppermute | solution.py:262
  90.6 3.4 %collective-permute-start.5 = (bf16[128,2048]{1,0:T(8,128)(2,1)S(1)}, bf16[128,2048]{1,0:T(8,128)(2,1)S(1)}, u32[]{:S(2)}, u32[]{:S(2)}) collective-permute-start(bf16[128,2048]{1,0:T(8,128)(2,1)S(1)} %copy-done.8), channel_id=1, source_target_pairs={{64,0},{128,64},{192,128},{65,1},{129,65},{193,129},{66,2},{130,66... | collective-permute-start | bytes 1572872 | tf_op jit(solution)/shard_map/ppermute | solution.py:266
  94.0 0.6 fusion.10
  94.6 1.9 %collective-permute-start.6 = (s32[1]{0:T(128)}, s32[1]{0:T(128)}, u32[]{:S(2)}, u32[]{:S(2)}) collective-permute-start(s32[1]{0:T(128)} %get-tuple-element.39), channel_id=1, source_target_pairs={{64,0},{128,64},{192,128},{65,1},{129,65},{193,129},{66,2},{130,66... | collective-permute-start | bytes 20 | tf_op jit(solution)/shard_map/ppermute | solution.py:265
  96.5 18.7 %collective-permute-done.6 = s32[1]{0:T(128)} collective-permute-done((s32[1]{0:T(128)}, s32[1]{0:T(128)}, u32[]{:S(2)}, u32[]{:S(2)}) %collective-permute-start.6) | collective-permute-done | bytes 36 | tf_op jit(solution)/shard_map/ppermute | solution.py:265
  115.2 0.0 collective-permute-done.4.right_ref
  115.2 1.4 copy-done.2
  116.6 1.0 copy-done.3
  117.6 0.9 copy-done.5
  118.5 5.4 %shard_map.75 = (bf16[2,128,256]{2,1,0:T(8,128)(2,1)S(1)}, bf16[2,128,256]{2,1,0:T(8,128)(2,1)S(1)}, bf16[2,128,256]{2,1,0:T(8,128)(2,1)S(1)}, bf16[2,128,256]{2,1,0:T(8,128)(2,1)S(1)}) custom-call(s32[13]{0:T(128)S(1)} %copy-done.6, bf16[8,128,256]{2,1,0:T(8,128)(2,1)S(1)} %copy-done.3, bf16[2,128,256]{2,1,0:T(8,128)(2,1)S(1)} %copy-done.5, ...), custom_call_target="tpu_custom_call" | custom-call | tf_op jit(solution)/shard_map/pallas_call | solution.py:58
  124.0 0.6 copy-done.4
  124.6 0.0 collective-permute-start.8
  124.6 0.0 collective-permute-start.10
  124.6 2.1 %collective-permute-start.11 = (bf16[2,128,256]{2,1,0:T(8,128)(2,1)S(1)}, bf16[2,128,256]{2,1,0:T(8,128)(2,1)S(1)}, u32[]{:S(2)}, u32[]{:S(2)}) collective-permute-start(bf16[2,128,256]{2,1,0:T(8,128)(2,1)S(1)} %get-tuple-element.52), channel_id=1, source_target_pairs={{0,192},{64,128},{128,64},{192,0},{1,193},{65,129},{129,65},{193,1... | collective-permute-start | bytes 393224 | tf_op jit(solution)/shard_map/ppermute | solution.py:284
  126.7 1.4 fusion.8
  128.2 1.4 subtract_sqrt_fusion.1
  129.6 0.1 pad_maximum_fusion.2
  129.6 0.6 reshape.153.coefs
  130.2 0.0 collective-permute-done.10.o2
  130.2 2.4 %collective-permute-done.11.o3 = bf16[2,128,256]{2,1,0:T(8,128)(2,1)S(1)} collective-permute-done((bf16[2,128,256]{2,1,0:T(8,128)(2,1)S(1)}, bf16[2,128,256]{2,1,0:T(8,128)(2,1)S(1)}, u32[]{:S(2)}, u32[]{:S(2)}) %collective-permute-start.11) | collective-permute-done | bytes 131104 | tf_op jit(solution)/shard_map/ppermute | solution.py:284
  132.7 0.6 copy-done.13
  133.3 0.1 copy-done.14
  133.4 5.8 %shard_map.76 = bf16[2,128,2048]{2,1,0:T(8,128)(2,1)} custom-call(s32[13]{0:T(128)} %stack.68.ids, f32[8]{0:T(128)} %reshape.153.coefs, bf16[4,2,4,128,256]{4,3,2,1,0:T(8,128)(2,1)} %bitcast.28, bf16[4,2,4,128,256]{4,3,2,1,0:T(8,128)(2,1)} %collective-permute-done.8.wb_hbm, bf16[2,128,2048]{2,1,0:T(8,128)(2,1)} %x0_hbm.1, bf16[128,2048]{1,0:T(8,128)(2,1)} %copy-done.11, ...), custom_call_target="tpu_custom_call" | custom-call | tf_op jit(solution)/shard_map/pallas_call | solution.py:58
  (46 shorter events, 0.2 us)
Async XLA Ops:
  6.5 18.0 %copy-start = (bf16[256,4096]{1,0:T(8,128)(2,1)S(1)}, bf16[256,4096]{1,0:T(8,128)(2,1)}, u32[]{:S(2)}) copy-start(bf16[256,4096]{1,0:T(8,128)(2,1)} %param.10) | copy-start | bytes 6291460
  6.5 18.4 %copy-start.1 = (bf16[2,128,2048]{2,1,0:T(8,128)(2,1)S(1)}, bf16[2,128,2048]{2,1,0:T(8,128)(2,1)}, u32[]{:S(2)}) copy-start(bf16[2,128,2048]{2,1,0:T(8,128)(2,1)} %x0_hbm.1) | copy-start | bytes 3145732
  6.5 68.3 %all-gather.5.cloned.1.call-start = ((), (), s32[]{:S(2)}) async-start(), calls=%async_computation.2 | async-start | bytes 3538944 | tf_op jit(solution)/shard_map/all_gather | solution.py:240
  7.5 23.9 %copy-start.15 = (bf16[16,2048]{1,0:T(8,128)(2,1)S(1)}, bf16[16,2048]{1,0:T(8,128)(2,1)}, u32[]{:S(2)}) copy-start(bf16[16,2048]{1,0:T(8,128)(2,1)} %param.13) | copy-start | bytes 196612
  23.7 100.9 %all-gather.7.cloned.1.call-start = ((), (), s32[]{:S(2)}) async-start(), calls=%async_computation.3 | async-start | bytes 2621440 | tf_op jit(solution)/shard_map/all_gather | solution.py:254
  24.9 44.4 %copy-start.17 = (f32[8]{0:T(128)S(1)}, f32[8]{0:T(128)}, u32[]{:S(2)}) copy-start(f32[8]{0:T(128)} %param.12) | copy-start | bytes 100
  27.8 0.8 copy-start.7
  28.6 25.6 %collective-permute-start.1 = (bf16[2,128,2048]{2,1,0:T(8,128)(2,1)}, bf16[2,128,2048]{2,1,0:T(8,128)(2,1)S(1)}, u32[]{:S(2)}, u32[]{:S(2)}) collective-permute-start(bf16[2,128,2048]{2,1,0:T(8,128)(2,1)} %get-tuple-element.31.x0), channel_id=1, source_target_pairs={{0,64},{64,0},{1,65},{65,1},{2,66},{66,2},{3,67},{67,3},{4,68},{68... | collective-permute-start | bytes 3145736 | tf_op jit(solution)/shard_map/ppermute | solution.py:35
  31.0 25.1 %collective-permute-start = (bf16[2,128,2048]{2,1,0:T(8,128)(2,1)}, bf16[2,128,2048]{2,1,0:T(8,128)(2,1)}, u32[]{:S(2)}, u32[]{:S(2)}) collective-permute-start(bf16[2,128,2048]{2,1,0:T(8,128)(2,1)} %get-tuple-element.31.x0), channel_id=1, source_target_pairs={{0,128},{128,0},{1,129},{129,1},{2,130},{130,2},{3,131},{131,3},{4... | collective-permute-start | bytes 3145736 | tf_op jit(solution)/shard_map/ppermute | solution.py:35
  54.3 20.6 %copy-start.9 = (bf16[2,128,2048]{2,1,0:T(8,128)(2,1)}, bf16[2,128,2048]{2,1,0:T(8,128)(2,1)S(1)}, u32[]{:S(2)}) copy-start(bf16[2,128,2048]{2,1,0:T(8,128)(2,1)S(1)} %collective-permute-done.1.x1) | copy-start | bytes 3145732
  56.1 3.3 %collective-permute-start.2 = (bf16[2,128,2048]{2,1,0:T(8,128)(2,1)}, bf16[2,128,2048]{2,1,0:T(8,128)(2,1)S(1)}, u32[]{:S(2)}, u32[]{:S(2)}) collective-permute-start(bf16[2,128,2048]{2,1,0:T(8,128)(2,1)} %collective-permute-done.x2), channel_id=1, source_target_pairs={{0,64},{64,0},{1,65},{65,1},{2,66},{66,2},{3,67},{67,3},{4,68},{68... | collective-permute-start | bytes 3145736 | tf_op jit(solution)/shard_map/ppermute | solution.py:35
  59.4 9.0 %copy-start.10 = (bf16[2,128,2048]{2,1,0:T(8,128)(2,1)}, bf16[2,128,2048]{2,1,0:T(8,128)(2,1)S(1)}, u32[]{:S(2)}) copy-start(bf16[2,128,2048]{2,1,0:T(8,128)(2,1)S(1)} %collective-permute-done.2.x3) | copy-start | bytes 3145732
  59.4 9.0 %collective-permute-start.7 = (bf16[4,128,256]{2,1,0:T(8,128)(2,1)S(1)}, bf16[4,128,256]{2,1,0:T(8,128)(2,1)S(1)}, u32[]{:S(2)}, u32[]{:S(2)}) collective-permute-start(bf16[4,128,256]{2,1,0:T(8,128)(2,1)S(1)} %bitcast.30), channel_id=1, source_target_pairs={{0,8},{8,0},{1,9},{9,1},{2,10},{10,2},{3,11},{11,3},{4,12},{12,4},... | collective-permute-start | bytes 786440 | tf_op jit(solution)/shard_map/ppermute | solution.py:35
  74.8 15.8 %copy-start.8 = (bf16[128,2048]{1,0:T(8,128)(2,1)S(1)}, bf16[128,2048]{1,0:T(8,128)(2,1)}, u32[]{:S(2)}) copy-start(bf16[128,2048]{1,0:T(8,128)(2,1)} %copy-done.7) | copy-start | bytes 1572868
  74.8 19.2 %copy-start.16 = (s32[2]{0:T(128)S(1)}, s32[2]{0:T(128)}, u32[]{:S(2)}) copy-start(s32[2]{0:T(128)} %param.8) | copy-start | bytes 28
  74.8 40.4 %copy-start.6 = (s32[13]{0:T(128)S(1)}, s32[13]{0:T(128)}, u32[]{:S(2)}) copy-start(s32[13]{0:T(128)} %stack.68.ids) | copy-start | bytes 160
  83.4 31.8 %collective-permute-start.3 = (bf16[7,2,128,256]{3,2,1,0:T(8,128)(2,1)}, bf16[7,2,128,256]{3,2,1,0:T(8,128)(2,1)S(1)}, u32[]{:S(2)}, u32[]{:S(2)}) collective-permute-start(bf16[7,2,128,256]{3,2,1,0:T(8,128)(2,1)} %get-tuple-element.36.kv_ref), channel_id=1, source_target_pairs={{0,1},{1,2},{2,3},{3,4},{4,5},{5,6},{6,7},{7,8},{8,9},{9,10},{10,1... | collective-permute-start | bytes 2752520 | tf_op jit(solution)/shard_map/ppermute | solution.py:262
  83.4 31.8 %collective-permute-start.4 = (bf16[7,2,128,256]{3,2,1,0:T(8,128)(2,1)}, bf16[7,2,128,256]{3,2,1,0:T(8,128)(2,1)S(1)}, u32[]{:S(2)}, u32[]{:S(2)}) collective-permute-start(bf16[7,2,128,256]{3,2,1,0:T(8,128)(2,1)} %get-tuple-element.36.kv_ref), channel_id=1, source_target_pairs={{1,0},{2,1},{3,2},{4,3},{5,4},{6,5},{7,6},{8,7},{9,8},{10,9},{11,1... | collective-permute-start | bytes 2752520 | tf_op jit(solution)/shard_map/ppermute | solution.py:262
  90.6 24.6 %collective-permute-start.5 = (bf16[128,2048]{1,0:T(8,128)(2,1)S(1)}, bf16[128,2048]{1,0:T(8,128)(2,1)S(1)}, u32[]{:S(2)}, u32[]{:S(2)}) collective-permute-start(bf16[128,2048]{1,0:T(8,128)(2,1)S(1)} %copy-done.8), channel_id=1, source_target_pairs={{64,0},{128,64},{192,128},{65,1},{129,65},{193,129},{66,2},{130,66... | collective-permute-start | bytes 1572872 | tf_op jit(solution)/shard_map/ppermute | solution.py:266
  94.6 20.6 %collective-permute-start.6 = (s32[1]{0:T(128)}, s32[1]{0:T(128)}, u32[]{:S(2)}, u32[]{:S(2)}) collective-permute-start(s32[1]{0:T(128)} %get-tuple-element.39), channel_id=1, source_target_pairs={{64,0},{128,64},{192,128},{65,1},{129,65},{193,129},{66,2},{130,66... | collective-permute-start | bytes 20 | tf_op jit(solution)/shard_map/ppermute | solution.py:265
  115.2 17.5 %copy-start.11 = (bf16[128,2048]{1,0:T(8,128)(2,1)}, bf16[128,2048]{1,0:T(8,128)(2,1)S(1)}, u32[]{:S(2)}) copy-start(bf16[128,2048]{1,0:T(8,128)(2,1)S(1)} %collective-permute-done.5.x1_hbm) | copy-start | bytes 1572868
  115.2 1.4 copy-start.2
  116.6 1.0 copy-start.3
  117.6 0.9 copy-start.5
  123.9 0.7 copy-start.4
  124.6 8.0 %collective-permute-start.8 = (bf16[4,2,4,128,256]{4,3,2,1,0:T(8,128)(2,1)}, bf16[4,2,4,128,256]{4,3,2,1,0:T(8,128)(2,1)}, u32[]{:S(2)}, u32[]{:S(2)}) collective-permute-start(bf16[4,2,4,128,256]{4,3,2,1,0:T(8,128)(2,1)} %bitcast.27), channel_id=1, source_target_pairs={{0,64},{64,0},{1,65},{65,1},{2,66},{66,2},{3,67},{67,3},{4,68},{68... | collective-permute-start | bytes 6291464 | tf_op jit(solution)/shard_map/ppermute | solution.py:35
  124.6 5.6 %collective-permute-start.10 = (bf16[2,128,256]{2,1,0:T(8,128)(2,1)S(1)}, bf16[2,128,256]{2,1,0:T(8,128)(2,1)S(1)}, u32[]{:S(2)}, u32[]{:S(2)}) collective-permute-start(bf16[2,128,256]{2,1,0:T(8,128)(2,1)S(1)} %get-tuple-element.51), channel_id=1, source_target_pairs={{0,128},{128,0},{1,129},{129,1},{2,130},{130,2},{3,131},{131,3},{4... | collective-permute-start | bytes 393224 | tf_op jit(solution)/shard_map/ppermute | solution.py:35
  124.6 8.0 %collective-permute-start.11 = (bf16[2,128,256]{2,1,0:T(8,128)(2,1)S(1)}, bf16[2,128,256]{2,1,0:T(8,128)(2,1)S(1)}, u32[]{:S(2)}, u32[]{:S(2)}) collective-permute-start(bf16[2,128,256]{2,1,0:T(8,128)(2,1)S(1)} %get-tuple-element.52), channel_id=1, source_target_pairs={{0,192},{64,128},{128,64},{192,0},{1,193},{65,129},{129,65},{193,1... | collective-permute-start | bytes 393224 | tf_op jit(solution)/shard_map/ppermute | solution.py:284
  126.7 5.9 %collective-permute-start.9 = (bf16[2,128,256]{2,1,0:T(8,128)(2,1)S(1)}, bf16[2,128,256]{2,1,0:T(8,128)(2,1)S(1)}, u32[]{:S(2)}, u32[]{:S(2)}) collective-permute-start(bf16[2,128,256]{2,1,0:T(8,128)(2,1)S(1)} %get-tuple-element.50), channel_id=1, source_target_pairs={{0,64},{64,0},{1,65},{65,1},{2,66},{66,2},{3,67},{67,3},{4,68},{68... | collective-permute-start | bytes 393224 | tf_op jit(solution)/shard_map/ppermute | solution.py:35
  130.2 2.4 %copy-start.12 = (bf16[2,128,256]{2,1,0:T(8,128)(2,1)}, bf16[2,128,256]{2,1,0:T(8,128)(2,1)S(1)}, u32[]{:S(2)}) copy-start(bf16[2,128,256]{2,1,0:T(8,128)(2,1)S(1)} %collective-permute-done.10.o2) | copy-start | bytes 393220
  132.6 0.7 copy-start.13
  132.6 0.7 copy-start.14
Sparse Core Ops, SparseCore 0:
  23.8 50.9 all-gather.4
  76.6 32.2 all-gather.6

commit v4 on v3

--- a/solution.py
+++ b/solution.py
@@ -243,11 +243,16 @@
     own, first_x = norm_rows(frames_in, mod[:, :width], mod[:, width:])
     across = swap(after(own, block), "yl")
     beside = swap(own, "core")
+    back = [(i + 1, i) for i in range(3)]
+    next_level = lax.ppermute(after(levels[:1], block), ("yl", "core"), back)
+    next_x = lax.ppermute(after(first_x, block), ("yl", "core"), back)
 
     half = lax.dynamic_slice(w_out, (0, 1024 * c), (16, 1024))
     half = half.reshape(16, 4, 256).transpose(1, 0, 2).reshape(64, 256)
     half = gather(after(half, block), "z")
-    half, across, beside = lax.optimization_barrier((half, across, beside))
+    half, across, beside, next_x, next_level = lax.optimization_barrier(
+        (half, across, beside, next_x, next_level)
+    )
     half = half.reshape(8, 4, 16, 256).transpose(1, 0, 2, 3).reshape(4, 128, 256)
     diagonal = swap(across, "core")
     other = swap(after(half, diagonal), "yh")
@@ -261,12 +266,6 @@
     first, here, queries = project(ids, gains, rows, xs)
     from_left, from_right = lax.ppermute(here, line, right), lax.ppermute(here, line, left)
 
-    back = [(i + 1, i) for i in range(3)]
-    next_level = lax.ppermute(after(levels[:1], here), ("yl", "core"), back)
-    next_x = lax.ppermute(after(first_x, here), ("yl", "core"), back)
-    from_left, from_right, next_x, next_level = lax.optimization_barrier(
-        (from_left, from_right, next_x, next_level)
-    )
     pair = jax.ShapeDtypeStruct((2, 128, 256), BF16)
     o = call(
         attend_kernel,

time: 149 us -> 153 us (1.027); the launches traced: 146 us -> 153 us
  blocking collectives: 38.9 us -> 16.1 us
  waiting for transfers between devices: 37.9 us -> 59 us
  starting transfers between devices: 19 us -> 27 us
    all_to_all x2 -> x1, blocking collectives: 38.9 us -> 16.1 us  [gather(): return lax.all_to_all(copies, axis, 0, 0)]
    ppermute x1, waiting for transfers between devices: 0.01 us -> 19.2 us  [body(): lax.ppermute(here, line, left)]
    all_to_all x0 -> x1, starting transfers between devices: none -> 8.19 us  [gather(): return lax.all_to_all(copies, axis, 0, 0)]
    ppermute x1, waiting for transfers between devices: 0.01 us -> 7.51 us  [body(): lax.ppermute(here, line, right)]
    all_gather x1, waiting for transfers between devices: 4.21 us -> 0.01 us  [body(): rows = lax.all_gather(block, 'z', axis=0)]
    ppermute x2, waiting for transfers between devices: 18.7 us -> 16.9 us  [the longest x1 16.9 us: body(): next_level = lax.ppermute(after(levels[:1], block), ('yl', 'core'), back)]
    ppermute x7, starting transfers between devices: 4.28 us -> 5.88 us  [swap(): return lax.ppermute(array, axis, [(0, 1), (1, 0)])]
    unnamed x36 -> x32, local copies, waits for them, and re-layouts: 5.49 us -> 5.23 us
  transfers between devices with their start and end apart: 14 -> 15, of which waited for: 6 -> 7; matrix products, arithmetic and copies ran while one was open for 5% -> 5% of each run, Pallas kernels for 12% -> 11%
where the time goes in v4:
time: 153 us
  waiting for transfers between devices  59 us (39%)
  starting transfers between devices  27 us (18%)
  Pallas kernels  22.6 us (15%)
  blocking collectives  16.1 us (11%)
  between operations  13.7 us (9%)
  local copies, waits for them, and re-layouts  9.55 us (6%)
  other arithmetic  4.32 us (3%)
    pallas_call x4, Pallas kernels, call(): pl.pallas_call(body, out_shape=out_shape, in_specs=specs, out_specs=jax.t...  22.6 us
    ppermute x1, waiting for transfers between devices, body(): lax.ppermute(here, line, left)  19.2 us
    ppermute x1, waiting for transfers between devices, body(): next_level = lax.ppermute(after(levels[:1], block), ('yl', 'core'), back)  16.9 us
    all_to_all x1, blocking collectives, gather(): return lax.all_to_all(copies, axis, 0, 0)  16.1 us
    ppermute x7, waiting for transfers between devices, swap(): return lax.ppermute(array, axis, [(0, 1), (1, 0)])  12 us
    all_to_all x1, starting transfers between devices, gather(): return lax.all_to_all(copies, axis, 0, 0)  8.19 us
    ppermute x1, waiting for transfers between devices, body(): lax.ppermute(here, line, right)  7.51 us
    ppermute x1, starting transfers between devices, body(): lax.ppermute(here, line, left)  6.83 us
  transfers between devices with their start and end apart: 15, of which 7 were waited for; matrix products, arithmetic and copies ran while one was open for 5% of the time, Pallas kernels for 11%

profile of v4, /device:TPU:1, one launch (start us, length us, event | category | flops | bytes accessed | tf_op | source)
XLA Modules:
  0.0 152.7 jit_solution(16807534296972128353)
XLA Ops:
  6.5 0.9 constant_dynamic-slice_fusion.2
  7.5 0.0 copy-start.13
  7.5 16.1 %all_to_all.10 = bf16[8,96,256]{2,1,0:T(8,128)(2,1)} all-to-all(bf16[8,96,256]{2,1,0:T(8,128)(2,1)S(1)} %broadcast_in_dim.4), channel_id=1, replica_groups=mesh['yl'=2,'core'=2,'x'=4,'yh'=2,'z'=8] {'x','yh'}, dimensions={0} | all-to-all | bytes 786432 | tf_op jit(solution)/shard_map/all_to_all | solution.py:50
  23.6 0.0 all-gather.7.cloned.1.call-update
  23.7 0.7 convert_element_type.32
  24.3 0.1 fusion
  24.5 0.0 copy-start.14
  24.5 0.4 fusion.2
  24.9 2.9 %shard_map.73 = (bf16[2,128,2048]{2,1,0:T(8,128)(2,1)}, bf16[128,2048]{1,0:T(8,128)(2,1)S(1)}) custom-call(bf16[2,128,2048]{2,1,0:T(8,128)(2,1)S(1)} %copy-done.1, f32[2,2048]{1,0:T(2,128)S(1)} %get-tuple-element.55.shift_ref, f32[2,2048]{1,0:T(2,128)S(1)} %get-tuple-element.54.scale_ref), custom_call_target="tpu_custom_call" | custom-call | tf_op jit(solution)/shard_map/pallas_call | solution.py:58
  27.8 0.8 copy-done.7
  28.6 2.3 %collective-permute-start.1 = (bf16[2,128,2048]{2,1,0:T(8,128)(2,1)}, bf16[2,128,2048]{2,1,0:T(8,128)(2,1)S(1)}, u32[]{:S(2)}, u32[]{:S(2)}) collective-permute-start(bf16[2,128,2048]{2,1,0:T(8,128)(2,1)} %get-tuple-element.29.x0), channel_id=1, source_target_pairs={{0,64},{64,0},{1,65},{65,1},{2,66},{66,2},{3,67},{67,3},{4,68},{68... | collective-permute-start | bytes 3145736 | tf_op jit(solution)/shard_map/ppermute | solution.py:35
  30.9 0.4 collective-permute-start
  31.3 2.2 %collective-permute-start.2 = (bf16[128,2048]{1,0:T(8,128)(2,1)}, bf16[128,2048]{1,0:T(8,128)(2,1)}, u32[]{:S(2)}, u32[]{:S(2)}) collective-permute-start(bf16[128,2048]{1,0:T(8,128)(2,1)} %copy-done.7), channel_id=1, source_target_pairs={{64,0},{128,64},{192,128},{65,1},{129,65},{193,129},{66,2},{130,66... | collective-permute-start | bytes 1572872 | tf_op jit(solution)/shard_map/ppermute | solution.py:248
  33.6 0.7 broadcast_in_dim.5
  34.3 8.2 %all-to-all-start.1 = ((bf16[8,64,256]{2,1,0:T(8,128)(2,1)}), bf16[8,64,256]{2,1,0:T(8,128)(2,1)S(1)}, u32[]{:S(2)}, u32[]{:S(2)}) async-start(bf16[8,64,256]{2,1,0:T(8,128)(2,1)} %broadcast_in_dim.5), calls=%async_computation.1 | async-start | bytes 524288 | tf_op jit(solution)/shard_map/all_to_all | solution.py:50
  42.5 0.0 all-gather.5.cloned.1.call-start
  42.5 0.6 fusion.10
  43.2 1.9 %collective-permute-start.3 = (s32[1]{0:T(128)}, s32[1]{0:T(128)}, u32[]{:S(2)}, u32[]{:S(2)}) collective-permute-start(s32[1]{0:T(128)} %get-tuple-element.32), channel_id=1, source_target_pairs={{64,0},{128,64},{192,128},{65,1},{129,65},{193,129},{66,2},{130,66... | collective-permute-start | bytes 20 | tf_op jit(solution)/shard_map/ppermute | solution.py:247
  45.1 16.9 %collective-permute-done.3 = s32[1]{0:T(128)} collective-permute-done((s32[1]{0:T(128)}, s32[1]{0:T(128)}, u32[]{:S(2)}, u32[]{:S(2)}) %collective-permute-start.3) | collective-permute-done | bytes 36 | tf_op jit(solution)/shard_map/ppermute | solution.py:247
  62.1 0.1 collective-permute-start.4
  62.2 2.8 %collective-permute-done.4.x3 = bf16[2,128,2048]{2,1,0:T(8,128)(2,1)S(1)} collective-permute-done((bf16[2,128,2048]{2,1,0:T(8,128)(2,1)}, bf16[2,128,2048]{2,1,0:T(8,128)(2,1)S(1)}, u32[]{:S(2)}, u32[]{:S(2)}) %collective-permute-start.4) | collective-permute-done | bytes 1048608 | tf_op jit(solution)/shard_map/ppermute | solution.py:35
  65.0 0.8 collective-permute-start.5
  65.8 8.5 %collective-permute-done.5 = bf16[4,128,256]{2,1,0:T(8,128)(2,1)S(1)} collective-permute-done((bf16[4,128,256]{2,1,0:T(8,128)(2,1)S(1)}, bf16[4,128,256]{2,1,0:T(8,128)(2,1)S(1)}, u32[]{:S(2)}, u32[]{:S(2)}) %collective-permute-start.5) | collective-permute-done | bytes 262176 | tf_op jit(solution)/shard_map/ppermute | solution.py:35
  74.3 0.9 pad_maximum_fusion
  75.2 0.0 all-gather.5.cloned.1.call-update
  75.2 0.7 dynamic_slice.19.gains
  75.9 0.7 stack.68.ids
  76.6 8.5 %shard_map.74 = (bf16[2,128,256]{2,1,0:T(8,128)(2,1)}, bf16[7,2,128,256]{3,2,1,0:T(8,128)(2,1)}, bf16[8,128,256]{2,1,0:T(8,128)(2,1)}) custom-call(s32[13]{0:T(128)} %stack.68.ids, f32[2]{0:T(128)} %dynamic_slice.19.gains, bf16[8,8,96,256]{3,2,1,0:T(8,128)(2,1)} %bitcast.26, bf16[2,128,2048]{2,1,0:T(8,128)(2,1)} %get-tuple-element.29.x0, ...), custom_call_target="tpu_custom_call" | custom-call | tf_op jit(solution)/shard_map/pallas_call | solution.py:58
  85.0 6.8 %collective-permute-start.7 = (bf16[7,2,128,256]{3,2,1,0:T(8,128)(2,1)}, bf16[7,2,128,256]{3,2,1,0:T(8,128)(2,1)S(1)}, u32[]{:S(2)}, u32[]{:S(2)}) collective-permute-start(bf16[7,2,128,256]{3,2,1,0:T(8,128)(2,1)} %get-tuple-element.42.kv_ref), channel_id=1, source_target_pairs={{1,0},{2,1},{3,2},{4,3},{5,4},{6,5},{7,6},{8,7},{9,8},{10,9},{11,1... | collective-permute-start | bytes 2752520 | tf_op jit(solution)/shard_map/ppermute | solution.py:267
  91.9 19.2 %collective-permute-done.7.right_ref = bf16[7,2,128,256]{3,2,1,0:T(8,128)(2,1)S(1)} collective-permute-done((bf16[7,2,128,256]{3,2,1,0:T(8,128)(2,1)}, bf16[7,2,128,256]{3,2,1,0:T(8,128)(2,1)S(1)}, u32[]{:S(2)}, u32[]{:S(2)}) %collective-permute-start.7) | collective-permute-done | bytes 917536 | tf_op jit(solution)/shard_map/ppermute | solution.py:267
  111.1 7.5 %collective-permute-done.6.left_ref = bf16[7,2,128,256]{3,2,1,0:T(8,128)(2,1)S(1)} collective-permute-done((bf16[7,2,128,256]{3,2,1,0:T(8,128)(2,1)}, bf16[7,2,128,256]{3,2,1,0:T(8,128)(2,1)S(1)}, u32[]{:S(2)}, u32[]{:S(2)}) %collective-permute-start.6) | collective-permute-done | bytes 917536 | tf_op jit(solution)/shard_map/ppermute | solution.py:267
  118.6 1.2 copy-done.2
  119.8 1.0 copy-done.3
  120.8 0.9 copy-done.5
  121.7 5.4 %shard_map.75 = (bf16[2,128,256]{2,1,0:T(8,128)(2,1)S(1)}, bf16[2,128,256]{2,1,0:T(8,128)(2,1)S(1)}, bf16[2,128,256]{2,1,0:T(8,128)(2,1)S(1)}, bf16[2,128,256]{2,1,0:T(8,128)(2,1)S(1)}) custom-call(s32[13]{0:T(128)S(1)} %copy-done.6, bf16[8,128,256]{2,1,0:T(8,128)(2,1)S(1)} %copy-done.3, bf16[2,128,256]{2,1,0:T(8,128)(2,1)S(1)} %copy-done.5, ...), custom_call_target="tpu_custom_call" | custom-call | tf_op jit(solution)/shard_map/pallas_call | solution.py:58
  127.1 0.6 copy-done.4
  127.8 2.1 %collective-permute-start.8 = (bf16[4,2,4,128,256]{4,3,2,1,0:T(8,128)(2,1)}, bf16[4,2,4,128,256]{4,3,2,1,0:T(8,128)(2,1)}, u32[]{:S(2)}, u32[]{:S(2)}) collective-permute-start(bf16[4,2,4,128,256]{4,3,2,1,0:T(8,128)(2,1)} %bitcast.27), channel_id=1, source_target_pairs={{0,64},{64,0},{1,65},{65,1},{2,66},{66,2},{3,67},{67,3},{4,68},{68... | collective-permute-start | bytes 6291464 | tf_op jit(solution)/shard_map/ppermute | solution.py:35
  129.9 1.3 fusion.8
  131.2 0.1 collective-permute-start.9
  131.3 0.1 collective-permute-start.10
  131.4 2.0 %collective-permute-start.11 = (bf16[2,128,256]{2,1,0:T(8,128)(2,1)S(1)}, bf16[2,128,256]{2,1,0:T(8,128)(2,1)S(1)}, u32[]{:S(2)}, u32[]{:S(2)}) collective-permute-start(bf16[2,128,256]{2,1,0:T(8,128)(2,1)S(1)} %get-tuple-element.48), channel_id=1, source_target_pairs={{0,192},{64,128},{128,64},{192,0},{1,193},{65,129},{129,65},{193,1... | collective-permute-start | bytes 393224 | tf_op jit(solution)/shard_map/ppermute | solution.py:283
  133.4 1.3 subtract_sqrt_fusion.1
  134.7 0.1 pad_maximum_fusion.2
  134.8 0.6 reshape.153.coefs
  135.4 0.6 collective-permute-done.10.o2
  136.1 3.4 %collective-permute-done.11.o3 = bf16[2,128,256]{2,1,0:T(8,128)(2,1)S(1)} collective-permute-done((bf16[2,128,256]{2,1,0:T(8,128)(2,1)S(1)}, bf16[2,128,256]{2,1,0:T(8,128)(2,1)S(1)}, u32[]{:S(2)}, u32[]{:S(2)}) %collective-permute-start.11) | collective-permute-done | bytes 131104 | tf_op jit(solution)/shard_map/ppermute | solution.py:283
  139.4 0.6 copy-done.12
  140.1 5.8 %shard_map.76 = bf16[2,128,2048]{2,1,0:T(8,128)(2,1)} custom-call(s32[13]{0:T(128)} %stack.68.ids, f32[8]{0:T(128)} %reshape.153.coefs, bf16[4,2,4,128,256]{4,3,2,1,0:T(8,128)(2,1)} %bitcast.28, bf16[4,2,4,128,256]{4,3,2,1,0:T(8,128)(2,1)} %collective-permute-done.8.wb_hbm, bf16[2,128,2048]{2,1,0:T(8,128)(2,1)} %x0_hbm.1, ...), custom_call_target="tpu_custom_call" | custom-call | tf_op jit(solution)/shard_map/pallas_call | solution.py:58
  (43 shorter events, 0.2 us)
Async XLA Ops:
  6.5 17.9 %copy-start = (bf16[256,4096]{1,0:T(8,128)(2,1)S(1)}, bf16[256,4096]{1,0:T(8,128)(2,1)}, u32[]{:S(2)}) copy-start(bf16[256,4096]{1,0:T(8,128)(2,1)} %param.10) | copy-start | bytes 6291460
  6.5 18.3 %copy-start.1 = (bf16[2,128,2048]{2,1,0:T(8,128)(2,1)S(1)}, bf16[2,128,2048]{2,1,0:T(8,128)(2,1)}, u32[]{:S(2)}) copy-start(bf16[2,128,2048]{2,1,0:T(8,128)(2,1)} %x0_hbm.1) | copy-start | bytes 3145732
  6.5 70.0 %all-gather.7.cloned.1.call-start = ((), (), s32[]{:S(2)}) async-start(), calls=%async_computation.3 | async-start | bytes 3538944 | tf_op jit(solution)/shard_map/all_gather | solution.py:240
  7.5 26.0 %copy-start.13 = (bf16[16,2048]{1,0:T(8,128)(2,1)S(1)}, bf16[16,2048]{1,0:T(8,128)(2,1)}, u32[]{:S(2)}) copy-start(bf16[16,2048]{1,0:T(8,128)(2,1)} %param.13) | copy-start | bytes 196612
  24.5 18.1 %copy-start.14 = (s32[2]{0:T(128)S(1)}, s32[2]{0:T(128)}, u32[]{:S(2)}) copy-start(s32[2]{0:T(128)} %param.8) | copy-start | bytes 28
  24.9 50.4 %copy-start.15 = (f32[8]{0:T(128)S(1)}, f32[8]{0:T(128)}, u32[]{:S(2)}) copy-start(f32[8]{0:T(128)} %param.12) | copy-start | bytes 100
  27.8 0.8 copy-start.7
  28.6 33.5 %collective-permute-start.1 = (bf16[2,128,2048]{2,1,0:T(8,128)(2,1)}, bf16[2,128,2048]{2,1,0:T(8,128)(2,1)S(1)}, u32[]{:S(2)}, u32[]{:S(2)}) collective-permute-start(bf16[2,128,2048]{2,1,0:T(8,128)(2,1)} %get-tuple-element.29.x0), channel_id=1, source_target_pairs={{0,64},{64,0},{1,65},{65,1},{2,66},{66,2},{3,67},{67,3},{4,68},{68... | collective-permute-start | bytes 3145736 | tf_op jit(solution)/shard_map/ppermute | solution.py:35
  30.9 31.1 %collective-permute-start = (bf16[2,128,2048]{2,1,0:T(8,128)(2,1)}, bf16[2,128,2048]{2,1,0:T(8,128)(2,1)}, u32[]{:S(2)}, u32[]{:S(2)}) collective-permute-start(bf16[2,128,2048]{2,1,0:T(8,128)(2,1)} %get-tuple-element.29.x0), channel_id=1, source_target_pairs={{0,128},{128,0},{1,129},{129,1},{2,130},{130,2},{3,131},{131,3},{4... | collective-permute-start | bytes 3145736 | tf_op jit(solution)/shard_map/ppermute | solution.py:35
  31.3 30.7 %collective-permute-start.2 = (bf16[128,2048]{1,0:T(8,128)(2,1)}, bf16[128,2048]{1,0:T(8,128)(2,1)}, u32[]{:S(2)}, u32[]{:S(2)}) collective-permute-start(bf16[128,2048]{1,0:T(8,128)(2,1)} %copy-done.7), channel_id=1, source_target_pairs={{64,0},{128,64},{192,128},{65,1},{129,65},{193,129},{66,2},{130,66... | collective-permute-start | bytes 1572872 | tf_op jit(solution)/shard_map/ppermute | solution.py:248
  34.3 27.7 %all-to-all-start.1 = ((bf16[8,64,256]{2,1,0:T(8,128)(2,1)}), bf16[8,64,256]{2,1,0:T(8,128)(2,1)S(1)}, u32[]{:S(2)}, u32[]{:S(2)}) async-start(bf16[8,64,256]{2,1,0:T(8,128)(2,1)} %broadcast_in_dim.5), calls=%async_computation.1 | async-start | bytes 524288 | tf_op jit(solution)/shard_map/all_to_all | solution.py:50
  42.5 85.3 %all-gather.5.cloned.1.call-start = ((), (), s32[]{:S(2)}) async-start(), calls=%async_computation.2 | async-start | bytes 2621440 | tf_op jit(solution)/shard_map/all_gather | solution.py:259
  43.2 18.9 %collective-permute-start.3 = (s32[1]{0:T(128)}, s32[1]{0:T(128)}, u32[]{:S(2)}, u32[]{:S(2)}) collective-permute-start(s32[1]{0:T(128)} %get-tuple-element.32), channel_id=1, source_target_pairs={{64,0},{128,64},{192,128},{65,1},{129,65},{193,129},{66,2},{130,66... | collective-permute-start | bytes 20 | tf_op jit(solution)/shard_map/ppermute | solution.py:247
  62.1 14.5 %copy-start.8 = (bf16[2,128,2048]{2,1,0:T(8,128)(2,1)}, bf16[2,128,2048]{2,1,0:T(8,128)(2,1)S(1)}, u32[]{:S(2)}) copy-start(bf16[2,128,2048]{2,1,0:T(8,128)(2,1)S(1)} %collective-permute-done.1.x1) | copy-start | bytes 3145732
  62.1 3.0 %collective-permute-start.4 = (bf16[2,128,2048]{2,1,0:T(8,128)(2,1)}, bf16[2,128,2048]{2,1,0:T(8,128)(2,1)S(1)}, u32[]{:S(2)}, u32[]{:S(2)}) collective-permute-start(bf16[2,128,2048]{2,1,0:T(8,128)(2,1)} %collective-permute-done.x2), channel_id=1, source_target_pairs={{0,64},{64,0},{1,65},{65,1},{2,66},{66,2},{3,67},{67,3},{4,68},{68... | collective-permute-start | bytes 3145736 | tf_op jit(solution)/shard_map/ppermute | solution.py:35
  65.0 9.3 %copy-start.9 = (bf16[2,128,2048]{2,1,0:T(8,128)(2,1)}, bf16[2,128,2048]{2,1,0:T(8,128)(2,1)S(1)}, u32[]{:S(2)}) copy-start(bf16[2,128,2048]{2,1,0:T(8,128)(2,1)S(1)} %collective-permute-done.4.x3) | copy-start | bytes 3145732
  65.0 9.3 %collective-permute-start.5 = (bf16[4,128,256]{2,1,0:T(8,128)(2,1)S(1)}, bf16[4,128,256]{2,1,0:T(8,128)(2,1)S(1)}, u32[]{:S(2)}, u32[]{:S(2)}) collective-permute-start(bf16[4,128,256]{2,1,0:T(8,128)(2,1)S(1)} %bitcast.30), channel_id=1, source_target_pairs={{0,8},{8,0},{1,9},{9,1},{2,10},{10,2},{3,11},{11,3},{4,12},{12,4},... | collective-permute-start | bytes 786440 | tf_op jit(solution)/shard_map/ppermute | solution.py:35
  76.6 42.0 %copy-start.6 = (s32[13]{0:T(128)S(1)}, s32[13]{0:T(128)}, u32[]{:S(2)}) copy-start(s32[13]{0:T(128)} %stack.68.ids) | copy-start | bytes 160
  85.0 26.0 %collective-permute-start.7 = (bf16[7,2,128,256]{3,2,1,0:T(8,128)(2,1)}, bf16[7,2,128,256]{3,2,1,0:T(8,128)(2,1)S(1)}, u32[]{:S(2)}, u32[]{:S(2)}) collective-permute-start(bf16[7,2,128,256]{3,2,1,0:T(8,128)(2,1)} %get-tuple-element.42.kv_ref), channel_id=1, source_target_pairs={{1,0},{2,1},{3,2},{4,3},{5,4},{6,5},{7,6},{8,7},{9,8},{10,9},{11,1... | collective-permute-start | bytes 2752520 | tf_op jit(solution)/shard_map/ppermute | solution.py:267
  91.9 26.7 %collective-permute-start.6 = (bf16[7,2,128,256]{3,2,1,0:T(8,128)(2,1)}, bf16[7,2,128,256]{3,2,1,0:T(8,128)(2,1)S(1)}, u32[]{:S(2)}, u32[]{:S(2)}) collective-permute-start(bf16[7,2,128,256]{3,2,1,0:T(8,128)(2,1)} %get-tuple-element.42.kv_ref), channel_id=1, source_target_pairs={{0,1},{1,2},{2,3},{3,4},{4,5},{5,6},{6,7},{7,8},{8,9},{9,10},{10,1... | collective-permute-start | bytes 2752520 | tf_op jit(solution)/shard_map/ppermute | solution.py:267
  118.6 1.2 copy-start.2
  119.8 1.0 copy-start.3
  120.8 0.9 copy-start.5
  127.1 0.6 copy-start.4
  127.8 11.7 %collective-permute-start.8 = (bf16[4,2,4,128,256]{4,3,2,1,0:T(8,128)(2,1)}, bf16[4,2,4,128,256]{4,3,2,1,0:T(8,128)(2,1)}, u32[]{:S(2)}, u32[]{:S(2)}) collective-permute-start(bf16[4,2,4,128,256]{4,3,2,1,0:T(8,128)(2,1)} %bitcast.27), channel_id=1, source_target_pairs={{0,64},{64,0},{1,65},{65,1},{2,66},{66,2},{3,67},{67,3},{4,68},{68... | collective-permute-start | bytes 6291464 | tf_op jit(solution)/shard_map/ppermute | solution.py:35
  131.2 4.2 %collective-permute-start.9 = (bf16[2,128,256]{2,1,0:T(8,128)(2,1)S(1)}, bf16[2,128,256]{2,1,0:T(8,128)(2,1)S(1)}, u32[]{:S(2)}, u32[]{:S(2)}) collective-permute-start(bf16[2,128,256]{2,1,0:T(8,128)(2,1)S(1)} %get-tuple-element.46), channel_id=1, source_target_pairs={{0,64},{64,0},{1,65},{65,1},{2,66},{66,2},{3,67},{67,3},{4,68},{68... | collective-permute-start | bytes 393224 | tf_op jit(solution)/shard_map/ppermute | solution.py:35
  131.3 4.8 %collective-permute-start.10 = (bf16[2,128,256]{2,1,0:T(8,128)(2,1)S(1)}, bf16[2,128,256]{2,1,0:T(8,128)(2,1)S(1)}, u32[]{:S(2)}, u32[]{:S(2)}) collective-permute-start(bf16[2,128,256]{2,1,0:T(8,128)(2,1)S(1)} %get-tuple-element.47), channel_id=1, source_target_pairs={{0,128},{128,0},{1,129},{129,1},{2,130},{130,2},{3,131},{131,3},{4... | collective-permute-start | bytes 393224 | tf_op jit(solution)/shard_map/ppermute | solution.py:35
  131.4 8.0 %collective-permute-start.11 = (bf16[2,128,256]{2,1,0:T(8,128)(2,1)S(1)}, bf16[2,128,256]{2,1,0:T(8,128)(2,1)S(1)}, u32[]{:S(2)}, u32[]{:S(2)}) collective-permute-start(bf16[2,128,256]{2,1,0:T(8,128)(2,1)S(1)} %get-tuple-element.48), channel_id=1, source_target_pairs={{0,192},{64,128},{128,64},{192,0},{1,193},{65,129},{129,65},{193,1... | collective-permute-start | bytes 393224 | tf_op jit(solution)/shard_map/ppermute | solution.py:283
  135.4 4.0 %copy-start.10 = (bf16[2,128,256]{2,1,0:T(8,128)(2,1)}, bf16[2,128,256]{2,1,0:T(8,128)(2,1)S(1)}, u32[]{:S(2)}) copy-start(bf16[2,128,256]{2,1,0:T(8,128)(2,1)S(1)} %collective-permute-done.9.o1) | copy-start | bytes 393220
  136.1 3.4 %copy-start.11 = (bf16[2,128,256]{2,1,0:T(8,128)(2,1)}, bf16[2,128,256]{2,1,0:T(8,128)(2,1)S(1)}, u32[]{:S(2)}) copy-start(bf16[2,128,256]{2,1,0:T(8,128)(2,1)S(1)} %collective-permute-done.10.o2) | copy-start | bytes 393220
  139.4 0.7 copy-start.12
Sparse Core Ops, SparseCore 0:
  23.8 50.9 all-gather.6
  76.6 32.2 all-gather.4

commit v5 on v4

--- a/solution.py
+++ b/solution.py
@@ -264,7 +264,9 @@
     right = [(i, (i + 1) % 64) for i in range(64)]
     left = [((i + 1) % 64, i) for i in range(64)]
     first, here, queries = project(ids, gains, rows, xs)
-    from_left, from_right = lax.ppermute(here, line, right), lax.ppermute(here, line, left)
+    from_right = lax.ppermute(here, line, left)
+    from_left = lax.ppermute(here, line, right)
+    from_right, from_left = lax.optimization_barrier((from_right, from_left))
 
     pair = jax.ShapeDtypeStruct((2, 128, 256), BF16)
     o = call(

time: 153 us -> 151 us (0.987)
  the two profiles are of different devices: /device:TPU:1 before, /device:TPU:17 now
where the time goes in v5:
time: 151 us; the launch traced here: 150 us
  waiting for transfers between devices  58.7 us (39%)
  starting transfers between devices  27.6 us (18%)
  Pallas kernels  22.6 us (15%)
  between operations  13.7 us (9%)
  blocking collectives  13.6 us (9%)
  local copies, waits for them, and re-layouts  9.55 us (6%)
  other arithmetic  4.32 us (3%)
    pallas_call x4, Pallas kernels, call(): pl.pallas_call(body, out_shape=out_shape, in_specs=specs, out_specs=jax.t...  22.6 us
    ppermute x1, waiting for transfers between devices, body(): from_left = lax.ppermute(here, line, right)  19.9 us
    ppermute x1, waiting for transfers between devices, body(): next_level = lax.ppermute(after(levels[:1], block), ('yl', 'core'), back)  16.3 us
    all_to_all x1, blocking collectives, gather(): return lax.all_to_all(copies, axis, 0, 0)  13.6 us
    ppermute x7, waiting for transfers between devices, swap(): return lax.ppermute(array, axis, [(0, 1), (1, 0)])  10.6 us
    all_gather x1, waiting for transfers between devices, body(): out_rows = lax.all_gather(jnp.stack([half, other]), 'x', axis=0)  8.34 us
    all_to_all x1, starting transfers between devices, gather(): return lax.all_to_all(copies, axis, 0, 0)  8.19 us
    ppermute x1, starting transfers between devices, body(): from_right = lax.ppermute(here, line, left)  5.96 us
  transfers between devices with their start and end apart: 15, of which 8 were waited for; matrix products, arithmetic and copies ran while one was open for 5% of the time, Pallas kernels for 11%

profile of v5, /device:TPU:17, one launch (start us, length us, event | category | flops | bytes accessed | tf_op | source)
XLA Modules:
  0.0 150.5 jit_solution(13854151741884476468)
XLA Ops:
  6.5 0.9 constant_dynamic-slice_fusion.2
  7.5 13.6 %all_to_all.10 = bf16[8,96,256]{2,1,0:T(8,128)(2,1)} all-to-all(bf16[8,96,256]{2,1,0:T(8,128)(2,1)S(1)} %broadcast_in_dim.4), channel_id=1, replica_groups=mesh['yl'=2,'core'=2,'x'=4,'yh'=2,'z'=8] {'x','yh'}, dimensions={0} | all-to-all | bytes 786432 | tf_op jit(solution)/shard_map/all_to_all | solution.py:50
  21.1 0.0 all-gather.7.cloned.1.call-update
  21.1 0.7 convert_element_type.32
  21.8 0.1 fusion
  22.0 0.4 fusion.2
  22.4 2.9 %shard_map.73 = (bf16[2,128,2048]{2,1,0:T(8,128)(2,1)}, bf16[128,2048]{1,0:T(8,128)(2,1)S(1)}) custom-call(bf16[2,128,2048]{2,1,0:T(8,128)(2,1)S(1)} %copy-done.1, f32[2,2048]{1,0:T(2,128)S(1)} %get-tuple-element.59.shift_ref, f32[2,2048]{1,0:T(2,128)S(1)} %get-tuple-element.58.scale_ref), custom_call_target="tpu_custom_call" | custom-call | tf_op jit(solution)/shard_map/pallas_call | solution.py:58
  25.3 0.8 copy-done.7
  26.1 1.9 %collective-permute-start.1 = (bf16[2,128,2048]{2,1,0:T(8,128)(2,1)}, bf16[2,128,2048]{2,1,0:T(8,128)(2,1)S(1)}, u32[]{:S(2)}, u32[]{:S(2)}) collective-permute-start(bf16[2,128,2048]{2,1,0:T(8,128)(2,1)} %get-tuple-element.31.x0), channel_id=1, source_target_pairs={{0,64},{64,0},{1,65},{65,1},{2,66},{66,2},{3,67},{67,3},{4,68},{68... | collective-permute-start | bytes 3145736 | tf_op jit(solution)/shard_map/ppermute | solution.py:35
  27.9 1.0 collective-permute-start
  28.9 2.2 %collective-permute-start.2 = (bf16[128,2048]{1,0:T(8,128)(2,1)}, bf16[128,2048]{1,0:T(8,128)(2,1)}, u32[]{:S(2)}, u32[]{:S(2)}) collective-permute-start(bf16[128,2048]{1,0:T(8,128)(2,1)} %copy-done.7), channel_id=1, source_target_pairs={{64,0},{128,64},{192,128},{65,1},{129,65},{193,129},{66,2},{130,66... | collective-permute-start | bytes 1572872 | tf_op jit(solution)/shard_map/ppermute | solution.py:248
  31.2 0.7 broadcast_in_dim.5
  31.9 8.2 %all-to-all-start.1 = ((bf16[8,64,256]{2,1,0:T(8,128)(2,1)}), bf16[8,64,256]{2,1,0:T(8,128)(2,1)S(1)}, u32[]{:S(2)}, u32[]{:S(2)}) async-start(bf16[8,64,256]{2,1,0:T(8,128)(2,1)} %broadcast_in_dim.5), calls=%async_computation.1 | async-start | bytes 524288 | tf_op jit(solution)/shard_map/all_to_all | solution.py:50
  40.1 0.0 all-gather.5.cloned.1.call-start
  40.2 0.6 fusion.10
  40.8 1.9 %collective-permute-start.3 = (s32[1]{0:T(128)}, s32[1]{0:T(128)}, u32[]{:S(2)}, u32[]{:S(2)}) collective-permute-start(s32[1]{0:T(128)} %get-tuple-element.34), channel_id=1, source_target_pairs={{64,0},{128,64},{192,128},{65,1},{129,65},{193,129},{66,2},{130,66... | collective-permute-start | bytes 20 | tf_op jit(solution)/shard_map/ppermute | solution.py:247
  42.7 16.3 %collective-permute-done.3 = s32[1]{0:T(128)} collective-permute-done((s32[1]{0:T(128)}, s32[1]{0:T(128)}, u32[]{:S(2)}, u32[]{:S(2)}) %collective-permute-start.3) | collective-permute-done | bytes 36 | tf_op jit(solution)/shard_map/ppermute | solution.py:247
  59.1 0.1 collective-permute-start.4
  59.2 2.8 %collective-permute-done.4.x3 = bf16[2,128,2048]{2,1,0:T(8,128)(2,1)S(1)} collective-permute-done((bf16[2,128,2048]{2,1,0:T(8,128)(2,1)}, bf16[2,128,2048]{2,1,0:T(8,128)(2,1)S(1)}, u32[]{:S(2)}, u32[]{:S(2)}) %collective-permute-start.4) | collective-permute-done | bytes 1048608 | tf_op jit(solution)/shard_map/ppermute | solution.py:35
  62.0 2.2 %collective-permute-start.5 = (bf16[4,128,256]{2,1,0:T(8,128)(2,1)S(1)}, bf16[4,128,256]{2,1,0:T(8,128)(2,1)S(1)}, u32[]{:S(2)}, u32[]{:S(2)}) collective-permute-start(bf16[4,128,256]{2,1,0:T(8,128)(2,1)S(1)} %bitcast.30), channel_id=1, source_target_pairs={{0,8},{8,0},{1,9},{9,1},{2,10},{10,2},{3,11},{11,3},{4,12},{12,4},... | collective-permute-start | bytes 786440 | tf_op jit(solution)/shard_map/ppermute | solution.py:35
  64.3 7.2 %collective-permute-done.5 = bf16[4,128,256]{2,1,0:T(8,128)(2,1)S(1)} collective-permute-done((bf16[4,128,256]{2,1,0:T(8,128)(2,1)S(1)}, bf16[4,128,256]{2,1,0:T(8,128)(2,1)S(1)}, u32[]{:S(2)}, u32[]{:S(2)}) %collective-permute-start.5) | collective-permute-done | bytes 262176 | tf_op jit(solution)/shard_map/ppermute | solution.py:35
  71.4 0.9 pad_maximum_fusion
  72.3 0.0 all-gather.5.cloned.1.call-update
  72.4 0.7 dynamic_slice.19.gains
  73.0 0.7 stack.68.ids
  73.7 0.1 all-gather.7.cloned.1.call-done
  73.8 8.5 %shard_map.74 = (bf16[2,128,256]{2,1,0:T(8,128)(2,1)}, bf16[7,2,128,256]{3,2,1,0:T(8,128)(2,1)}, bf16[8,128,256]{2,1,0:T(8,128)(2,1)}) custom-call(s32[13]{0:T(128)} %stack.68.ids, f32[2]{0:T(128)} %dynamic_slice.19.gains, bf16[8,8,96,256]{3,2,1,0:T(8,128)(2,1)} %bitcast.26, bf16[2,128,2048]{2,1,0:T(8,128)(2,1)} %get-tuple-element.31.x0, ...), custom_call_target="tpu_custom_call" | custom-call | tf_op jit(solution)/shard_map/pallas_call | solution.py:58
  82.3 1.5 %collective-permute-start.7 = (bf16[7,2,128,256]{3,2,1,0:T(8,128)(2,1)}, bf16[7,2,128,256]{3,2,1,0:T(8,128)(2,1)S(1)}, u32[]{:S(2)}, u32[]{:S(2)}) collective-permute-start(bf16[7,2,128,256]{3,2,1,0:T(8,128)(2,1)} %get-tuple-element.44.kv_ref), channel_id=1, source_target_pairs={{0,1},{1,2},{2,3},{3,4},{4,5},{5,6},{6,7},{7,8},{8,9},{9,10},{10,1... | collective-permute-start | bytes 2752520 | tf_op jit(solution)/shard_map/ppermute | solution.py:268
  83.8 6.0 %collective-permute-start.6 = (bf16[7,2,128,256]{3,2,1,0:T(8,128)(2,1)}, bf16[7,2,128,256]{3,2,1,0:T(8,128)(2,1)S(1)}, u32[]{:S(2)}, u32[]{:S(2)}) collective-permute-start(bf16[7,2,128,256]{3,2,1,0:T(8,128)(2,1)} %get-tuple-element.44.kv_ref), channel_id=1, source_target_pairs={{1,0},{2,1},{3,2},{4,3},{5,4},{6,5},{7,6},{8,7},{9,8},{10,9},{11,1... | collective-permute-start | bytes 2752520 | tf_op jit(solution)/shard_map/ppermute | solution.py:267
  89.7 19.9 %collective-permute-done.7.left_ref = bf16[7,2,128,256]{3,2,1,0:T(8,128)(2,1)S(1)} collective-permute-done((bf16[7,2,128,256]{3,2,1,0:T(8,128)(2,1)}, bf16[7,2,128,256]{3,2,1,0:T(8,128)(2,1)S(1)}, u32[]{:S(2)}, u32[]{:S(2)}) %collective-permute-start.7) | collective-permute-done | bytes 917536 | tf_op jit(solution)/shard_map/ppermute | solution.py:268
  109.6 1.2 copy-done.2
  110.8 1.0 copy-done.3
  111.8 0.9 copy-done.5
  112.7 5.4 %shard_map.75 = (bf16[2,128,256]{2,1,0:T(8,128)(2,1)S(1)}, bf16[2,128,256]{2,1,0:T(8,128)(2,1)S(1)}, bf16[2,128,256]{2,1,0:T(8,128)(2,1)S(1)}, bf16[2,128,256]{2,1,0:T(8,128)(2,1)S(1)}) custom-call(s32[13]{0:T(128)S(1)} %copy-done.6, bf16[8,128,256]{2,1,0:T(8,128)(2,1)S(1)} %copy-done.3, bf16[2,128,256]{2,1,0:T(8,128)(2,1)S(1)} %copy-done.5, ...), custom_call_target="tpu_custom_call" | custom-call | tf_op jit(solution)/shard_map/pallas_call | solution.py:58
  118.2 0.6 copy-done.4
  118.8 8.3 %all-gather.5.cloned.1.call-done = bf16[8,4,128,256]{3,2,1,0:T(8,128)(2,1)} async-done(((bf16[2,4,128,256]{3,2,1,0:T(8,128)(2,1)}), bf16[8,4,128,256]{3,2,1,0:T(8,128)(2,1)}) %all-gather.5.cloned.1.call-update) | async-done | bytes 2097168 | tf_op jit(solution)/shard_map/all_gather | solution.py:259
  127.2 0.5 collective-permute-start.8
  127.6 1.3 fusion.8
  128.9 0.1 collective-permute-start.9
  129.1 0.1 collective-permute-start.10
  129.1 2.0 %collective-permute-start.11 = (bf16[2,128,256]{2,1,0:T(8,128)(2,1)S(1)}, bf16[2,128,256]{2,1,0:T(8,128)(2,1)S(1)}, u32[]{:S(2)}, u32[]{:S(2)}) collective-permute-start(bf16[2,128,256]{2,1,0:T(8,128)(2,1)S(1)} %get-tuple-element.52), channel_id=1, source_target_pairs={{0,192},{64,128},{128,64},{192,0},{1,193},{65,129},{129,65},{193,1... | collective-permute-start | bytes 393224 | tf_op jit(solution)/shard_map/ppermute | solution.py:285
  131.2 1.3 subtract_sqrt_fusion.1
  132.5 0.1 pad_maximum_fusion.2
  132.5 0.6 reshape.153.coefs
  133.2 0.6 collective-permute-done.10.o2
  133.8 3.4 %collective-permute-done.11.o3 = bf16[2,128,256]{2,1,0:T(8,128)(2,1)S(1)} collective-permute-done((bf16[2,128,256]{2,1,0:T(8,128)(2,1)S(1)}, bf16[2,128,256]{2,1,0:T(8,128)(2,1)S(1)}, u32[]{:S(2)}, u32[]{:S(2)}) %collective-permute-start.11) | collective-permute-done | bytes 131104 | tf_op jit(solution)/shard_map/ppermute | solution.py:285
  137.2 0.6 copy-done.12
  137.8 5.8 %shard_map.76 = bf16[2,128,2048]{2,1,0:T(8,128)(2,1)} custom-call(s32[13]{0:T(128)} %stack.68.ids, f32[8]{0:T(128)} %reshape.153.coefs, bf16[4,2,4,128,256]{4,3,2,1,0:T(8,128)(2,1)} %bitcast.28, bf16[4,2,4,128,256]{4,3,2,1,0:T(8,128)(2,1)} %collective-permute-done.8.wb_hbm, bf16[2,128,2048]{2,1,0:T(8,128)(2,1)} %x0_hbm.1, ...), custom_call_target="tpu_custom_call" | custom-call | tf_op jit(solution)/shard_map/pallas_call | solution.py:58
  (43 shorter events, 0.2 us)
Async XLA Ops:
  6.5 15.4 %copy-start = (bf16[256,4096]{1,0:T(8,128)(2,1)S(1)}, bf16[256,4096]{1,0:T(8,128)(2,1)}, u32[]{:S(2)}) copy-start(bf16[256,4096]{1,0:T(8,128)(2,1)} %param.10) | copy-start | bytes 6291460
  6.5 15.8 %copy-start.1 = (bf16[2,128,2048]{2,1,0:T(8,128)(2,1)S(1)}, bf16[2,128,2048]{2,1,0:T(8,128)(2,1)}, u32[]{:S(2)}) copy-start(bf16[2,128,2048]{2,1,0:T(8,128)(2,1)} %x0_hbm.1) | copy-start | bytes 3145732
  6.5 67.3 %all-gather.7.cloned.1.call-start = ((), (), s32[]{:S(2)}) async-start(), calls=%async_computation.3 | async-start | bytes 3538944 | tf_op jit(solution)/shard_map/all_gather | solution.py:240
  7.5 23.6 %copy-start.13 = (bf16[16,2048]{1,0:T(8,128)(2,1)S(1)}, bf16[16,2048]{1,0:T(8,128)(2,1)}, u32[]{:S(2)}) copy-start(bf16[16,2048]{1,0:T(8,128)(2,1)} %param.13) | copy-start | bytes 196612
  21.9 18.2 %copy-start.14 = (s32[2]{0:T(128)S(1)}, s32[2]{0:T(128)}, u32[]{:S(2)}) copy-start(s32[2]{0:T(128)} %param.8) | copy-start | bytes 28
  22.3 50.0 %copy-start.15 = (f32[8]{0:T(128)S(1)}, f32[8]{0:T(128)}, u32[]{:S(2)}) copy-start(f32[8]{0:T(128)} %param.12) | copy-start | bytes 100
  25.3 0.8 copy-start.7
  26.1 33.0 %collective-permute-start.1 = (bf16[2,128,2048]{2,1,0:T(8,128)(2,1)}, bf16[2,128,2048]{2,1,0:T(8,128)(2,1)S(1)}, u32[]{:S(2)}, u32[]{:S(2)}) collective-permute-start(bf16[2,128,2048]{2,1,0:T(8,128)(2,1)} %get-tuple-element.31.x0), channel_id=1, source_target_pairs={{0,64},{64,0},{1,65},{65,1},{2,66},{66,2},{3,67},{67,3},{4,68},{68... | collective-permute-start | bytes 3145736 | tf_op jit(solution)/shard_map/ppermute | solution.py:35
  27.9 31.1 %collective-permute-start = (bf16[2,128,2048]{2,1,0:T(8,128)(2,1)}, bf16[2,128,2048]{2,1,0:T(8,128)(2,1)}, u32[]{:S(2)}, u32[]{:S(2)}) collective-permute-start(bf16[2,128,2048]{2,1,0:T(8,128)(2,1)} %get-tuple-element.31.x0), channel_id=1, source_target_pairs={{0,128},{128,0},{1,129},{129,1},{2,130},{130,2},{3,131},{131,3},{4... | collective-permute-start | bytes 3145736 | tf_op jit(solution)/shard_map/ppermute | solution.py:35
  28.9 30.1 %collective-permute-start.2 = (bf16[128,2048]{1,0:T(8,128)(2,1)}, bf16[128,2048]{1,0:T(8,128)(2,1)}, u32[]{:S(2)}, u32[]{:S(2)}) collective-permute-start(bf16[128,2048]{1,0:T(8,128)(2,1)} %copy-done.7), channel_id=1, source_target_pairs={{64,0},{128,64},{192,128},{65,1},{129,65},{193,129},{66,2},{130,66... | collective-permute-start | bytes 1572872 | tf_op jit(solution)/shard_map/ppermute | solution.py:248
  31.9 27.1 %all-to-all-start.1 = ((bf16[8,64,256]{2,1,0:T(8,128)(2,1)}), bf16[8,64,256]{2,1,0:T(8,128)(2,1)S(1)}, u32[]{:S(2)}, u32[]{:S(2)}) async-start(bf16[8,64,256]{2,1,0:T(8,128)(2,1)} %broadcast_in_dim.5), calls=%async_computation.1 | async-start | bytes 524288 | tf_op jit(solution)/shard_map/all_to_all | solution.py:50
  40.1 87.1 %all-gather.5.cloned.1.call-start = ((), (), s32[]{:S(2)}) async-start(), calls=%async_computation.2 | async-start | bytes 2621440 | tf_op jit(solution)/shard_map/all_gather | solution.py:259
  40.8 18.3 %collective-permute-start.3 = (s32[1]{0:T(128)}, s32[1]{0:T(128)}, u32[]{:S(2)}, u32[]{:S(2)}) collective-permute-start(s32[1]{0:T(128)} %get-tuple-element.34), channel_id=1, source_target_pairs={{64,0},{128,64},{192,128},{65,1},{129,65},{193,129},{66,2},{130,66... | collective-permute-start | bytes 20 | tf_op jit(solution)/shard_map/ppermute | solution.py:247
  59.1 14.7 %copy-start.8 = (bf16[2,128,2048]{2,1,0:T(8,128)(2,1)}, bf16[2,128,2048]{2,1,0:T(8,128)(2,1)S(1)}, u32[]{:S(2)}) copy-start(bf16[2,128,2048]{2,1,0:T(8,128)(2,1)S(1)} %collective-permute-done.1.x1) | copy-start | bytes 3145732
  59.1 3.0 %collective-permute-start.4 = (bf16[2,128,2048]{2,1,0:T(8,128)(2,1)}, bf16[2,128,2048]{2,1,0:T(8,128)(2,1)S(1)}, u32[]{:S(2)}, u32[]{:S(2)}) collective-permute-start(bf16[2,128,2048]{2,1,0:T(8,128)(2,1)} %collective-permute-done.x2), channel_id=1, source_target_pairs={{0,64},{64,0},{1,65},{65,1},{2,66},{66,2},{3,67},{67,3},{4,68},{68... | collective-permute-start | bytes 3145736 | tf_op jit(solution)/shard_map/ppermute | solution.py:35
  62.0 9.4 %copy-start.9 = (bf16[2,128,2048]{2,1,0:T(8,128)(2,1)}, bf16[2,128,2048]{2,1,0:T(8,128)(2,1)S(1)}, u32[]{:S(2)}) copy-start(bf16[2,128,2048]{2,1,0:T(8,128)(2,1)S(1)} %collective-permute-done.4.x3) | copy-start | bytes 3145732
  62.0 9.4 %collective-permute-start.5 = (bf16[4,128,256]{2,1,0:T(8,128)(2,1)S(1)}, bf16[4,128,256]{2,1,0:T(8,128)(2,1)S(1)}, u32[]{:S(2)}, u32[]{:S(2)}) collective-permute-start(bf16[4,128,256]{2,1,0:T(8,128)(2,1)S(1)} %bitcast.30), channel_id=1, source_target_pairs={{0,8},{8,0},{1,9},{9,1},{2,10},{10,2},{3,11},{11,3},{4,12},{12,4},... | collective-permute-start | bytes 786440 | tf_op jit(solution)/shard_map/ppermute | solution.py:35
  73.8 35.8 %copy-start.6 = (s32[13]{0:T(128)S(1)}, s32[13]{0:T(128)}, u32[]{:S(2)}) copy-start(s32[13]{0:T(128)} %stack.68.ids) | copy-start | bytes 160
  82.3 27.4 %collective-permute-start.7 = (bf16[7,2,128,256]{3,2,1,0:T(8,128)(2,1)}, bf16[7,2,128,256]{3,2,1,0:T(8,128)(2,1)S(1)}, u32[]{:S(2)}, u32[]{:S(2)}) collective-permute-start(bf16[7,2,128,256]{3,2,1,0:T(8,128)(2,1)} %get-tuple-element.44.kv_ref), channel_id=1, source_target_pairs={{0,1},{1,2},{2,3},{3,4},{4,5},{5,6},{6,7},{7,8},{8,9},{9,10},{10,1... | collective-permute-start | bytes 2752520 | tf_op jit(solution)/shard_map/ppermute | solution.py:268
  83.8 25.8 %collective-permute-start.6 = (bf16[7,2,128,256]{3,2,1,0:T(8,128)(2,1)}, bf16[7,2,128,256]{3,2,1,0:T(8,128)(2,1)S(1)}, u32[]{:S(2)}, u32[]{:S(2)}) collective-permute-start(bf16[7,2,128,256]{3,2,1,0:T(8,128)(2,1)} %get-tuple-element.44.kv_ref), channel_id=1, source_target_pairs={{1,0},{2,1},{3,2},{4,3},{5,4},{6,5},{7,6},{8,7},{9,8},{10,9},{11,1... | collective-permute-start | bytes 2752520 | tf_op jit(solution)/shard_map/ppermute | solution.py:267
  109.6 1.2 copy-start.2
  110.8 1.0 copy-start.3
  111.8 0.9 copy-start.5
  118.2 0.6 copy-start.4
  127.2 10.0 %collective-permute-start.8 = (bf16[4,2,4,128,256]{4,3,2,1,0:T(8,128)(2,1)}, bf16[4,2,4,128,256]{4,3,2,1,0:T(8,128)(2,1)}, u32[]{:S(2)}, u32[]{:S(2)}) collective-permute-start(bf16[4,2,4,128,256]{4,3,2,1,0:T(8,128)(2,1)} %bitcast.27), channel_id=1, source_target_pairs={{0,64},{64,0},{1,65},{65,1},{2,66},{66,2},{3,67},{67,3},{4,68},{68... | collective-permute-start | bytes 6291464 | tf_op jit(solution)/shard_map/ppermute | solution.py:35
  128.9 4.2 %collective-permute-start.9 = (bf16[2,128,256]{2,1,0:T(8,128)(2,1)S(1)}, bf16[2,128,256]{2,1,0:T(8,128)(2,1)S(1)}, u32[]{:S(2)}, u32[]{:S(2)}) collective-permute-start(bf16[2,128,256]{2,1,0:T(8,128)(2,1)S(1)} %get-tuple-element.50), channel_id=1, source_target_pairs={{0,64},{64,0},{1,65},{65,1},{2,66},{66,2},{3,67},{67,3},{4,68},{68... | collective-permute-start | bytes 393224 | tf_op jit(solution)/shard_map/ppermute | solution.py:35
  129.1 4.7 %collective-permute-start.10 = (bf16[2,128,256]{2,1,0:T(8,128)(2,1)S(1)}, bf16[2,128,256]{2,1,0:T(8,128)(2,1)S(1)}, u32[]{:S(2)}, u32[]{:S(2)}) collective-permute-start(bf16[2,128,256]{2,1,0:T(8,128)(2,1)S(1)} %get-tuple-element.51), channel_id=1, source_target_pairs={{0,128},{128,0},{1,129},{129,1},{2,130},{130,2},{3,131},{131,3},{4... | collective-permute-start | bytes 393224 | tf_op jit(solution)/shard_map/ppermute | solution.py:35
  129.1 8.0 %collective-permute-start.11 = (bf16[2,128,256]{2,1,0:T(8,128)(2,1)S(1)}, bf16[2,128,256]{2,1,0:T(8,128)(2,1)S(1)}, u32[]{:S(2)}, u32[]{:S(2)}) collective-permute-start(bf16[2,128,256]{2,1,0:T(8,128)(2,1)S(1)} %get-tuple-element.52), channel_id=1, source_target_pairs={{0,192},{64,128},{128,64},{192,0},{1,193},{65,129},{129,65},{193,1... | collective-permute-start | bytes 393224 | tf_op jit(solution)/shard_map/ppermute | solution.py:285
  133.2 4.0 %copy-start.10 = (bf16[2,128,256]{2,1,0:T(8,128)(2,1)}, bf16[2,128,256]{2,1,0:T(8,128)(2,1)S(1)}, u32[]{:S(2)}) copy-start(bf16[2,128,256]{2,1,0:T(8,128)(2,1)S(1)} %collective-permute-done.9.o1) | copy-start | bytes 393220
  133.8 3.4 %copy-start.11 = (bf16[2,128,256]{2,1,0:T(8,128)(2,1)}, bf16[2,128,256]{2,1,0:T(8,128)(2,1)S(1)}, u32[]{:S(2)}) copy-start(bf16[2,128,256]{2,1,0:T(8,128)(2,1)S(1)} %collective-permute-done.10.o2) | copy-start | bytes 393220
  137.1 0.7 copy-start.12
Sparse Core Ops, SparseCore 0:
  21.3 52.4 all-gather.6
  75.6 51.5 all-gather.4
